TPU v7x, 128 devices: a whole 4x4x4 slice. The times are simulated.
128 devices in a mesh: sgt: 8 (over z, core), work: 16 (over y, x).
Axes of the slice: x: 4, y: 4, z: 4, core: 2. Of those that a mesh axis runs over, the one named last changes fastest.
Arguments:
- sgt_tensor: bfloat16 [32, 6, 2, 128, 1024], P('sgt'), may hold values from -6 to 6
- moment: float32 [32, 6, 128], P('sgt'), may hold values from -2.5 to 2.5
- slip_rate: bfloat16 [128, 8, 64, 128, 32], P(('sgt', 'work')), may hold values from 0 to 0.011047363
- footprint: int32 [128, 8], replicated, may hold values from 0 to 31, as said below
- live_blocks: int32 [128], replicated, may hold values from 1 to 8
- start_delay: int32 [128, 8], replicated, may hold values from 0 to 255
- frequency: float32 [44], replicated, may hold values from 0.05 to 1.5
- period_owner: int32 [44], replicated, may hold values from 0 to 15, as said below
Outputs:
- spectral_peaks: float32 [16, 3, 2, 128, 64], P('work', None, None, 'sgt')
Inputs may be any that keep to these rules, and one draw needn't show every extreme that they name: `footprint`: slot k of rupture r names block ((c + k) mod 8) * 4 + ((c + k) mod 32) // 8 for a strike column c of that rupture; so the slots of one rupture name blocks of distinct indices of sgt, block b being held by index b // 4. `period_owner`: each index of work owns 44 // 16 or 3 periods.
All inputs are finite; a program needn't handle non-finite values.
Results may differ from a plain program's by a relative error of at most 0.0024.
Values may be sent and summed in bfloat16 or wider, within the bound.
No kernel may reach another device: no remote copies, remote signals or barrier semaphores. Data moves between devices by JAX's collectives and lax.ppermute only.
A program may use at most 192 MiB of HBM per device.

v0:
```python
import math

import jax
import jax.numpy as jnp
from jax import lax
from jax.sharding import PartitionSpec as P

NT = 1024
NCOMP = 2
L = 32
OFFMAX = 256
KIR = 512
V = 64


damping = 0.05


def project(sgt_tensor, moment):
    summed = jnp.sum(moment[:, :, None, :, None] * sgt_tensor.astype(jnp.float32), axis=1)
    return summed.astype(jnp.bfloat16)


def hankel(shifted, width, steps):
    length = shifted.shape[-1]
    leading = shifted.shape[:-1]
    repeated = jnp.broadcast_to(shifted[..., None, :], leading + (width, length))
    flattened = repeated.reshape(leading + (width * length,))
    flattened = jnp.concatenate([flattened, jnp.zeros(leading + (width,), shifted.dtype)], axis=-1)
    return flattened.reshape(leading + (width, length + 1))[..., :steps]


def convolve(tensor_block, slip_window, delay):
    channels, points, samples = tensor_block.shape
    padding = jnp.zeros((channels, points, OFFMAX + L - 1), tensor_block.dtype)
    ending = jnp.zeros((channels, points, 1), tensor_block.dtype)
    extended = jnp.concatenate([padding, tensor_block, ending], axis=2)
    begin = OFFMAX - delay
    shifted = lax.dynamic_slice_in_dim(extended, begin, samples + L, axis=2)
    windows = hankel(shifted, L, samples)
    return jnp.einsum(
        "viq,ciqt->vct", slip_window[:, :, ::-1], windows, preferred_element_type=jnp.float32
    )


def response_matrix(angular):
    delays = jnp.arange(NT)[None, :] - jnp.arange(NT)[:, None]
    elapsed = jnp.maximum(delays, 0).astype(jnp.float32)
    damped = angular * math.sqrt(1.0 - damping * damping)
    kernel = (
        angular
        * angular
        * jnp.exp(-damping * angular * elapsed)
        * jnp.sin(damped * elapsed)
        / damped
    )
    inside = (delays >= 0) & (delays < KIR)
    return jnp.where(inside, kernel, jnp.zeros_like(kernel)).astype(jnp.bfloat16)


def local(
    sgt_tensor, moment, slip_rate, footprint, live_blocks, start_delay, frequency, period_owner
):
    sgt_devices = lax.axis_size("sgt")
    work_devices = lax.axis_size("work")
    sgt_place = lax.axis_index("sgt")
    work_place = lax.axis_index("work")
    held_blocks = sgt_tensor.shape[0]
    slot_total = footprint.shape[1]
    projected = project(sgt_tensor, moment)
    rupture = sgt_place * work_devices + work_place
    own_blocks = lax.dynamic_index_in_dim(footprint, rupture, 0, keepdims=False)
    own_count = lax.dynamic_index_in_dim(live_blocks, rupture, 0, keepdims=False)
    own_delays = lax.dynamic_index_in_dim(start_delay, rupture, 0, keepdims=False)
    own_slips = slip_rate[0]
    asking = jnp.arange(sgt_devices) * work_devices + work_place
    asked_blocks = jnp.take(footprint, asking, axis=0)
    asked_count = jnp.take(live_blocks, asking, axis=0)
    slot_ids = jnp.arange(slot_total)
    held_mask = (slot_ids[None, :] < asked_count[:, None]) & (
        asked_blocks // held_blocks == sgt_place
    )
    requested = jnp.any(held_mask, axis=1)
    local_block = jnp.sum(jnp.where(held_mask, asked_blocks % held_blocks, 0), axis=1)
    gathered = jnp.take(projected, local_block, axis=0)
    outgoing = jnp.where(requested[:, None, None, None], gathered, jnp.zeros_like(gathered))
    incoming = lax.all_to_all(outgoing, "sgt", split_axis=0, concat_axis=0, tiled=True)

    def add_slot(slot_index, running):
        owner_index = own_blocks[slot_index] // held_blocks
        tensor_block = lax.dynamic_index_in_dim(incoming, owner_index, 0, keepdims=False)
        slip_window = lax.dynamic_index_in_dim(own_slips, slot_index, 0, keepdims=False)
        return running + convolve(tensor_block, slip_window, own_delays[slot_index])

    running = lax.fori_loop(0, own_count, add_slot, jnp.zeros((V, NCOMP, NT), jnp.float32))
    traces = running.astype(jnp.bfloat16)
    period_total = frequency.shape[0]
    slot_count = -(-period_total // work_devices)
    period_ids = jnp.arange(period_total)
    same_owner = period_owner[:, None] == period_owner[None, :]
    earlier = period_ids[None, :] < period_ids[:, None]
    period_rank = jnp.sum(same_owner & earlier, axis=1)
    slot_numbers = jnp.arange(slot_count)
    owned_mask = period_owner == work_place
    chosen = owned_mask[None, :] & (period_rank[None, :] == slot_numbers[:, None])
    valid_slot = jnp.any(chosen, axis=1)
    slot_rates = jnp.sum(jnp.where(chosen, frequency[None, :], 0.0), axis=1)
    slot_rates = jnp.where(valid_slot, slot_rates, 1.0)
    tables = jax.vmap(response_matrix)(slot_rates)
    portion = lax.all_gather(traces[None], "work", axis=0, tiled=True)
    trace_rows = portion.reshape(-1, NT)
    motion = jnp.einsum("rt,jts->jrs", trace_rows, tables, preferred_element_type=jnp.float32)
    highest = jnp.max(jnp.abs(motion), axis=2).reshape(slot_count, portion.shape[0], V, NCOMP)
    result = jnp.transpose(highest, (0, 3, 1, 2))
    result = jnp.where(valid_slot[:, None, None, None], result, jnp.zeros_like(result))
    return result[None]


def solution(mesh):
    in_specs = (
        P("sgt", None, None, None, None),
        P("sgt", None, None),
        P(("sgt", "work"), None, None, None, None),
        P(),
        P(),
        P(),
        P(),
        P(),
    )
    out_specs = P("work", None, None, "sgt", None)
    return jax.shard_map(local, mesh=mesh, in_specs=in_specs, out_specs=out_specs, check_vma=False)
```

profile of v0, /device:TPU:0, one launch (start us, length us, event | category | flops | bytes accessed | tf_op | source)
XLA Modules:
  0.0 563.8 jit_solution(12710795290089663039)
XLA Ops:
  6.6 1.3 gather_fusion
  10.4 7.5 %multiply_reduce_fusion = bf16[4,2,128,1024]{3,2,1,0:T(8,128)(2,1)S(1)} fusion(bf16[4,6,2,128,1024]{4,3,2,1,0:T(8,128)(2,1)} %param.10, f32[4,6,128]{2,1,0:T(8,128)S(1)} %copy.29), kind=kLoop, calls=%fused_computation.12 | loop fusion | flops 17825792 | bytes 14692352 | tf_op jit(solution)/shard_map/reduce_sum | solution.py:20
  17.9 2.7 gather_fusion.2
  20.6 4.6 select_select_fusion
  25.3 5.5 all-to-all-start
  31.5 5.8 %copy.37 = bf16[1,8,64,128,32]{3,2,4,1,0:T(8,128)(2,1)} copy(bf16[1,8,64,128,32]{3,4,2,1,0:T(8,128)(2,1)} %param.12) | data formatting | bytes 8388608 | tf_op args[2]
  37.5 43.1 %all-to-all-done = bf16[8,2,128,1024]{3,2,1,0:T(8,128)(2,1)} async-done(((bf16[8,2,128,1024]{3,2,1,0:T(8,128)(2,1)}), bf16[8,2,128,1024]{3,2,1,0:T(8,128)(2,1)}, u32[]{:S(2)}, u32[]{:S(2)}) %all-to-all-start) | async-done | bytes 4194336 | tf_op jit(solution)/shard_map/all_to_all | solution.py:87
  80.6 306.1 %while.12 = (s32[]{:T(128)}, f32[64,2,1024]{2,0,1:T(8,128)S(1)}, s32[]{:T(128)}, bf16[8,64,128,32]{2,1,3,0:T(8,128)(2,1)}, s32[8]{0:T(128)S(1)}, /*index=5*/bf16...) while((s32[]{:T(128)}, f32[64,2,1024]{2,0,1:T(8,128)S(1)}, ...), condition=%wide.region_7.8_spmd, body=%wide.region_6.7_spmd.sunk | while | flops 1073872896 | bytes 112214472 | solution.py:95
  84.8 1.1 constant_dynamic-slice_fusion.4
  86.2 1.6 concatenate.11
  89.6 2.4 broadcast_in_dim.160
  92.0 6.7 %concatenate.12 = bf16[2,128,33824]{1,2,0:T(8,128)(2,1)} pad(bf16[2,128,33792]{1,2,0:T(8,128)(2,1)S(1)} %bitcast.49, bf16[]{:T(256)} %constant.152.clone.1..sunk), padding=0_0x0_0x0_32 | pad | bytes 34619392 | tf_op jit(solution)/shard_map/while/body/concatenate | solution.py:29
  98.7 15.7 %reshape.146 = bf16[2,128,32,1057]{1,3,2,0:T(8,128)(2,1)} reshape(bf16[2,128,33824]{1,2,0:T(8,128)(2,1)} %concatenate.12) | data formatting | bytes 34635776 | tf_op jit(solution)/shard_map/while/body/reshape | solution.py:30
  114.4 1.1 dynamic-slice_bitcast_fusion.2
  115.6 8.7 %fusion.40 = f32[64,2,1024]{2,0,1:T(8,128)S(1)} fusion(f32[64,2,1024]{2,0,1:T(8,128)S(1)} %get-tuple-element.196, bf16[2,128,32,1057]{1,3,2,0:T(8,128)(2,1)} %reshape.146, bf16[64,128,32]{1,0,2:T(8,128)(2,1)S(1)} %rev.7), kind=kOutput, calls=%fused_computation.6.clone.1 | convolution fusion | flops 1073872896 | bytes 18350080 | tf_op jit(solution)/shard_map/while/body/viq,ciqt->vct/dot_general | solution.py:41
  128.4 1.1 constant_dynamic-slice_fusion.4
  129.8 1.6 concatenate.11
  133.2 2.4 broadcast_in_dim.160
  135.6 6.7 %concatenate.12 = bf16[2,128,33824]{1,2,0:T(8,128)(2,1)} pad(bf16[2,128,33792]{1,2,0:T(8,128)(2,1)S(1)} %bitcast.49, bf16[]{:T(256)} %constant.152.clone.1..sunk), padding=0_0x0_0x0_32 | pad | bytes 34619392 | tf_op jit(solution)/shard_map/while/body/concatenate | solution.py:29
  142.3 15.7 %reshape.146 = bf16[2,128,32,1057]{1,3,2,0:T(8,128)(2,1)} reshape(bf16[2,128,33824]{1,2,0:T(8,128)(2,1)} %concatenate.12) | data formatting | bytes 34635776 | tf_op jit(solution)/shard_map/while/body/reshape | solution.py:30
  158.1 1.1 dynamic-slice_bitcast_fusion.2
  159.2 8.7 %fusion.40 = f32[64,2,1024]{2,0,1:T(8,128)S(1)} fusion(f32[64,2,1024]{2,0,1:T(8,128)S(1)} %get-tuple-element.196, bf16[2,128,32,1057]{1,3,2,0:T(8,128)(2,1)} %reshape.146, bf16[64,128,32]{1,0,2:T(8,128)(2,1)S(1)} %rev.7), kind=kOutput, calls=%fused_computation.6.clone.1 | convolution fusion | flops 1073872896 | bytes 18350080 | tf_op jit(solution)/shard_map/while/body/viq,ciqt->vct/dot_general | solution.py:41
  172.0 1.1 constant_dynamic-slice_fusion.4
  173.4 1.6 concatenate.11
  176.8 2.4 broadcast_in_dim.160
  179.2 6.7 %concatenate.12 = bf16[2,128,33824]{1,2,0:T(8,128)(2,1)} pad(bf16[2,128,33792]{1,2,0:T(8,128)(2,1)S(1)} %bitcast.49, bf16[]{:T(256)} %constant.152.clone.1..sunk), padding=0_0x0_0x0_32 | pad | bytes 34619392 | tf_op jit(solution)/shard_map/while/body/concatenate | solution.py:29
  185.9 15.7 %reshape.146 = bf16[2,128,32,1057]{1,3,2,0:T(8,128)(2,1)} reshape(bf16[2,128,33824]{1,2,0:T(8,128)(2,1)} %concatenate.12) | data formatting | bytes 34635776 | tf_op jit(solution)/shard_map/while/body/reshape | solution.py:30
  201.7 1.1 dynamic-slice_bitcast_fusion.2
  202.8 8.7 %fusion.40 = f32[64,2,1024]{2,0,1:T(8,128)S(1)} fusion(f32[64,2,1024]{2,0,1:T(8,128)S(1)} %get-tuple-element.196, bf16[2,128,32,1057]{1,3,2,0:T(8,128)(2,1)} %reshape.146, bf16[64,128,32]{1,0,2:T(8,128)(2,1)S(1)} %rev.7), kind=kOutput, calls=%fused_computation.6.clone.1 | convolution fusion | flops 1073872896 | bytes 18350080 | tf_op jit(solution)/shard_map/while/body/viq,ciqt->vct/dot_general | solution.py:41
  215.6 1.1 constant_dynamic-slice_fusion.4
  217.0 1.6 concatenate.11
  220.4 2.4 broadcast_in_dim.160
  222.8 6.7 %concatenate.12 = bf16[2,128,33824]{1,2,0:T(8,128)(2,1)} pad(bf16[2,128,33792]{1,2,0:T(8,128)(2,1)S(1)} %bitcast.49, bf16[]{:T(256)} %constant.152.clone.1..sunk), padding=0_0x0_0x0_32 | pad | bytes 34619392 | tf_op jit(solution)/shard_map/while/body/concatenate | solution.py:29
  229.5 15.7 %reshape.146 = bf16[2,128,32,1057]{1,3,2,0:T(8,128)(2,1)} reshape(bf16[2,128,33824]{1,2,0:T(8,128)(2,1)} %concatenate.12) | data formatting | bytes 34635776 | tf_op jit(solution)/shard_map/while/body/reshape | solution.py:30
  245.3 1.1 dynamic-slice_bitcast_fusion.2
  246.4 8.7 %fusion.40 = f32[64,2,1024]{2,0,1:T(8,128)S(1)} fusion(f32[64,2,1024]{2,0,1:T(8,128)S(1)} %get-tuple-element.196, bf16[2,128,32,1057]{1,3,2,0:T(8,128)(2,1)} %reshape.146, bf16[64,128,32]{1,0,2:T(8,128)(2,1)S(1)} %rev.7), kind=kOutput, calls=%fused_computation.6.clone.1 | convolution fusion | flops 1073872896 | bytes 18350080 | tf_op jit(solution)/shard_map/while/body/viq,ciqt->vct/dot_general | solution.py:41
  259.2 1.1 constant_dynamic-slice_fusion.4
  260.6 1.6 concatenate.11
  264.1 2.4 broadcast_in_dim.160
  266.4 6.7 %concatenate.12 = bf16[2,128,33824]{1,2,0:T(8,128)(2,1)} pad(bf16[2,128,33792]{1,2,0:T(8,128)(2,1)S(1)} %bitcast.49, bf16[]{:T(256)} %constant.152.clone.1..sunk), padding=0_0x0_0x0_32 | pad | bytes 34619392 | tf_op jit(solution)/shard_map/while/body/concatenate | solution.py:29
  273.2 15.7 %reshape.146 = bf16[2,128,32,1057]{1,3,2,0:T(8,128)(2,1)} reshape(bf16[2,128,33824]{1,2,0:T(8,128)(2,1)} %concatenate.12) | data formatting | bytes 34635776 | tf_op jit(solution)/shard_map/while/body/reshape | solution.py:30
  288.9 1.1 dynamic-slice_bitcast_fusion.2
  290.0 8.7 %fusion.40 = f32[64,2,1024]{2,0,1:T(8,128)S(1)} fusion(f32[64,2,1024]{2,0,1:T(8,128)S(1)} %get-tuple-element.196, bf16[2,128,32,1057]{1,3,2,0:T(8,128)(2,1)} %reshape.146, bf16[64,128,32]{1,0,2:T(8,128)(2,1)S(1)} %rev.7), kind=kOutput, calls=%fused_computation.6.clone.1 | convolution fusion | flops 1073872896 | bytes 18350080 | tf_op jit(solution)/shard_map/while/body/viq,ciqt->vct/dot_general | solution.py:41
  302.8 1.1 constant_dynamic-slice_fusion.4
  304.2 1.6 concatenate.11
  307.7 2.4 broadcast_in_dim.160
  310.0 6.7 %concatenate.12 = bf16[2,128,33824]{1,2,0:T(8,128)(2,1)} pad(bf16[2,128,33792]{1,2,0:T(8,128)(2,1)S(1)} %bitcast.49, bf16[]{:T(256)} %constant.152.clone.1..sunk), padding=0_0x0_0x0_32 | pad | bytes 34619392 | tf_op jit(solution)/shard_map/while/body/concatenate | solution.py:29
  316.8 15.7 %reshape.146 = bf16[2,128,32,1057]{1,3,2,0:T(8,128)(2,1)} reshape(bf16[2,128,33824]{1,2,0:T(8,128)(2,1)} %concatenate.12) | data formatting | bytes 34635776 | tf_op jit(solution)/shard_map/while/body/reshape | solution.py:30
  332.5 1.1 dynamic-slice_bitcast_fusion.2
  333.6 8.7 %fusion.40 = f32[64,2,1024]{2,0,1:T(8,128)S(1)} fusion(f32[64,2,1024]{2,0,1:T(8,128)S(1)} %get-tuple-element.196, bf16[2,128,32,1057]{1,3,2,0:T(8,128)(2,1)} %reshape.146, bf16[64,128,32]{1,0,2:T(8,128)(2,1)S(1)} %rev.7), kind=kOutput, calls=%fused_computation.6.clone.1 | convolution fusion | flops 1073872896 | bytes 18350080 | tf_op jit(solution)/shard_map/while/body/viq,ciqt->vct/dot_general | solution.py:41
  346.4 1.1 constant_dynamic-slice_fusion.4
  347.8 1.6 concatenate.11
  351.3 2.4 broadcast_in_dim.160
  353.6 6.7 %concatenate.12 = bf16[2,128,33824]{1,2,0:T(8,128)(2,1)} pad(bf16[2,128,33792]{1,2,0:T(8,128)(2,1)S(1)} %bitcast.49, bf16[]{:T(256)} %constant.152.clone.1..sunk), padding=0_0x0_0x0_32 | pad | bytes 34619392 | tf_op jit(solution)/shard_map/while/body/concatenate | solution.py:29
  360.4 15.7 %reshape.146 = bf16[2,128,32,1057]{1,3,2,0:T(8,128)(2,1)} reshape(bf16[2,128,33824]{1,2,0:T(8,128)(2,1)} %concatenate.12) | data formatting | bytes 34635776 | tf_op jit(solution)/shard_map/while/body/reshape | solution.py:30
  376.1 1.1 dynamic-slice_bitcast_fusion.2
  377.2 8.7 %fusion.40 = f32[64,2,1024]{2,0,1:T(8,128)S(1)} fusion(f32[64,2,1024]{2,0,1:T(8,128)S(1)} %get-tuple-element.196, bf16[2,128,32,1057]{1,3,2,0:T(8,128)(2,1)} %reshape.146, bf16[64,128,32]{1,0,2:T(8,128)(2,1)S(1)} %rev.7), kind=kOutput, calls=%fused_computation.6.clone.1 | convolution fusion | flops 1073872896 | bytes 18350080 | tf_op jit(solution)/shard_map/while/body/viq,ciqt->vct/dot_general | solution.py:41
  387.9 2.5 maximum_convert_fusion
  390.8 90.3 %all-gather.3.cloned.1.call-done = bf16[1024,2,1024]{2,0,1:T(8,128)(2,1)} async-done(((bf16[64,2,1024]{2,0,1:T(8,128)(2,1)}), bf16[1024,2,1024]{2,0,1:T(8,128)(2,1)}) %all-gather.3.cloned.1.call-update) | async-done | bytes 4194320 | tf_op jit(solution)/shard_map/all_gather | solution.py:110
  481.0 8.5 %copy.31 = bf16[1024,2,1024]{2,1,0:T(2,128)(2,1)} copy(bf16[1024,2,1024]{2,0,1:T(8,128)(2,1)} %all-gather.3.cloned.1.call-done) | data formatting | bytes 8388608 | tf_op jit(solution)/shard_map/all_gather | solution.py:110
  489.5 7.2 %reshape.141 = bf16[2048,1024,1]{1,0,2:T(8,128)(2,1)} reshape(bf16[1024,2,1024]{2,1,0:T(2,128)(2,1)} %copy.31) | data formatting | bytes 8388608 | tf_op jit(solution)/shard_map/reshape | solution.py:111
  496.7 57.2 %abs_reduce_fusion = f32[3,2048]{1,0:T(4,128)S(1)} fusion(bf16[2048,1024,1]{1,0,2:T(8,128)(2,1)} %reshape.141, f32[3]{0:T(128)S(1)} %get-tuple-element.132, f32[1024,1024]{0,1:T(8,128)} %maximum_convert_fusion, f32[3]{0:T(128)S(1)} %get-tuple-element.131, f32[3]{0:T(128)S(1)} %get-tuple-element.130, pred[1024,1024]{0,1:T(8,128)(4,1)S(1)} %fusion.17), kind=kOutput, calls=%fused_computation.11 | convolution fusion | flops 12919498752 | bytes 9461796 | tf_op jit(solution)/shard_map/rt,jts->jrs/dot_general | solution.py:112
  553.9 1.6 reshape.112
  555.8 1.1 copy.32
  (84 shorter events, 17.4 us)
Async XLA Ops:
  25.3 5.6 copy-start
  25.3 55.3 %all-to-all-start = ((bf16[8,2,128,1024]{3,2,1,0:T(8,128)(2,1)}), bf16[8,2,128,1024]{3,2,1,0:T(8,128)(2,1)}, u32[]{:S(2)}, u32[]{:S(2)}) async-start(bf16[8,2,128,1024]{3,2,1,0:T(8,128)(2,1)} %select_select_fusion), calls=%async_computation | async-start | bytes 8388608 | tf_op jit(solution)/shard_map/all_to_all | solution.py:87
  30.8 450.3 %all-gather.3.cloned.1.call-start = ((), (), s32[]{:S(2)}) async-start(), calls=%async_computation.1 | async-start | bytes 4456448 | tf_op jit(solution)/shard_map/all_gather | solution.py:110
  31.5 5.8 %copy-start.1 = (s32[128,8]{0,1:T(8,128)S(1)}, s32[128,8]{0,1:T(8,128)}, u32[]{:S(2)}) copy-start(s32[128,8]{0,1:T(8,128)} %param.13) | copy-start | bytes 12292
  31.5 5.8 %copy-start.2 = (s32[128,8]{0,1:T(8,128)S(1)}, s32[128,8]{0,1:T(8,128)}, u32[]{:S(2)}) copy-start(s32[128,8]{0,1:T(8,128)} %param.15) | copy-start | bytes 12292
  80.6 306.9 %copy-start.4 = (s32[44]{0:T(128)S(1)}, s32[44]{0:T(128)}, u32[]{:S(2)}) copy-start(s32[44]{0:T(128)} %param.17) | copy-start | bytes 532
  80.6 307.2 %copy-start.3 = (f32[44]{0:T(128)S(1)}, f32[44]{0:T(128)}, u32[]{:S(2)}) copy-start(f32[44]{0:T(128)} %param.16) | copy-start | bytes 532
Sparse Core Ops, SparseCore 0:
  387.6 93.4 all-gather.2
where the time goes:
time: 567 us; the launch traced here: 564 us
  local copies, waits for them, and re-layouts  243 us (43%)
  waiting for transfers between devices  133 us (23%)
  matrix products  118 us (21%)
  loops' own time  33.1 us (6%)
  other arithmetic  16.9 us (3%)
  between operations  13.5 us (2%)
    reshape x7, local copies, waits for them, and re-layouts, hankel(): return flattened.reshape(leading + (width, length + 1))[..., :steps]  110 us
    all_gather x1, waiting for transfers between devices, local(): portion = lax.all_gather(traces[None], 'work', axis=0, tiled=True)  90.3 us
    dot_general x7, matrix products, convolve(): jnp.einsum('viq,ciqt->vct', slip_window[:, :, ::-1], windows, preferred_e...  60.8 us
    dot_general x1, matrix products, local(): jnp.einsum('rt,jts->jrs', trace_rows, tables, preferred_element_type=jnp....  57.2 us
    concatenate x7, local copies, waits for them, and re-layouts, hankel(): jnp.concatenate([flattened, jnp.zeros(leading + (width,), shifted.dtype)]...  47 us
    all_to_all x1, waiting for transfers between devices, local(): lax.all_to_all(outgoing, 'sgt', split_axis=0, concat_axis=0, tiled=True)  43.1 us
    another operation x1, loops' own time, local(): lax.fori_loop(0, own_count, add_slot, jnp.zeros((V, NCOMP, NT), jnp.float...  33.1 us
    broadcast_in_dim x7, local copies, waits for them, and re-layouts, hankel(): jnp.broadcast_to(shifted[..., None, :], leading + (width, length))  16.6 us
  transfers between devices with their start and end apart: 2, of which 2 were waited for; matrix products, arithmetic and copies ran while one was open for 2% of the time, Pallas kernels for 0%

commit v1 on v0

v1 whole, which is shorter than its diff:
```python
import functools
import math

import jax
import jax.numpy as jnp
from jax import lax
from jax.experimental import pallas as pl
from jax.experimental.pallas import tpu as pltpu
from jax.sharding import PartitionSpec as P

NT = 1024
L = 32
KIR = 512
V = 64
PB = 128
NPER = 44
SLOTS = 8
HELD = 4
NJ = 6
PMAX = 3
OWNERS = 16
damping = 0.05

PHASES = 4
TAPS = 9
PADROWS = 16
BLOCK = 256
QSTEP = 4
VMEM = 60 * 1024 * 1024


def project_kernel(fp_ref, sgt_ref, mom_ref, out_ref, scr, sem):
    b = pl.program_id(0)
    me = lax.axis_index("sgt")
    work = lax.axis_index("work")
    weights = jnp.transpose(mom_ref[0])
    for c in range(2):
        for i in range(0, PB, 16):
            total = None
            for j in range(NJ):
                term = weights[i : i + 16, j : j + 1] * sgt_ref[0, j, c, i : i + 16, :].astype(
                    jnp.float32
                )
                total = term if total is None else total + term
            scr[b, c, i : i + 16, :] = total.astype(jnp.bfloat16)

    def wanted(g):
        base = (g * OWNERS + work) * SLOTS
        found = jnp.int32(0)
        for k in range(SLOTS):
            block = fp_ref[base + k]
            found = jnp.where(block // HELD == me, block % HELD, found)
        return found

    for g in range(SLOTS):
        copy = pltpu.make_async_copy(scr.at[b], out_ref.at[g], sem.at[g])
        pl.when(wanted(g) == b)(copy.start)

    @pl.when(b == HELD - 1)
    def _():
        for g in range(SLOTS):
            pltpu.make_async_copy(scr.at[0], out_ref.at[g], sem.at[g]).wait()


def project(footprint, sgt_tensor, moment):
    return pl.pallas_call(
        project_kernel,
        out_shape=jax.ShapeDtypeStruct((SLOTS, 2, PB, NT), jnp.bfloat16),
        grid_spec=pltpu.PrefetchScalarGridSpec(
            num_scalar_prefetch=1,
            grid=(HELD,),
            in_specs=[
                pl.BlockSpec((1, NJ, 2, PB, NT), lambda b, fp: (b, 0, 0, 0, 0)),
                pl.BlockSpec((1, NJ, PB), lambda b, fp: (b, 0, 0)),
            ],
            out_specs=pl.BlockSpec(memory_space=pl.ANY),
            scratch_shapes=[
                pltpu.VMEM((HELD, 2, PB, NT), jnp.bfloat16),
                pltpu.SemaphoreType.DMA((SLOTS,)),
            ],
        ),
        compiler_params=pltpu.CompilerParams(vmem_limit_bytes=VMEM),
        name="project",
    )(footprint, sgt_tensor, moment)


def tables_kernel(u_ref, v_ref, out_ref):
    columns = jnp.transpose(u_ref[0])
    row = lax.broadcasted_iota(jnp.int32, (BLOCK, BLOCK), 0)
    lane = lax.broadcasted_iota(jnp.int32, (BLOCK, BLOCK), 1)
    source = (lane % (BLOCK // PHASES)) * PHASES + lane // (BLOCK // PHASES)
    for n in range(QSTEP):
        sine = columns[:, 2 * n : 2 * n + 1]
        cosine = columns[:, 2 * n + 1 : 2 * n + 2]
        for j in range(3):
            span = slice(j * BLOCK, (j + 1) * BLOCK)
            value = sine * v_ref[0, 2 * n : 2 * n + 1, span] - (
                cosine * v_ref[0, 2 * n + 1 : 2 * n + 2, span]
            )
            if j == 0:
                value = jnp.where(row >= source, value, 0.0)
            if j == 2:
                value = jnp.where(row < source, value, 0.0)
            out_ref[n, :, span] = value.astype(jnp.bfloat16)


def tables(frequency):
    angular = frequency[:, None]
    damped = angular * math.sqrt(1.0 - damping * damping)
    rows = jnp.arange(BLOCK, dtype=jnp.float32)[None, :]
    decay = jnp.exp(-damping * angular * rows)
    u = jnp.stack([decay * jnp.sin(damped * rows), decay * jnp.cos(damped * rows)], axis=1)
    lane = jnp.arange(3 * BLOCK)
    inner = lane % BLOCK
    source = (inner % (BLOCK // PHASES)) * PHASES + inner // (BLOCK // PHASES)
    back = (source - (lane // BLOCK) * BLOCK).astype(jnp.float32)[None, :]
    growth = angular * angular / damped * jnp.exp(damping * angular * back)
    v = jnp.stack([growth * jnp.cos(damped * back), growth * jnp.sin(damped * back)], axis=1)
    steps = NPER // QSTEP
    return pl.pallas_call(
        tables_kernel,
        out_shape=jax.ShapeDtypeStruct((NPER, BLOCK, 3 * BLOCK), jnp.bfloat16),
        grid=(steps,),
        in_specs=[
            pl.BlockSpec((1, 2 * QSTEP, BLOCK), lambda s: (s, 0, 0)),
            pl.BlockSpec((1, 2 * QSTEP, 3 * BLOCK), lambda s: (s, 0, 0)),
        ],
        out_specs=pl.BlockSpec((QSTEP, BLOCK, 3 * BLOCK), lambda s: (s, 0, 0)),
        compiler_params=pltpu.CompilerParams(vmem_limit_bytes=VMEM),
        cost_estimate=pl.CostEstimate(
            flops=NPER * 3 * BLOCK * BLOCK * 5, bytes_accessed=20000000, transcendentals=0
        ),
        name="tables",
    )(u.reshape(steps, 2 * QSTEP, BLOCK), v.reshape(steps, 2 * QSTEP, 3 * BLOCK))


def gather_phases(delay, tensor_ref, phases):
    rows = lax.broadcasted_iota(jnp.int32, (BLOCK, 2 * BLOCK), 0)
    lane = lax.broadcasted_iota(jnp.int32, (BLOCK, 2 * BLOCK), 1)
    part = BLOCK // PHASES
    source = BLOCK + (rows % part) * PHASES + rows // part - delay
    pick = jnp.where(lane == source, 1.0, 0.0).astype(jnp.bfloat16)
    for a in range(NT // BLOCK):
        low = max(a - 1, 0) * BLOCK
        window = tensor_ref[:, low : (a + 1) * BLOCK]
        chosen = pick[:, 2 * BLOCK - window.shape[1] :]
        moved = lax.dot_general(
            chosen, window, (((1,), (1,)), ((), ())), preferred_element_type=jnp.float32
        )
        for c in range(2):
            for b in range(PHASES):
                phases[
                    c, PADROWS + a * part : PADROWS + (a + 1) * part, b * PB : (b + 1) * PB
                ] = moved[b * part : (b + 1) * part, c * PB : (c + 1) * PB]


def convolve_kernel(info_ref, tensor_ref, slip_ref, out_ref, phases, left, right, total):
    k = pl.program_id(0)

    @pl.when(k == 0)
    def _():
        total[...] = jnp.zeros_like(total)
        phases[:, :PADROWS, :] = jnp.zeros((2, PADROWS, PHASES * PB), jnp.float32)

    @pl.when(k < info_ref[0])
    def _():
        gather_phases(info_ref[1 + SLOTS + k], tensor_ref.at[0], phases)
        depth = PHASES * PB
        for j in range(TAPS):
            for c in range(2):
                left[c * BLOCK : (c + 1) * BLOCK, j * depth : (j + 1) * depth] = phases[
                    c, PADROWS - j : PADROWS - j + BLOCK, :
                ].astype(jnp.bfloat16)
            for b in range(PHASES):
                first = (PHASES * j - b + PHASES - b % 2) * V
                right[j * depth + b * PB : j * depth + (b + 1) * PB, :] = slip_ref[
                    0, b % 2, :, first : first + PHASES * V
                ]
        total[...] += jnp.dot(left[...], right[...], preferred_element_type=jnp.float32)

    @pl.when(k == SLOTS - 1)
    def _():
        part = BLOCK // PHASES
        lane = lax.broadcasted_iota(jnp.int32, (part, 2 * V), 1)
        for a in range(NT // BLOCK):
            for b in range(PHASES):
                half = slice((b // 2) * 2 * V, (b // 2 + 1) * 2 * V)
                first = total[a * part : (a + 1) * part, half]
                second = total[BLOCK + a * part : BLOCK + (a + 1) * part, half]
                if b % 2 == 0:
                    second = pltpu.roll(second, V, 1)
                else:
                    first = pltpu.roll(first, V, 1)
                out_ref[b * part : (b + 1) * part, a * 2 * V : (a + 1) * 2 * V] = jnp.where(
                    lane < V, first, second
                ).astype(jnp.bfloat16)


def convolve(info, incoming, slips):
    def live(k, info):
        return jnp.minimum(k, info[0] - 1)

    width = slips.shape[-1]
    return pl.pallas_call(
        convolve_kernel,
        out_shape=jax.ShapeDtypeStruct((BLOCK, NT // BLOCK * 2 * V), jnp.bfloat16),
        grid_spec=pltpu.PrefetchScalarGridSpec(
            num_scalar_prefetch=1,
            grid=(SLOTS,),
            in_specs=[
                pl.BlockSpec((1, 2 * PB, NT), lambda k, info: (info[1 + live(k, info)], 0, 0)),
                pl.BlockSpec((1, 2, PB, width), lambda k, info: (live(k, info), 0, 0, 0)),
            ],
            out_specs=pl.BlockSpec((BLOCK, NT // BLOCK * 2 * V), lambda k, info: (0, 0)),
            scratch_shapes=[
                pltpu.VMEM((2, PADROWS + BLOCK, PHASES * PB), jnp.float32),
                pltpu.VMEM((2 * BLOCK, TAPS * PHASES * PB), jnp.bfloat16),
                pltpu.VMEM((TAPS * PHASES * PB, PHASES * V), jnp.bfloat16),
                pltpu.VMEM((2 * BLOCK, PHASES * V), jnp.float32),
            ],
        ),
        compiler_params=pltpu.CompilerParams(vmem_limit_bytes=VMEM),
        name="convolve",
    )(info, incoming, slips)


def motion_kernel(place_ref, table_ref, trace_ref, out_ref, stacked):
    step = pl.program_id(0)
    width = NT // BLOCK * 2 * V

    @pl.when(step == 0)
    def _():
        out_ref[...] = jnp.zeros_like(out_ref)
        for j in range(3):
            shift = j * 2 * V
            rows = slice(j * BLOCK, (j + 1) * BLOCK)
            if j > 0:
                stacked[rows, :shift] = jnp.zeros((BLOCK, shift), jnp.bfloat16)
            stacked[rows, shift:] = trace_ref[:, : width - shift]

    for n in range(QSTEP):
        early = jnp.dot(
            table_ref[n, :, : 2 * BLOCK],
            stacked[: 2 * BLOCK, : width // 2],
            preferred_element_type=jnp.float32,
        )
        late = jnp.dot(
            table_ref[n], stacked[:, width // 2 :], preferred_element_type=jnp.float32
        )
        both = jnp.maximum(jnp.abs(early), jnp.abs(late))
        highest = jnp.max(both, axis=0, keepdims=True)
        highest = jnp.maximum(highest[:, : 2 * V], highest[:, 2 * V :])
        out_ref[pl.ds(place_ref[step * QSTEP + n], 1), :] = highest


def motion(place, table, traces):
    return pl.pallas_call(
        motion_kernel,
        out_shape=jax.ShapeDtypeStruct((OWNERS * PMAX, 2 * V), jnp.float32),
        grid_spec=pltpu.PrefetchScalarGridSpec(
            num_scalar_prefetch=1,
            grid=(NPER // QSTEP,),
            in_specs=[
                pl.BlockSpec((QSTEP, BLOCK, 3 * BLOCK), lambda s, place: (s, 0, 0)),
                pl.BlockSpec((BLOCK, NT // BLOCK * 2 * V), lambda s, place: (0, 0)),
            ],
            out_specs=pl.BlockSpec((OWNERS * PMAX, 2 * V), lambda s, place: (0, 0)),
            scratch_shapes=[pltpu.VMEM((3 * BLOCK, NT // BLOCK * 2 * V), jnp.bfloat16)],
        ),
        compiler_params=pltpu.CompilerParams(vmem_limit_bytes=VMEM),
        name="motion",
    )(place, table, traces)


def local(
    sgt_tensor, moment, slip_rate, footprint, live_blocks, start_delay, frequency, period_owner
):
    rupture = lax.axis_index("sgt") * OWNERS + lax.axis_index("work")
    outgoing = project(footprint.reshape(-1), sgt_tensor, moment)
    incoming = lax.all_to_all(outgoing, "sgt", split_axis=0, concat_axis=0, tiled=True)

    own_blocks = lax.dynamic_index_in_dim(footprint, rupture, 0, keepdims=False)
    own_count = lax.dynamic_index_in_dim(live_blocks, rupture, 0)
    own_delays = lax.dynamic_index_in_dim(start_delay, rupture, 0, keepdims=False)
    info = jnp.concatenate([own_count, own_blocks // HELD, own_delays])

    slips = jnp.transpose(slip_rate[0], (0, 2, 3, 1)).reshape(SLOTS, PB, L * V)
    zeros = jnp.zeros((SLOTS, PB, PHASES * V), slips.dtype)
    even = jnp.concatenate([zeros, slips, zeros], axis=2)
    odd = jnp.concatenate([zeros[..., V:], slips, zeros, zeros[..., :V]], axis=2)
    slips = jnp.stack([even, odd], axis=1)

    table = tables(frequency)
    period_ids = jnp.arange(NPER)
    same_owner = period_owner[:, None] == period_owner[None, :]
    earlier = period_ids[None, :] < period_ids[:, None]
    place = period_owner * PMAX + jnp.sum(same_owner & earlier, axis=1).astype(jnp.int32)

    traces = convolve(info, incoming.reshape(SLOTS, 2 * PB, NT), slips)
    peaks = motion(place, table, traces)
    peaks = lax.all_to_all(
        peaks.reshape(OWNERS, PMAX, 2 * V), "work", split_axis=0, concat_axis=0, tiled=True
    )
    result = jnp.transpose(peaks.reshape(OWNERS, PMAX, 2, V), (1, 2, 0, 3))
    return result[None]


def solution(mesh):
    in_specs = (
        P("sgt", None, None, None, None),
        P("sgt", None, None),
        P(("sgt", "work"), None, None, None, None),
        P(),
        P(),
        P(),
        P(),
        P(),
    )
    out_specs = P("work", None, None, "sgt", None)
    return jax.shard_map(local, mesh=mesh, in_specs=in_specs, out_specs=out_specs, check_vma=False)
```

time: 567 us -> 126 us (0.22)
  local copies, waits for them, and re-layouts: 243 us -> 29.2 us
  waiting for transfers between devices: 133 us -> 0.01 us
  matrix products: 118 us -> 0 us
  Pallas kernels: 0 us -> 54.6 us
  loops' own time: 33.1 us -> 0 us
  blocking collectives: 0 us -> 13.9 us
  between operations: 13.5 us -> 0.12 us
    dot_general x8 -> x0, matrix products: 118 us -> none  [the longest x7 60.8 us: convolve(): jnp.einsum('viq,ciqt->vct', slip_window[:, :, ::-1], windows, preferred_e...]
    reshape x9 -> x6, local copies, waits for them, and re-layouts: 119 us -> 9.7 us  [the longest x1 6.59 us: local(): slips = jnp.transpose(slip_rate[0], (0, 2, 3, 1)).reshape(SLOTS, PB, L * V)]
    all_gather x1 -> x0, waiting for transfers between devices: 90.3 us -> none  [local(): portion = lax.all_gather(traces[None], 'work', axis=0, tiled=True)]
    pallas_call x0 -> x4, Pallas kernels: none -> 54.6 us  [the longest x1 17.5 us: convolve(): pl.pallas_call(convolve_kernel, out_shape=jax.ShapeDtypeStruct((BLOCK, NT...]
    concatenate x14 -> x1, local copies, waits for them, and re-layouts: 58.4 us -> 10 us  [local(): jnp.concatenate([zeros[..., V:], slips, zeros, zeros[..., :V]], axis=2)]
    all_to_all x1, waiting for transfers between devices: 43.1 us -> 0.01 us  [local(): lax.all_to_all(outgoing, 'sgt', split_axis=0, concat_axis=0, tiled=True)]
    another operation x1 -> x0, loops' own time: 33.1 us -> none  [local(): lax.fori_loop(0, own_count, add_slot, jnp.zeros((V, NCOMP, NT), jnp.float...]
    dynamic_slice x36 -> x1, local copies, waits for them, and re-layouts: 19.8 us -> 0.58 us  [local(): own_count = lax.dynamic_index_in_dim(live_blocks, rupture, 0)]
  transfers between devices with their start and end apart: 2 -> 1, of which waited for: 2 -> 0; matrix products, arithmetic and copies ran while one was open for 2% -> 38% of each run, Pallas kernels for 0% -> 10%
where the time goes in v1:
time: 126 us
  Pallas kernels  54.6 us (43%)
  local copies, waits for them, and re-layouts  29.2 us (23%)
  other arithmetic  22.3 us (18%)
  blocking collectives  13.9 us (11%)
  starting transfers between devices  5.53 us (4%)
    pallas_call x1, Pallas kernels, convolve(): pl.pallas_call(convolve_kernel, out_shape=jax.ShapeDtypeStruct((BLOCK, NT...  17.5 us
    pallas_call x1, Pallas kernels, motion(): pl.pallas_call(motion_kernel, out_shape=jax.ShapeDtypeStruct((OWNERS * PM...  15.2 us
    another operation x2, other arithmetic, local(): slips = jnp.stack([even, odd], axis=1)  14 us
    all_to_all x1, blocking collectives, local(): lax.all_to_all(peaks.reshape(OWNERS, PMAX, 2 * V), 'work', split_axis=0,...  13.9 us
    pallas_call x1, Pallas kernels, tables(): pl.pallas_call(tables_kernel, out_shape=jax.ShapeDtypeStruct((NPER, BLOCK...  12.2 us
    concatenate x1, local copies, waits for them, and re-layouts, local(): jnp.concatenate([zeros[..., V:], slips, zeros, zeros[..., :V]], axis=2)  10 us
    pallas_call x1, Pallas kernels, project(): pl.pallas_call(project_kernel, out_shape=jax.ShapeDtypeStruct((SLOTS, 2,...  9.65 us
    unnamed x13, local copies, waits for them, and re-layouts  7.96 us
  transfers between devices with their start and end apart: 1, of which 0 were waited for; matrix products, arithmetic and copies ran while one was open for 38% of the time, Pallas kernels for 10%

profile of v1, /device:TPU:0, one launch (start us, length us, event | category | flops | bytes accessed | tf_op | source)
XLA Modules:
  0.0 125.6 jit_solution(10134256352542719960)
XLA Ops:
  0.0 0.8 copy.19
  0.8 0.7 reshape.384.fp_ref
  1.5 1.3 %copy.20.mom_ref = f32[4,6,128]{2,1,0:T(8,128)} copy(f32[4,6,128]{2,0,1:T(4,128)} %param.9) | data formatting | bytes 24576 | tf_op args[1]
  2.8 9.7 %project.1 = bf16[8,2,128,1024]{3,2,1,0:T(8,128)(2,1)} custom-call(s32[1024]{0:T(1024)} %reshape.384.fp_ref, bf16[4,6,2,128,1024]{4,3,2,1,0:T(8,128)(2,1)} %sgt_ref.1, f32[4,6,128]{2,1,0:T(8,128)} %copy.20.mom_ref), custom_call_target="tpu_custom_call" | custom-call | tf_op jit(solution)/shard_map/project/pallas_call | solution.py:66
  12.4 5.5 %all-to-all-start = ((bf16[8,2,128,1024]{3,2,1,0:T(8,128)(2,1)}), bf16[8,2,128,1024]{3,2,1,0:T(8,128)(2,1)}, u32[]{:S(2)}, u32[]{:S(2)}) async-start(bf16[8,2,128,1024]{3,2,1,0:T(8,128)(2,1)} %project.1), calls=%async_computation | async-start | bytes 8388608 | tf_op jit(solution)/shard_map/all_to_all | solution.py:280
  18.0 5.8 %copy.21 = bf16[1,8,64,128,32]{3,2,4,1,0:T(8,128)(2,1)} copy(bf16[1,8,64,128,32]{3,4,2,1,0:T(8,128)(2,1)} %param.10) | data formatting | bytes 8388608 | tf_op args[2]
  23.8 0.0 copy-start.2
  23.8 0.0 copy-start.3
  23.8 6.6 %copy.22 = bf16[8,128,2048]{2,1,0:T(8,128)(2,1)} copy(bf16[8,128,2048]{1,2,0:T(8,128)(2,1)} %bitcast.15) | data formatting | bytes 8388608 | tf_op jit(solution)/shard_map/reshape | solution.py:287
  30.4 0.0 copy-done.2
  30.4 4.4 %fusion = (f32[44,1,768]{2,1,0:T(1,128)S(1)}, f32[44,1,768]{2,1,0:T(1,128)S(1)}) fusion(f32[768]{0:T(1024)S(1)} %fusion.12, f32[44]{0:T(128)S(1)} %get-tuple-element.10, f32[44]{0:T(128)S(1)} %get-tuple-element.12, f32[44]{0:T(128)S(1)} %get-tuple-element.9), kind=kLoop, calls=%fused_computation.5 | loop fusion | flops 168960 | bytes 273936 | tf_op jit(solution)/shard_map/mul | solution.py:118
  34.8 0.2 pad_maximum_fusion.1
  35.1 0.9 reshape.383.v_ref
  36.0 1.5 %sine_multiply_fusion = (f32[44,1,256]{2,1,0:T(1,128)S(1)}, f32[44,1,256]{2,1,0:T(1,128)S(1)}) fusion(f32[44]{0:T(128)S(1)} %get-tuple-element.10, f32[44]{0:T(128)S(1)} %get-tuple-element.11), kind=kLoop, calls=%fused_computation.10 | loop fusion | flops 45056 | bytes 90464 | tf_op jit(solution)/shard_map/mul | solution.py:112
  37.5 0.1 pad_maximum_fusion.2
  37.6 0.7 reshape.382.u_ref
  38.3 0.0 copy-done.3
  38.3 0.6 dynamic_slice.11
  39.0 0.0 copy-start
  39.0 0.0 copy-start.1
  39.0 10.0 %concatenate.11 = bf16[8,128,2560]{2,1,0:T(8,128)(2,1)} concatenate(bf16[8,128,192]{2,1,0:T(8,128)(2,1)S(1)} %slice.6, bf16[8,128,2048]{2,1,0:T(8,128)(2,1)} %copy.22, bf16[8,128,256]{2,1,0:T(8,128)(2,1)S(1)} %broadcast_in_dim.4, bf16[8,128,64]{2,1,0:T(8,128)(2,1)S(1)} %slice.7), dimensions={2} | concatenate | bytes 10485760 | tf_op jit(solution)/shard_map/concatenate | solution.py:290
  49.1 0.0 copy-done
  49.1 0.0 copy-done.1
  49.1 0.2 dynamic-slice_reduce_fusion
  49.3 0.0 copy-start.4
  49.3 12.2 %tables.1.table_ref = bf16[44,256,768]{2,1,0:T(8,128)(2,1)} custom-call(f32[11,8,256]{2,1,0:T(8,128)} %reshape.382.u_ref, f32[11,8,768]{2,1,0:T(8,128)} %reshape.383.v_ref), custom_call_target="tpu_custom_call" | custom-call | flops 43253760 | bytes 20000000 | tf_op jit(solution)/shard_map/tables/pallas_call | solution.py:120
  61.5 1.2 pad_add_fusion.info_ref
  62.8 0.0 copy-done.4
  62.8 0.2 convert_reduce_fusion
  62.9 0.6 multiply_add_fusion.place_ref
  63.5 5.0 %maximum_bitcast_fusion = bf16[8,1,128,2560]{3,2,1,0:T(8,128)(2,1)} fusion(bf16[8,128,256]{2,1,0:T(8,128)(2,1)S(1)} %broadcast_in_dim.4, bf16[8,128,2048]{2,1,0:T(8,128)(2,1)} %copy.22), kind=kLoop, calls=%fused_computation.1 | loop fusion | flops 15728640 | bytes 9961472 | tf_op jit(solution)/shard_map/stack | solution.py:291
  68.5 9.0 %pad_maximum_fusion.slip_ref = bf16[8,2,128,2560]{3,2,1,0:T(8,128)(2,1)} fusion(bf16[8,1,128,2560]{3,2,1,0:T(8,128)(2,1)} %bitcast.14, bf16[8,1,128,2560]{3,2,1,0:T(8,128)(2,1)} %maximum_bitcast_fusion), kind=kLoop, calls=%fused_computation | loop fusion | flops 5242880 | bytes 20971520 | tf_op jit(solution)/shard_map/stack | solution.py:291
  77.6 0.0 all-to-all-done
  77.6 17.5 %convolve.1.trace_ref = bf16[256,512]{1,0:T(8,128)(2,1)} custom-call(s32[17]{0:T(128)} %pad_add_fusion.info_ref, bf16[8,256,1024]{2,1,0:T(8,128)(2,1)} %bitcast.tensor_ref, bf16[8,2,128,2560]{3,2,1,0:T(8,128)(2,1)} %pad_maximum_fusion.slip_ref), custom_call_target="tpu_custom_call" | custom-call | tf_op jit(solution)/shard_map/convolve/pallas_call | solution.py:204
  95.1 15.2 %motion.1 = f32[48,128]{1,0:T(8,128)} custom-call(s32[44]{0:T(128)} %multiply_add_fusion.place_ref, bf16[44,256,768]{2,1,0:T(8,128)(2,1)} %tables.1.table_ref, bf16[256,512]{1,0:T(8,128)(2,1)} %convolve.1.trace_ref), custom_call_target="tpu_custom_call" | custom-call | tf_op jit(solution)/shard_map/motion/pallas_call | solution.py:257
  110.3 0.8 reshape.387
  111.1 13.9 %all_to_all.10 = f32[16,3,128]{2,1,0:T(4,128)S(1)} all-to-all(f32[16,3,128]{2,1,0:T(4,128)S(1)} %reshape.387), channel_id=1, replica_groups=mesh['sgt'=8,'work'=16] {'work'}, dimensions={0} | all-to-all | bytes 49152 | tf_op jit(solution)/shard_map/all_to_all | solution.py:301
  124.9 0.1 reshape.388
  125.0 0.6 copy.25
  (7 shorter events, 0.1 us)
Async XLA Ops:
  12.4 65.1 %all-to-all-start = ((bf16[8,2,128,1024]{3,2,1,0:T(8,128)(2,1)}), bf16[8,2,128,1024]{3,2,1,0:T(8,128)(2,1)}, u32[]{:S(2)}, u32[]{:S(2)}) async-start(bf16[8,2,128,1024]{3,2,1,0:T(8,128)(2,1)} %project.1), calls=%async_computation | async-start | bytes 8388608 | tf_op jit(solution)/shard_map/all_to_all | solution.py:280
  23.8 6.6 %copy-start.2 = (f32[44]{0:T(128)S(1)}, f32[44]{0:T(128)}, u32[]{:S(2)}) copy-start(f32[44]{0:T(128)} %param.14) | copy-start | bytes 532
  23.8 14.5 %copy-start.3 = (s32[128]{0:T(128)S(1)}, s32[128]{0:T(128)}, u32[]{:S(2)}) copy-start(s32[128]{0:T(128)} %param.12) | copy-start | bytes 1540
  39.0 10.1 %copy-start = (s32[128,8]{0,1:T(8,128)S(1)}, s32[128,8]{0,1:T(8,128)}, u32[]{:S(2)}) copy-start(s32[128,8]{0,1:T(8,128)} %param.11) | copy-start | bytes 12292
  39.0 10.1 %copy-start.1 = (s32[128,8]{0,1:T(8,128)S(1)}, s32[128,8]{0,1:T(8,128)}, u32[]{:S(2)}) copy-start(s32[128,8]{0,1:T(8,128)} %param.13) | copy-start | bytes 12292
  49.3 13.5 %copy-start.4 = (s32[44]{0:T(128)S(1)}, s32[44]{0:T(128)}, u32[]{:S(2)}) copy-start(s32[44]{0:T(128)} %param.15) | copy-start | bytes 532

commit v2 on v0

v2 whole, which is shorter than its diff:
```python
import functools
import math

import jax
import jax.numpy as jnp
from jax import lax
from jax.experimental import pallas as pl
from jax.experimental.pallas import tpu as pltpu
from jax.sharding import PartitionSpec as P

NT = 1024
L = 32
KIR = 512
V = 64
PB = 128
NPER = 44
SLOTS = 8
HELD = 4
NJ = 6
PMAX = 3
OWNERS = 16
damping = 0.05

PHASES = 4
TAPS = 9
PADROWS = 16
BLOCK = 256
SPAN = 128
TSTEP = 4
QSTEP = 11
SMALL = 12 * 1024 * 1024
LARGE = 28 * 1024 * 1024
PROJECT = 48 * 1024 * 1024

STEPS = ((0, 0), (0, 1), (2, 0), (2, 1), (1, 0), (3, 0), (1, 1), (3, 1))
GROUPS = ((0, 1), (2, 3), (4, 5), (6,), (7,))


def target(place, dz, dc):
    return ((place + 2 * dz) & 7) ^ dc


def origin(place, dz, dc):
    return ((place - 2 * dz) & 7) ^ dc


def project_block(weights, taken, scr, c):
    for i in range(0, PB, 16):
        total = None
        for j in range(NJ):
            term = weights[i : i + 16, j : j + 1] * taken[j, c, i : i + 16, :].astype(jnp.float32)
            total = term if total is None else total + term
        scr[c * PB + i : c * PB + i + 16, :] = total.astype(jnp.bfloat16)


def project_kernel(steps, fp_ref, sgt_ref, mom_ref, *rest):
    count = len(steps)
    outs, taken, scr, table, moments, in_sem, out_sem, small_sem = rest[:count], *rest[count:]
    fetch_table = pltpu.make_async_copy(fp_ref, table, small_sem.at[0])
    fetch_moments = pltpu.make_async_copy(mom_ref, moments, small_sem.at[1])
    fetch_table.start()
    fetch_moments.start()
    me = lax.axis_index("sgt")
    work = lax.axis_index("work")

    def load(n, c):
        return pltpu.make_async_copy(
            sgt_ref.at[n, :, c], taken.at[n, :, c], in_sem.at[2 * n + c]
        )

    for n in range(HELD):
        for c in range(2):
            load(n, c).start()
    fetch_table.wait()
    chosen = []
    for dz, dc in steps:
        rupture = target(me, dz, dc) * OWNERS + work
        found = jnp.int32(0)
        for k in range(SLOTS):
            block = table[k, rupture]
            found = jnp.where((block >> 2) == me, block & 3, found)
        chosen.append(found)
    fetch_moments.wait()

    @pl.loop(0, HELD)
    def _(n):
        weights = jnp.transpose(
            jnp.concatenate([moments[j, pl.ds(n, 1), :] for j in range(NJ)], axis=0)
        )
        for c in range(2):
            load(n, c).wait()
            project_block(weights, taken.at[n], scr.at[n], c)
        for m in range(count):
            copy = pltpu.make_async_copy(scr.at[n], outs[m], out_sem.at[m])
            pl.when(chosen[m] == n)(copy.start)

    for m in range(count):
        pltpu.make_async_copy(scr.at[0], outs[m], out_sem.at[m]).wait()


def project(steps, footprint, sgt_tensor, moment):
    count = len(steps)
    return pl.pallas_call(
        functools.partial(project_kernel, steps),
        out_shape=[jax.ShapeDtypeStruct((2 * PB, NT), jnp.bfloat16)] * count,
        in_specs=[
            pl.BlockSpec(memory_space=pl.ANY),
            pl.BlockSpec(memory_space=pl.ANY),
            pl.BlockSpec(memory_space=pl.ANY),
        ],
        out_specs=[pl.BlockSpec(memory_space=pltpu.VMEM)] * count,
        scratch_shapes=[
            pltpu.VMEM((HELD, NJ, 2, PB, NT), jnp.bfloat16),
            pltpu.VMEM((HELD, 2 * PB, NT), jnp.bfloat16),
            pltpu.SMEM((SLOTS, 128), jnp.int32),
            pltpu.VMEM((NJ, HELD, PB), jnp.float32),
            pltpu.SemaphoreType.DMA((2 * HELD,)),
            pltpu.SemaphoreType.DMA((count,)),
            pltpu.SemaphoreType.DMA((2,)),
        ],
        compiler_params=pltpu.CompilerParams(vmem_limit_bytes=PROJECT),
        cost_estimate=pl.CostEstimate(
            flops=HELD * 100000000, bytes_accessed=HELD * 3200000, transcendentals=0
        ),
        name="project",
    )(footprint.T, sgt_tensor, jnp.transpose(moment, (1, 0, 2)))


def tables_kernel(u_ref, v_ref, out_ref):
    step = pl.program_id(0)
    columns = jnp.transpose(u_ref[0])
    row = lax.broadcasted_iota(jnp.int32, (SPAN, SPAN), 0)
    lane = lax.broadcasted_iota(jnp.int32, (SPAN, SPAN), 1)
    source = ((lane & 31) << 2) + (lane >> 5)
    for n in range(TSTEP):
        sine = columns[:, 2 * n : 2 * n + 1]
        cosine = columns[:, 2 * n + 1 : 2 * n + 2]
        for j in range(3):
            span = slice(j * SPAN, (j + 1) * SPAN)
            value = sine * v_ref[0, 2 * n : 2 * n + 1, span] + (
                cosine * v_ref[0, 2 * n + 1 : 2 * n + 2, span]
            )
            if j == 0:
                value = jnp.where(row >= source, value, 0.0)
            if j == 2:
                value = jnp.where(row < source, value, 0.0)
            out_ref[n, :, span] = value.astype(jnp.bfloat16)
        state = 2 * (step * TSTEP + n)
        value = jnp.where(lane == state, sine, 0.0) + jnp.where(lane == state + 1, cosine, 0.0)
        out_ref[n, :, 3 * SPAN :] = value.astype(jnp.bfloat16)


def tables(frequency):
    angular = frequency[:, None]
    damped = angular * math.sqrt(1.0 - damping * damping)
    rows = jnp.arange(SPAN, dtype=jnp.float32)[None, :]
    decay = jnp.exp(-damping * angular * rows)
    u = jnp.stack([decay * jnp.sin(damped * rows), decay * jnp.cos(damped * rows)], axis=1)
    lane = jnp.arange(5 * SPAN)
    inner = lane % SPAN
    source = ((inner & 31) << 2) + (inner >> 5)
    before = jnp.asarray([0, 1, 4, 2, 3])[lane // SPAN]
    back = (source - before * SPAN).astype(jnp.float32)[None, :]
    growth = angular * angular / damped * jnp.exp(damping * angular * back)
    v = jnp.stack([growth * jnp.cos(damped * back), -growth * jnp.sin(damped * back)], axis=1)
    weights = v[..., 3 * SPAN :].reshape(2 * NPER, 2 * SPAN)
    weights = jnp.pad(weights, ((0, SPAN - 2 * NPER), (0, 0))).astype(jnp.bfloat16)
    steps = NPER // TSTEP
    table = pl.pallas_call(
        tables_kernel,
        out_shape=jax.ShapeDtypeStruct((NPER, SPAN, 4 * SPAN), jnp.bfloat16),
        grid=(steps,),
        in_specs=[
            pl.BlockSpec((1, 2 * TSTEP, SPAN), lambda s: (s, 0, 0)),
            pl.BlockSpec((1, 2 * TSTEP, 3 * SPAN), lambda s: (s, 0, 0)),
        ],
        out_specs=pl.BlockSpec((TSTEP, SPAN, 4 * SPAN), lambda s: (s, 0, 0)),
        compiler_params=pltpu.CompilerParams(vmem_limit_bytes=SMALL),
        cost_estimate=pl.CostEstimate(
            flops=NPER * 4 * SPAN * SPAN * 5, bytes_accessed=6000000, transcendentals=0
        ),
        name="tables",
    )(u.reshape(steps, 2 * TSTEP, SPAN), v[..., : 3 * SPAN].reshape(steps, 2 * TSTEP, 3 * SPAN))
    return table, weights


def gather_phases(delay, tensor_ref, phases):
    rows = lax.broadcasted_iota(jnp.int32, (BLOCK, 2 * BLOCK), 0)
    lane = lax.broadcasted_iota(jnp.int32, (BLOCK, 2 * BLOCK), 1)
    part = BLOCK // PHASES
    source = BLOCK + ((rows & 63) << 2) + (rows >> 6) - delay
    pick = jnp.where(lane == source, 1.0, 0.0).astype(jnp.bfloat16)
    for a in range(NT // BLOCK):
        low = max(a - 1, 0) * BLOCK
        window = tensor_ref[:, low : (a + 1) * BLOCK]
        chosen = pick[:, 2 * BLOCK - window.shape[1] :]
        moved = lax.dot_general(
            chosen, window, (((1,), (1,)), ((), ())), preferred_element_type=jnp.float32
        )
        for c in range(2):
            for b in range(PHASES):
                phases[
                    c, PADROWS + a * part : PADROWS + (a + 1) * part, b * PB : (b + 1) * PB
                ] = moved[b * part : (b + 1) * part, c * PB : (c + 1) * PB]


def histories(slips, slot, shift):
    pieces = []
    for b in range(PHASES):
        first = PHASES * shift - b
        low, high = max(first, 0), min(first + PHASES, L)
        if high <= low:
            pieces.append(jnp.zeros((PHASES * V, PB), jnp.bfloat16))
            continue
        parts = [slips[slot, low * V : high * V, :]]
        if low > first:
            parts.insert(0, jnp.zeros(((low - first) * V, PB), jnp.bfloat16))
        if high < first + PHASES:
            parts.append(jnp.zeros(((first + PHASES - high) * V, PB), jnp.bfloat16))
        pieces.append(parts[0] if len(parts) == 1 else jnp.concatenate(parts, axis=0))
    return jnp.concatenate(pieces, axis=1)


def convolve_kernel(arrivals, begins, info_ref, *rest):
    count = len(arrivals)
    tensors, slips, rest = rest[:count], rest[count], rest[count + 1 :]
    before = None
    if not begins:
        before, rest = rest[0], rest[1:]
    out_ref, phases = rest
    for half in range(2):
        phases[half, :, :PADROWS, :] = jnp.zeros((2, PADROWS, PHASES * PB), jnp.float32)
    for n in range(count):
        half = n % 2
        slot = info_ref[arrivals[n]]
        gather_phases(info_ref[SLOTS + arrivals[n]], tensors[n], phases.at[half])
        for c in range(2):
            rows = slice(c * BLOCK, (c + 1) * BLOCK)
            term = None
            for j in range(TAPS):
                shifted = phases[half, c, PADROWS - j : PADROWS - j + BLOCK, :]
                product = lax.dot_general(
                    shifted.astype(jnp.bfloat16),
                    histories(slips, slot, j),
                    (((1,), (1,)), ((), ())),
                    preferred_element_type=jnp.float32,
                )
                term = product if term is None else term + product
            if n > 0:
                out_ref[rows, :] += term
            elif begins:
                out_ref[rows, :] = term
            else:
                out_ref[rows, :] = before[rows, :] + term


def convolve(arrivals, info, tensors, slips, before):
    count = len(arrivals)
    vmem = pl.BlockSpec(memory_space=pltpu.VMEM)
    begins = before is None
    return pl.pallas_call(
        functools.partial(convolve_kernel, arrivals, begins),
        out_shape=jax.ShapeDtypeStruct((2 * BLOCK, PHASES * V), jnp.float32),
        in_specs=[pl.BlockSpec(memory_space=pltpu.SMEM)]
        + [vmem] * (count + 1)
        + ([] if begins else [vmem]),
        out_specs=vmem,
        scratch_shapes=[
            pltpu.VMEM((2, 2, PADROWS + BLOCK, PHASES * PB), jnp.float32),
        ],
        compiler_params=pltpu.CompilerParams(vmem_limit_bytes=LARGE),
        cost_estimate=pl.CostEstimate(
            flops=count * 1800000000, bytes_accessed=count * 1048576, transcendentals=0
        ),
        name="convolve",
    )(info, *tensors, slips, *([] if begins else [before]))


def motion_kernel(place_ref, table_ref, weights_ref, total, out_ref, traces, stacked):
    step = pl.program_id(0)
    spans = NT // SPAN
    wide = 2 * V
    width = spans * wide

    @pl.when(step == 0)
    def _():
        out_ref[...] = jnp.zeros_like(out_ref)
        part = SPAN // PHASES
        lane = lax.broadcasted_iota(jnp.int32, (part, wide), 1)
        for a in range(spans):
            for b in range(PHASES):
                half = slice((b // 2) * wide, (b // 2 + 1) * wide)
                first = total[a * part : (a + 1) * part, half]
                second = total[BLOCK + a * part : BLOCK + (a + 1) * part, half]
                if b % 2 == 0:
                    second = pltpu.roll(second, V, 1)
                else:
                    first = pltpu.roll(first, V, 1)
                traces[b * part : (b + 1) * part, a * wide : (a + 1) * wide] = jnp.where(
                    lane < V, first, second
                ).astype(jnp.bfloat16)
        stacked[:SPAN, :] = traces[...]
        for j, n in ((1, 1), (2, 4)):
            rows = slice(j * SPAN, (j + 1) * SPAN)
            stacked[rows, : n * wide] = jnp.zeros((SPAN, n * wide), jnp.bfloat16)
            stacked[rows, n * wide :] = traces[:, : width - n * wide]
        stacked[3 * SPAN :, : 2 * wide] = jnp.zeros((SPAN, 2 * wide), jnp.bfloat16)
        states = jnp.dot(
            weights_ref[...],
            stacked[: 2 * SPAN, : width - 2 * wide],
            preferred_element_type=jnp.float32,
        )
        stacked[3 * SPAN :, 2 * wide :] = states.astype(jnp.bfloat16)

    table = table_ref[...].reshape(QSTEP * SPAN, 4 * SPAN)
    early = jnp.dot(
        table[:, : 2 * SPAN],
        stacked[: 2 * SPAN, : 2 * wide],
        preferred_element_type=jnp.float32,
    )
    both = jnp.abs(early)
    for n in range(2, spans, 2):
        late = jnp.dot(
            table, stacked[:, n * wide : (n + 2) * wide], preferred_element_type=jnp.float32
        )
        both = jnp.maximum(both, jnp.abs(late))
    for n in range(QSTEP):
        highest = jnp.max(both[n * SPAN : (n + 1) * SPAN], axis=0, keepdims=True)
        highest = jnp.maximum(highest[:, :wide], highest[:, wide:])
        q = step * QSTEP + n
        out_ref[place_ref[q], pl.ds(place_ref[NPER + q], 1), :] = highest


def motion(place, table, weights, total):
    return pl.pallas_call(
        motion_kernel,
        out_shape=jax.ShapeDtypeStruct((OWNERS, PMAX, 2 * V), jnp.float32),
        grid_spec=pltpu.PrefetchScalarGridSpec(
            num_scalar_prefetch=1,
            grid=(NPER // QSTEP,),
            in_specs=[
                pl.BlockSpec((QSTEP, SPAN, 4 * SPAN), lambda s, place: (s, 0, 0)),
                pl.BlockSpec((SPAN, 2 * SPAN), lambda s, place: (0, 0)),
                pl.BlockSpec((2 * BLOCK, PHASES * V), lambda s, place: (0, 0)),
            ],
            out_specs=pl.BlockSpec((OWNERS, PMAX, 2 * V), lambda s, place: (0, 0, 0)),
            scratch_shapes=[
                pltpu.VMEM((SPAN, NT // SPAN * 2 * V), jnp.bfloat16),
                pltpu.VMEM((4 * SPAN, NT // SPAN * 2 * V), jnp.bfloat16),
            ],
        ),
        compiler_params=pltpu.CompilerParams(vmem_limit_bytes=SMALL),
        name="motion",
    )(place, table, weights, total)


def send(block, n):
    pairs = [(g, target(g, *STEPS[n])) for g in range(SLOTS)]
    return lax.ppermute(block, "sgt", pairs)


def local(
    sgt_tensor, moment, slip_rate, footprint, live_blocks, start_delay, frequency, period_owner
):
    here = lax.axis_index("sgt")
    rupture = here * OWNERS + lax.axis_index("work")
    outgoing = project(STEPS, footprint, sgt_tensor, moment)
    tensors = [outgoing[0]]
    for n in range(1, SLOTS - 1):
        tensors.append(send(outgoing[n], n))
    slip_rate, frequency, tensors[1] = lax.optimization_barrier(
        (slip_rate, frequency, tensors[1])
    )
    own_blocks = lax.dynamic_index_in_dim(footprint, rupture, 0, keepdims=False)
    own_count = lax.dynamic_index_in_dim(live_blocks, rupture, 0, keepdims=False)
    own_delays = lax.dynamic_index_in_dim(start_delay, rupture, 0, keepdims=False)
    origins = jnp.stack([origin(here, dz, dc) for dz, dc in STEPS])
    match = (own_blocks >> 2)[None, :] == origins[:, None]
    slot = jnp.sum(jnp.where(match, jnp.arange(SLOTS)[None, :], 0), axis=1)
    delay = jnp.sum(jnp.where(match, own_delays[None, :], 0), axis=1)
    info = jnp.concatenate([slot, jnp.where(slot < own_count, delay, 4 * NT)])

    slips = jnp.transpose(slip_rate[0], (0, 3, 1, 2)).reshape(SLOTS, L * V, PB)
    table, weights = tables(frequency)
    period_ids = jnp.arange(NPER)
    same_owner = period_owner[:, None] == period_owner[None, :]
    earlier = period_ids[None, :] < period_ids[:, None]
    rank = jnp.sum(same_owner & earlier, axis=1).astype(jnp.int32)
    place = jnp.concatenate([period_owner, rank])

    running = None
    for n, arrivals in enumerate(GROUPS):
        running = convolve(arrivals, info, [tensors[n] for n in arrivals], slips, running)
        if n == 0:
            last, running = lax.optimization_barrier((outgoing[SLOTS - 1], running))
            tensors.append(send(last, SLOTS - 1))
    peaks = motion(place, table, weights, running)
    peaks = lax.all_to_all(peaks, "work", split_axis=0, concat_axis=0, tiled=True)
    result = jnp.transpose(peaks.reshape(OWNERS, PMAX, 2, V), (1, 2, 0, 3))
    return result[None]


def solution(mesh):
    in_specs = (
        P("sgt", None, None, None, None),
        P("sgt", None, None),
        P(("sgt", "work"), None, None, None, None),
        P(),
        P(),
        P(),
        P(),
        P(),
    )
    out_specs = P("work", None, None, "sgt", None)
    return jax.shard_map(local, mesh=mesh, in_specs=in_specs, out_specs=out_specs, check_vma=False)
```

time: 567 us -> 87.7 us (0.15)
  local copies, waits for them, and re-layouts: 243 us -> 8.53 us
  waiting for transfers between devices: 133 us -> 10.3 us
  matrix products: 118 us -> 0 us
  Pallas kernels: 0 us -> 37 us
  loops' own time: 33.1 us -> 0 us
  blocking collectives: 0 us -> 14.4 us
  between operations: 13.5 us -> 0.27 us
  other arithmetic: 16.9 us -> 6.02 us
    reshape x9 -> x3, local copies, waits for them, and re-layouts: 119 us -> 0.21 us  [the longest x1 0.09 us: tables(): v[..., :3 * SPAN].reshape(steps, 2 * TSTEP, 3 * SPAN)]
    dot_general x8 -> x0, matrix products: 118 us -> none  [the longest x7 60.8 us: convolve(): jnp.einsum('viq,ciqt->vct', slip_window[:, :, ::-1], windows, preferred_e...]
    all_gather x1 -> x0, waiting for transfers between devices: 90.3 us -> none  [local(): portion = lax.all_gather(traces[None], 'work', axis=0, tiled=True)]
    concatenate x14 -> x0, local copies, waits for them, and re-layouts: 58.4 us -> none  [the longest x7 47 us: hankel(): jnp.concatenate([flattened, jnp.zeros(leading + (width,), shifted.dtype)]...]
    all_to_all x1 -> x0, waiting for transfers between devices: 43.1 us -> none  [local(): lax.all_to_all(outgoing, 'sgt', split_axis=0, concat_axis=0, tiled=True)]
    pallas_call x0 -> x8, Pallas kernels: none -> 37 us  [the longest x5 19.6 us: convolve(): pl.pallas_call(functools.partial(convolve_kernel, arrivals, begins), out_...]
    another operation x1 -> x0, loops' own time: 33.1 us -> none  [local(): lax.fori_loop(0, own_count, add_slot, jnp.zeros((V, NCOMP, NT), jnp.float...]
    dynamic_slice x35 -> x0, local copies, waits for them, and re-layouts: 19.2 us -> none  [the longest x14 9.46 us: add_slot(): lax.dynamic_index_in_dim(incoming, owner_index, 0, keepdims=False)]
  transfers between devices with their start and end apart: 2 -> 7, of which waited for: 2 -> 4; matrix products, arithmetic and copies ran while one was open for 2% -> 12% of each run, Pallas kernels for 0% -> 24%
where the time goes in v2:
time: 87.7 us; the launch traced here: 87.2 us
  Pallas kernels  37 us (42%)
  blocking collectives  14.4 us (16%)
  starting transfers between devices  10.7 us (12%)
  waiting for transfers between devices  10.3 us (12%)
  local copies, waits for them, and re-layouts  8.53 us (10%)
  other arithmetic  6.02 us (7%)
    pallas_call x5, Pallas kernels, convolve(): pl.pallas_call(functools.partial(convolve_kernel, arrivals, begins), out_...  19.6 us
    all_to_all x1, blocking collectives, local(): lax.all_to_all(peaks, 'work', split_axis=0, concat_axis=0, tiled=True)  14.4 us
    ppermute x7, starting transfers between devices, send(): return lax.ppermute(block, 'sgt', pairs)  10.7 us
    ppermute x7, waiting for transfers between devices, send(): return lax.ppermute(block, 'sgt', pairs)  10.3 us
    pallas_call x1, Pallas kernels, motion(): pl.pallas_call(motion_kernel, out_shape=jax.ShapeDtypeStruct((OWNERS, PMA...  7.02 us
    pallas_call x1, Pallas kernels, project(): pl.pallas_call(functools.partial(project_kernel, steps), out_shape=[jax.S...  6.5 us
    pallas_call x1, Pallas kernels, tables(): pl.pallas_call(tables_kernel, out_shape=jax.ShapeDtypeStruct((NPER, SPAN,...  3.88 us
    transpose x1, local copies, waits for them, and re-layouts, local(): slips = jnp.transpose(slip_rate[0], (0, 3, 1, 2)).reshape(SLOTS, L * V, PB)  3.81 us
  transfers between devices with their start and end apart: 7, of which 4 were waited for; matrix products, arithmetic and copies ran while one was open for 12% of the time, Pallas kernels for 24%

profile of v2, /device:TPU:0, one launch (start us, length us, event | category | flops | bytes accessed | tf_op | source)
XLA Modules:
  0.0 87.2 jit_solution(17927891819258770000)
XLA Ops:
  0.0 0.0 copy-start
  0.0 0.0 copy-start.3
  0.0 0.7 copy-done.3
  0.7 0.7 copy-done.5
  1.4 0.0 copy-start.4
  1.4 0.0 copy-start.11
  1.4 0.0 copy-start.12
  1.4 6.5 %project.1 = (bf16[256,1024]{1,0:T(8,128)(2,1)S(1)}, bf16[256,1024]{1,0:T(8,128)(2,1)}, bf16[256,1024]{1,0:T(8,128)(2,1)}, bf16[256,1024]{1,0:T(8,128)(2,1)}, bf...) custom-call(s32[8,128]{1,0:T(8,128)S(1)} %bitcast.27, ...), custom_call_target="tpu_custom_call" | custom-call | flops 400000000 | bytes 12800000 | tf_op jit(solution)/shard_map/project/pallas_call | solution.py:103
  7.9 0.0 copy-start.6
  7.9 0.8 copy-done.6
  8.7 0.0 collective-permute-start
  8.7 3.9 %collective-permute-start.5 = (bf16[256,1024]{1,0:T(8,128)(2,1)}, bf16[256,1024]{1,0:T(8,128)(2,1)}, u32[]{:S(2)}, u32[]{:S(2)}) collective-permute-start(bf16[256,1024]{1,0:T(8,128)(2,1)} %get-tuple-element.28), channel_id=1, source_target_pairs={{0,64},{16,80},{32,96},{48,112},{64,0},{80,16},{96,32},{112,48},{1... | collective-permute-start | bytes 1572872 | tf_op jit(solution)/shard_map/ppermute | solution.py:359
  12.6 0.1 collective-permute-start.6
  12.8 1.3 %collective-permute-start.3 = (bf16[256,1024]{1,0:T(8,128)(2,1)S(1)}, bf16[256,1024]{1,0:T(8,128)(2,1)S(1)}, u32[]{:S(2)}, u32[]{:S(2)}) collective-permute-start(bf16[256,1024]{1,0:T(8,128)(2,1)S(1)} %get-tuple-element.26), channel_id=1, source_target_pairs={{0,32},{16,48},{32,64},{48,80},{64,96},{80,112},{96,0},{112,16},{1... | collective-permute-start | bytes 1572872 | tf_op jit(solution)/shard_map/ppermute | solution.py:359
  14.1 2.1 %collective-permute-start.4 = (bf16[256,1024]{1,0:T(8,128)(2,1)S(1)}, bf16[256,1024]{1,0:T(8,128)(2,1)S(1)}, u32[]{:S(2)}, u32[]{:S(2)}) collective-permute-start(bf16[256,1024]{1,0:T(8,128)(2,1)S(1)} %get-tuple-element.27), channel_id=1, source_target_pairs={{0,96},{16,112},{32,0},{48,16},{64,32},{80,48},{96,64},{112,80},{1... | collective-permute-start | bytes 1572872 | tf_op jit(solution)/shard_map/ppermute | solution.py:359
  16.2 0.0 copy-done.4
  16.2 0.2 shift-right-arithmetic_reduce_fusion
  16.4 0.0 copy-done
  16.4 0.2 dynamic-slice_reduce_fusion
  16.6 0.0 copy-done.11
  16.6 0.6 dynamic_slice.12
  17.2 0.1 stack.47
  17.2 0.2 fusion.5
  17.4 0.6 compare_select_fusion.7
  18.0 0.1 pad_add_fusion.1.info_ref
  18.1 0.0 copy-done.12
  18.1 0.2 convert_reduce_fusion
  18.2 0.1 pad_add_fusion.place_ref
  18.3 0.0 collective-permute-done.rest_1_
  18.3 0.1 collective-permute-start.2
  18.4 3.8 %copy.15 = bf16[8,32,64,128]{3,2,1,0:T(8,128)(2,1)S(1)} copy(bf16[8,32,64,128]{3,1,2,0:T(8,128)(2,1)} %bitcast.29) | data formatting | bytes 8388608 | tf_op jit(solution)/shard_map/transpose | solution.py:383
  22.2 0.0 copy-start.1
  22.3 0.0 copy-done.7
  22.3 0.0 copy-start.10
  22.3 5.0 %convolve.5.rest_3_ = f32[512,256]{1,0:T(8,128)S(1)} custom-call(s32[16]{0:T(128)S(1)} %pad_add_fusion.1.info_ref, bf16[256,1024]{1,0:T(8,128)(2,1)S(1)} %copy-done.7, bf16[256,1024]{1,0:T(8,128)(2,1)} %collective-permute-done.rest_1_, bf16[8,2048,128]{2,1,0:T(8,128)(2,1)S(1)} %bitcast.21), custom_call_target="tpu_custom_call" | custom-call | flops 3600000000 | bytes 2097152 | tf_op jit(solution)/shard_map/convolve/pallas_call | solution.py:261
  27.3 0.0 copy-done.10
  27.3 3.7 %fusion.2 = (f32[44,1,640]{2,1,0:T(1,128)S(1)}, f32[44,1,640]{2,1,0:T(1,128)S(1)}) fusion(f32[640]{0:T(1024)S(1)} %subtract_convert_fusion, f32[44]{0:T(128)S(1)} %get-tuple-element.39, f32[44]{0:T(128)S(1)} %get-tuple-element.38, f32[44]{0:T(128)S(1)} %get-tuple-element.37), kind=kLoop, calls=%fused_computation.6 | loop fusion | flops 168960 | bytes 228368 | tf_op jit(solution)/shard_map/mul | solution.py:165
  31.1 0.1 fusion
  31.2 0.7 sine_multiply_fusion
  31.9 0.0 collective-permute-done.5.rest_0_
  31.9 3.2 %collective-permute-start.1 = (bf16[256,1024]{1,0:T(8,128)(2,1)S(1)}, bf16[256,1024]{1,0:T(8,128)(2,1)}, u32[]{:S(2)}, u32[]{:S(2)}) collective-permute-start(bf16[256,1024]{1,0:T(8,128)(2,1)S(1)} %get-tuple-element.24), channel_id=1, source_target_pairs={{0,112},{16,96},{32,16},{48,0},{64,48},{80,32},{96,80},{112,64},{1... | collective-permute-start | bytes 1572872 | tf_op jit(solution)/shard_map/ppermute | solution.py:359
  35.1 1.6 %collective-permute-done.6.rest_1_ = bf16[256,1024]{1,0:T(8,128)(2,1)} collective-permute-done((bf16[256,1024]{1,0:T(8,128)(2,1)}, bf16[256,1024]{1,0:T(8,128)(2,1)}, u32[]{:S(2)}, u32[]{:S(2)}) %collective-permute-start.6) | collective-permute-done | bytes 524320 | tf_op jit(solution)/shard_map/ppermute | solution.py:359
  36.7 0.0 copy-done.1
  36.7 4.7 %convolve.6.rest_3_ = f32[512,256]{1,0:T(8,128)S(1)} custom-call(s32[16]{0:T(128)S(1)} %pad_add_fusion.1.info_ref, bf16[256,1024]{1,0:T(8,128)(2,1)} %collective-permute-done.5.rest_0_, bf16[256,1024]{1,0:T(8,128)(2,1)} %collective-permute-done.6.rest_1_, bf16[8,2048,128]{2,1,0:T(8,128)(2,1)S(1)} %bitcast.22, f32[512,256]{1,0:T(8,128)S(1)} %convolve.5.rest_3_), custom_call_target="tpu_custom_call" | custom-call | flops 3600000000 | bytes 2097152 | tf_op jit(solution)/shard_map/convolve/pallas_call | solution.py:261
  41.4 0.0 copy-start.8
  41.4 0.8 copy-done.8
  42.2 0.1 fusion.3
  42.4 0.1 reshape.392.v_ref
  42.5 0.0 copy-start.2
  42.5 0.0 copy-start.9
  42.5 3.9 %tables.1.table_ref = bf16[44,128,512]{2,1,0:T(8,128)(2,1)S(1)} custom-call(f32[11,8,128]{2,1,0:T(8,128)S(1)} %bitcast.26, f32[11,8,384]{2,1,0:T(8,128)S(1)} %reshape.392.v_ref), custom_call_target="tpu_custom_call" | custom-call | flops 14417920 | bytes 6000000 | tf_op jit(solution)/shard_map/tables/pallas_call | solution.py:169
  46.4 1.5 %collective-permute-done.3.rest_0_ = bf16[256,1024]{1,0:T(8,128)(2,1)S(1)} collective-permute-done((bf16[256,1024]{1,0:T(8,128)(2,1)S(1)}, bf16[256,1024]{1,0:T(8,128)(2,1)S(1)}, u32[]{:S(2)}, u32[]{:S(2)}) %collective-permute-start.3) | collective-permute-done | bytes 524320 | tf_op jit(solution)/shard_map/ppermute | solution.py:359
  48.0 1.1 %collective-permute-done.4.rest_1_ = bf16[256,1024]{1,0:T(8,128)(2,1)S(1)} collective-permute-done((bf16[256,1024]{1,0:T(8,128)(2,1)S(1)}, bf16[256,1024]{1,0:T(8,128)(2,1)S(1)}, u32[]{:S(2)}, u32[]{:S(2)}) %collective-permute-start.4) | collective-permute-done | bytes 524320 | tf_op jit(solution)/shard_map/ppermute | solution.py:359
  49.1 0.0 copy-done.2
  49.1 0.0 copy-done.9
  49.1 4.0 %convolve.7.rest_2_ = f32[512,256]{1,0:T(8,128)S(1)} custom-call(s32[16]{0:T(128)S(1)} %pad_add_fusion.1.info_ref, bf16[256,1024]{1,0:T(8,128)(2,1)S(1)} %collective-permute-done.3.rest_0_, bf16[256,1024]{1,0:T(8,128)(2,1)S(1)} %collective-permute-done.4.rest_1_, bf16[8,2048,128]{2,1,0:T(8,128)(2,1)S(1)} %bitcast.23, f32[512,256]{1,0:T(8,128)S(1)} %copy-done.9), custom_call_target="tpu_custom_call" | custom-call | flops 3600000000 | bytes 2097152 | tf_op jit(solution)/shard_map/convolve/pallas_call | solution.py:261
  53.1 6.1 %collective-permute-done.2.rest_0_ = bf16[256,1024]{1,0:T(8,128)(2,1)} collective-permute-done((bf16[256,1024]{1,0:T(8,128)(2,1)S(1)}, bf16[256,1024]{1,0:T(8,128)(2,1)}, u32[]{:S(2)}, u32[]{:S(2)}) %collective-permute-start.2) | collective-permute-done | bytes 524320 | tf_op jit(solution)/shard_map/ppermute | solution.py:359
  59.2 2.9 %convolve.8.rest_2_ = f32[512,256]{1,0:T(8,128)S(1)} custom-call(s32[16]{0:T(128)S(1)} %pad_add_fusion.1.info_ref, bf16[256,1024]{1,0:T(8,128)(2,1)} %collective-permute-done.2.rest_0_, bf16[8,2048,128]{2,1,0:T(8,128)(2,1)S(1)} %bitcast.24, f32[512,256]{1,0:T(8,128)S(1)} %convolve.7.rest_2_), custom_call_target="tpu_custom_call" | custom-call | flops 1800000000 | bytes 1048576 | tf_op jit(solution)/shard_map/convolve/pallas_call | solution.py:261
  62.1 0.0 collective-permute-done.1.rest_0_
  62.1 2.9 %convolve.9.total = f32[512,256]{1,0:T(8,128)S(1)} custom-call(s32[16]{0:T(128)S(1)} %pad_add_fusion.1.info_ref, bf16[256,1024]{1,0:T(8,128)(2,1)} %collective-permute-done.1.rest_0_, bf16[8,2048,128]{2,1,0:T(8,128)(2,1)S(1)} %bitcast.25, f32[512,256]{1,0:T(8,128)S(1)} %convolve.8.rest_2_), custom_call_target="tpu_custom_call" | custom-call | flops 1800000000 | bytes 1048576 | tf_op jit(solution)/shard_map/convolve/pallas_call | solution.py:261
  65.1 7.0 %motion.1 = f32[16,3,128]{2,1,0:T(4,128)S(1)} custom-call(s32[88]{0:T(128)S(1)} %pad_add_fusion.place_ref, bf16[44,128,512]{2,1,0:T(8,128)(2,1)S(1)} %tables.1.table_ref, bf16[128,256]{1,0:T(8,128)(2,1)S(1)} %pad.5.weights_ref, f32[512,256]{1,0:T(8,128)S(1)} %convolve.9.total), custom_call_target="tpu_custom_call" | custom-call | tf_op jit(solution)/shard_map/motion/pallas_call | solution.py:335
  72.1 14.4 %all_to_all.5 = f32[16,3,128]{2,1,0:T(4,128)S(1)} all-to-all(f32[16,3,128]{2,1,0:T(4,128)S(1)} %motion.1), channel_id=1, replica_groups=mesh['sgt'=8,'work'=16] {'work'}, dimensions={0} | all-to-all | bytes 49152 | tf_op jit(solution)/shard_map/all_to_all | solution.py:398
  86.5 0.1 reshape.395
  86.6 0.6 copy.17
  (9 shorter events, 0.1 us)
Async XLA Ops:
  0.0 16.4 %copy-start = (s32[128,8]{0,1:T(8,128)S(1)}, s32[128,8]{0,1:T(8,128)}, u32[]{:S(2)}) copy-start(s32[128,8]{0,1:T(8,128)} %param.14) | copy-start | bytes 12292
  0.0 0.7 copy-start.3
  0.7 0.7 copy-start.5
  1.4 14.8 %copy-start.4 = (s32[128,8]{0,1:T(8,128)S(1)}, s32[128,8]{0,1:T(8,128)}, u32[]{:S(2)}) copy-start(s32[128,8]{0,1:T(8,128)} %param.12) | copy-start | bytes 12292
  1.4 15.2 %copy-start.11 = (s32[128]{0:T(128)S(1)}, s32[128]{0:T(128)}, u32[]{:S(2)}) copy-start(s32[128]{0:T(128)} %param.13) | copy-start | bytes 1540
  1.4 16.7 %copy-start.12 = (s32[44]{0:T(128)S(1)}, s32[44]{0:T(128)}, u32[]{:S(2)}) copy-start(s32[44]{0:T(128)} %param.16) | copy-start | bytes 532
  7.9 0.8 copy-start.6
  8.7 9.6 %collective-permute-start = (bf16[256,1024]{1,0:T(8,128)(2,1)}, bf16[256,1024]{1,0:T(8,128)(2,1)}, u32[]{:S(2)}, u32[]{:S(2)}) collective-permute-start(bf16[256,1024]{1,0:T(8,128)(2,1)} %get-tuple-element.18), channel_id=1, source_target_pairs={{0,16},{16,0},{32,48},{48,32},{64,80},{80,64},{96,112},{112,96},{1... | collective-permute-start | bytes 1572872 | tf_op jit(solution)/shard_map/ppermute | solution.py:359
  8.7 23.2 %collective-permute-start.5 = (bf16[256,1024]{1,0:T(8,128)(2,1)}, bf16[256,1024]{1,0:T(8,128)(2,1)}, u32[]{:S(2)}, u32[]{:S(2)}) collective-permute-start(bf16[256,1024]{1,0:T(8,128)(2,1)} %get-tuple-element.28), channel_id=1, source_target_pairs={{0,64},{16,80},{32,96},{48,112},{64,0},{80,16},{96,32},{112,48},{1... | collective-permute-start | bytes 1572872 | tf_op jit(solution)/shard_map/ppermute | solution.py:359
  12.6 24.1 %collective-permute-start.6 = (bf16[256,1024]{1,0:T(8,128)(2,1)}, bf16[256,1024]{1,0:T(8,128)(2,1)}, u32[]{:S(2)}, u32[]{:S(2)}) collective-permute-start(bf16[256,1024]{1,0:T(8,128)(2,1)} %get-tuple-element.29), channel_id=1, source_target_pairs={{0,80},{16,64},{32,112},{48,96},{64,16},{80,0},{96,48},{112,32},{1... | collective-permute-start | bytes 1572872 | tf_op jit(solution)/shard_map/ppermute | solution.py:359
  12.8 35.2 %collective-permute-start.3 = (bf16[256,1024]{1,0:T(8,128)(2,1)S(1)}, bf16[256,1024]{1,0:T(8,128)(2,1)S(1)}, u32[]{:S(2)}, u32[]{:S(2)}) collective-permute-start(bf16[256,1024]{1,0:T(8,128)(2,1)S(1)} %get-tuple-element.26), channel_id=1, source_target_pairs={{0,32},{16,48},{32,64},{48,80},{64,96},{80,112},{96,0},{112,16},{1... | collective-permute-start | bytes 1572872 | tf_op jit(solution)/shard_map/ppermute | solution.py:359
  14.1 35.0 %collective-permute-start.4 = (bf16[256,1024]{1,0:T(8,128)(2,1)S(1)}, bf16[256,1024]{1,0:T(8,128)(2,1)S(1)}, u32[]{:S(2)}, u32[]{:S(2)}) collective-permute-start(bf16[256,1024]{1,0:T(8,128)(2,1)S(1)} %get-tuple-element.27), channel_id=1, source_target_pairs={{0,96},{16,112},{32,0},{48,16},{64,32},{80,48},{96,64},{112,80},{1... | collective-permute-start | bytes 1572872 | tf_op jit(solution)/shard_map/ppermute | solution.py:359
  17.2 5.0 %copy-start.7 = (bf16[256,1024]{1,0:T(8,128)(2,1)S(1)}, bf16[256,1024]{1,0:T(8,128)(2,1)}, u32[]{:S(2)}) copy-start(bf16[256,1024]{1,0:T(8,128)(2,1)} %copy-done.6) | copy-start | bytes 1572868
  18.3 40.9 %collective-permute-start.2 = (bf16[256,1024]{1,0:T(8,128)(2,1)S(1)}, bf16[256,1024]{1,0:T(8,128)(2,1)}, u32[]{:S(2)}, u32[]{:S(2)}) collective-permute-start(bf16[256,1024]{1,0:T(8,128)(2,1)S(1)} %get-tuple-element.25), channel_id=1, source_target_pairs={{0,48},{16,32},{32,80},{48,64},{64,112},{80,96},{96,16},{112,0},{1... | collective-permute-start | bytes 1572872 | tf_op jit(solution)/shard_map/ppermute | solution.py:359
  22.2 14.5 %copy-start.1 = (bf16[8,32,64,128]{3,2,1,0:T(8,128)(2,1)}, bf16[8,32,64,128]{3,2,1,0:T(8,128)(2,1)S(1)}, u32[]{:S(2)}) copy-start(bf16[8,32,64,128]{3,2,1,0:T(8,128)(2,1)S(1)} %copy.15) | copy-start | bytes 12582916
  22.3 5.0 %copy-start.10 = (f32[44]{0:T(128)S(1)}, f32[44]{0:T(128)}, u32[]{:S(2)}) copy-start(f32[44]{0:T(128)} %param.15) | copy-start | bytes 532
  31.9 30.2 %collective-permute-start.1 = (bf16[256,1024]{1,0:T(8,128)(2,1)S(1)}, bf16[256,1024]{1,0:T(8,128)(2,1)}, u32[]{:S(2)}, u32[]{:S(2)}) collective-permute-start(bf16[256,1024]{1,0:T(8,128)(2,1)S(1)} %get-tuple-element.24), channel_id=1, source_target_pairs={{0,112},{16,96},{32,16},{48,0},{64,48},{80,32},{96,80},{112,64},{1... | collective-permute-start | bytes 1572872 | tf_op jit(solution)/shard_map/ppermute | solution.py:359
  41.4 0.8 copy-start.8
  42.5 6.6 %copy-start.2 = (bf16[8,32,64,128]{3,2,1,0:T(8,128)(2,1)S(1)}, bf16[8,32,64,128]{3,2,1,0:T(8,128)(2,1)}, u32[]{:S(2)}) copy-start(bf16[8,32,64,128]{3,2,1,0:T(8,128)(2,1)} %copy-done.1) | copy-start | bytes 12582916
  42.5 6.6 %copy-start.9 = (f32[512,256]{1,0:T(8,128)S(1)}, f32[512,256]{1,0:T(8,128)}, u32[]{:S(2)}) copy-start(f32[512,256]{1,0:T(8,128)} %copy-done.8) | copy-start | bytes 1572868

commit v3 on v2

--- a/solution.py
+++ b/solution.py
@@ -25,15 +25,16 @@
 TAPS = 9
 PADROWS = 16
 BLOCK = 256
+HALF = NT // 2
 SPAN = 128
 TSTEP = 4
 QSTEP = 11
 SMALL = 12 * 1024 * 1024
 LARGE = 28 * 1024 * 1024
-PROJECT = 48 * 1024 * 1024
+PROJECT = 60 * 1024 * 1024
 
 STEPS = ((0, 0), (0, 1), (2, 0), (2, 1), (1, 0), (3, 0), (1, 1), (3, 1))
-GROUPS = ((0, 1), (2, 3), (4, 5), (6,), (7,))
+GROUPS = ((0, 1), (2, 3), (4, 5))
 
 
 def target(place, dz, dc):
@@ -53,9 +54,20 @@
         scr[c * PB + i : c * PB + i + 16, :] = total.astype(jnp.bfloat16)
 
 
+def pieces(steps):
+    parts = []
+    for n in range(len(steps)):
+        if n < len(steps) - 2:
+            parts.append((n, slice(0, NT)))
+        else:
+            parts += [(n, slice(0, HALF)), (n, slice(HALF, NT))]
+    return parts
+
+
 def project_kernel(steps, fp_ref, sgt_ref, mom_ref, *rest):
-    count = len(steps)
-    outs, taken, scr, table, moments, in_sem, out_sem, small_sem = rest[:count], *rest[count:]
+    parts = pieces(steps)
+    outs, rest = rest[: len(parts)], rest[len(parts) :]
+    taken, scr, table, moments, in_sem, out_sem, small_sem = rest
     fetch_table = pltpu.make_async_copy(fp_ref, table, small_sem.at[0])
     fetch_moments = pltpu.make_async_copy(mom_ref, moments, small_sem.at[1])
     fetch_table.start()
@@ -90,32 +102,34 @@
         for c in range(2):
             load(n, c).wait()
             project_block(weights, taken.at[n], scr.at[n], c)
-        for m in range(count):
-            copy = pltpu.make_async_copy(scr.at[n], outs[m], out_sem.at[m])
-            pl.when(chosen[m] == n)(copy.start)
-
-    for m in range(count):
-        pltpu.make_async_copy(scr.at[0], outs[m], out_sem.at[m]).wait()
+        for m, (step, span) in enumerate(parts):
+            copy = pltpu.make_async_copy(scr.at[n, :, span], outs[m], out_sem.at[m])
+            pl.when(chosen[step] == n)(copy.start)
+
+    for m, (step, span) in enumerate(parts):
+        pltpu.make_async_copy(scr.at[0, :, span], outs[m], out_sem.at[m]).wait()
 
 
 def project(steps, footprint, sgt_tensor, moment):
-    count = len(steps)
+    parts = pieces(steps)
     return pl.pallas_call(
         functools.partial(project_kernel, steps),
-        out_shape=[jax.ShapeDtypeStruct((2 * PB, NT), jnp.bfloat16)] * count,
+        out_shape=[
+            jax.ShapeDtypeStruct((2 * PB, span.stop - span.start), jnp.bfloat16) for _, span in parts
+        ],
         in_specs=[
             pl.BlockSpec(memory_space=pl.ANY),
             pl.BlockSpec(memory_space=pl.ANY),
             pl.BlockSpec(memory_space=pl.ANY),
         ],
-        out_specs=[pl.BlockSpec(memory_space=pltpu.VMEM)] * count,
+        out_specs=[pl.BlockSpec(memory_space=pl.ANY)] * len(parts),
         scratch_shapes=[
             pltpu.VMEM((HELD, NJ, 2, PB, NT), jnp.bfloat16),
             pltpu.VMEM((HELD, 2 * PB, NT), jnp.bfloat16),
             pltpu.SMEM((SLOTS, 128), jnp.int32),
             pltpu.VMEM((NJ, HELD, PB), jnp.float32),
             pltpu.SemaphoreType.DMA((2 * HELD,)),
-            pltpu.SemaphoreType.DMA((count,)),
+            pltpu.SemaphoreType.DMA((len(parts),)),
             pltpu.SemaphoreType.DMA((2,)),
         ],
         compiler_params=pltpu.CompilerParams(vmem_limit_bytes=PROJECT),
@@ -276,82 +290,166 @@
     )(info, *tensors, slips, *([] if begins else [before]))
 
 
-def motion_kernel(place_ref, table_ref, weights_ref, total, out_ref, traces, stacked):
-    step = pl.program_id(0)
-    spans = NT // SPAN
+def pick_phases(delay):
+    rows = lax.broadcasted_iota(jnp.int32, (BLOCK, 2 * BLOCK), 0)
+    lane = lax.broadcasted_iota(jnp.int32, (BLOCK, 2 * BLOCK), 1)
+    source = BLOCK + ((rows & 63) << 2) + (rows >> 6) - delay
+    return jnp.where(lane == source, 1.0, 0.0).astype(jnp.bfloat16)
+
+
+def gather_some(delay, blocks, chunks, phases):
+    pick = pick_phases(delay)
+    part = BLOCK // PHASES
+    dims = (((1,), (1,)), ((), ()))
+    for place, a in enumerate(chunks):
+        moved = lax.dot_general(
+            pick[:, BLOCK:], blocks[a], dims, preferred_element_type=jnp.float32
+        )
+        if a > 0:
+            moved += lax.dot_general(
+                pick[:, :BLOCK], blocks[a - 1], dims, preferred_element_type=jnp.float32
+            )
+        low = PADROWS + place * part
+        for c in range(2):
+            for b in range(PHASES):
+                phases[c, low : low + part, b * PB : (b + 1) * PB] = moved[
+                    b * part : (b + 1) * part, c * PB : (c + 1) * PB
+                ]
+
+
+def finish_kernel(late, info_ref, place_ref, *rest):
+    count = 4 if late else 2
+    tensors, rest = rest[:count], rest[count:]
+    slips, before, table_ref, weights_ref = rest[:4]
+    rest = rest[4:]
+    known, peaks = None, None
+    if late:
+        known, peaks = rest[:2]
+        rest = rest[2:]
+    out_ref, traces = rest[0], rest[1]
+    phases, total, stacked = rest[2:]
+    rows = BLOCK // 2
     wide = 2 * V
+    first_row = PADROWS + (64 if late else 0)
+    if not late:
+        phases[:, :, :PADROWS, :] = jnp.zeros((2, 2, PADROWS, PHASES * PB), jnp.float32)
+    for n in range(2):
+        arrival = SLOTS - 2 + n
+        slot = info_ref[arrival]
+        halves = tensors[2 * n : 2 * n + 2] if late else tensors[n : n + 1]
+        blocks = [half[:, i * BLOCK : (i + 1) * BLOCK] for half in halves for i in range(2)]
+        chunks = (1, 2, 3) if late else (0, 1)
+        gather_some(info_ref[SLOTS + arrival], blocks, chunks, phases.at[n])
+        term = None
+        for j in range(TAPS):
+            shifted = jnp.concatenate(
+                [phases[n, c, first_row - j : first_row - j + rows, :] for c in range(2)], axis=0
+            )
+            product = lax.dot_general(
+                shifted.astype(jnp.bfloat16),
+                histories(slips, slot, j),
+                (((1,), (1,)), ((), ())),
+                preferred_element_type=jnp.float32,
+            )
+            term = product if term is None else term + product
+        if n == 0:
+            for c in range(2):
+                low = c * BLOCK + (rows if late else 0)
+                total[c * rows : (c + 1) * rows, :] = (
+                    before[low : low + rows, :] + term[c * rows : (c + 1) * rows, :]
+                )
+        else:
+            total[...] += term
+
+    part = SPAN // PHASES
+    spans = rows // part
+    lane = lax.broadcasted_iota(jnp.int32, (part, wide), 1)
+    for a in range(spans):
+        for b in range(PHASES):
+            half = slice((b // 2) * wide, (b // 2 + 1) * wide)
+            first = total[a * part : (a + 1) * part, half]
+            second = total[rows + a * part : rows + (a + 1) * part, half]
+            if b % 2 == 0:
+                second = pltpu.roll(second, V, 1)
+            else:
+                first = pltpu.roll(first, V, 1)
+            traces[b * part : (b + 1) * part, a * wide : (a + 1) * wide] = jnp.where(
+                lane < V, first, second
+            ).astype(jnp.bfloat16)
+
     width = spans * wide
-
-    @pl.when(step == 0)
-    def _():
-        out_ref[...] = jnp.zeros_like(out_ref)
-        part = SPAN // PHASES
-        lane = lax.broadcasted_iota(jnp.int32, (part, wide), 1)
-        for a in range(spans):
-            for b in range(PHASES):
-                half = slice((b // 2) * wide, (b // 2 + 1) * wide)
-                first = total[a * part : (a + 1) * part, half]
-                second = total[BLOCK + a * part : BLOCK + (a + 1) * part, half]
-                if b % 2 == 0:
-                    second = pltpu.roll(second, V, 1)
-                else:
-                    first = pltpu.roll(first, V, 1)
-                traces[b * part : (b + 1) * part, a * wide : (a + 1) * wide] = jnp.where(
-                    lane < V, first, second
-                ).astype(jnp.bfloat16)
-        stacked[:SPAN, :] = traces[...]
-        for j, n in ((1, 1), (2, 4)):
-            rows = slice(j * SPAN, (j + 1) * SPAN)
-            stacked[rows, : n * wide] = jnp.zeros((SPAN, n * wide), jnp.bfloat16)
-            stacked[rows, n * wide :] = traces[:, : width - n * wide]
-        stacked[3 * SPAN :, : 2 * wide] = jnp.zeros((SPAN, 2 * wide), jnp.bfloat16)
-        states = jnp.dot(
-            weights_ref[...],
-            stacked[: 2 * SPAN, : width - 2 * wide],
-            preferred_element_type=jnp.float32,
-        )
-        stacked[3 * SPAN :, 2 * wide :] = states.astype(jnp.bfloat16)
-
-    table = table_ref[...].reshape(QSTEP * SPAN, 4 * SPAN)
-    early = jnp.dot(
-        table[:, : 2 * SPAN],
-        stacked[: 2 * SPAN, : 2 * wide],
+    nothing = jnp.zeros((SPAN, width), jnp.bfloat16)
+    stacked[:SPAN, :] = traces[...]
+    stacked[SPAN : 2 * SPAN, wide:] = traces[:, : width - wide]
+    if late:
+        stacked[SPAN : 2 * SPAN, :wide] = known[:, width - wide :]
+        stacked[2 * SPAN : 3 * SPAN, :] = known[...]
+        near = jnp.concatenate([known[:, 2 * wide :], traces[:, : 2 * wide]], axis=1)
+        far = jnp.concatenate([known[:, wide:], traces[:, :wide]], axis=1)
+        low = 0
+    else:
+        stacked[SPAN : 2 * SPAN, :wide] = nothing[:, :wide]
+        stacked[2 * SPAN : 3 * SPAN, :] = nothing
+        stacked[3 * SPAN :, : 2 * wide] = nothing[:, : 2 * wide]
+        near = traces[:, : 2 * wide]
+        far = jnp.concatenate([nothing[:, :wide], traces[:, :wide]], axis=1)
+        low = 2 * wide
+    states = jnp.dot(
+        weights_ref[...],
+        jnp.concatenate([near, far], axis=0),
         preferred_element_type=jnp.float32,
     )
-    both = jnp.abs(early)
-    for n in range(2, spans, 2):
-        late = jnp.dot(
-            table, stacked[:, n * wide : (n + 2) * wide], preferred_element_type=jnp.float32
+    stacked[3 * SPAN :, low:] = states.astype(jnp.bfloat16)
+    out_ref[...] = peaks[...] if late else jnp.zeros_like(out_ref)
+
+    @pl.loop(0, NPER // QSTEP)
+    def _(step):
+        table = table_ref[pl.ds(step * QSTEP, QSTEP)].reshape(QSTEP * SPAN, 4 * SPAN)
+        deep = 4 * SPAN if late else 2 * SPAN
+        one = jnp.dot(
+            table[:, :deep], stacked[:deep, : 2 * wide], preferred_element_type=jnp.float32
         )
-        both = jnp.maximum(both, jnp.abs(late))
-    for n in range(QSTEP):
-        highest = jnp.max(both[n * SPAN : (n + 1) * SPAN], axis=0, keepdims=True)
-        highest = jnp.maximum(highest[:, :wide], highest[:, wide:])
-        q = step * QSTEP + n
-        out_ref[place_ref[q], pl.ds(place_ref[NPER + q], 1), :] = highest
-
-
-def motion(place, table, weights, total):
+        two = jnp.dot(table, stacked[:, 2 * wide :], preferred_element_type=jnp.float32)
+        both = jnp.maximum(jnp.abs(one), jnp.abs(two))
+        for n in range(QSTEP):
+            highest = jnp.max(both[n * SPAN : (n + 1) * SPAN], axis=0, keepdims=True)
+            highest = jnp.maximum(highest[:, :wide], highest[:, wide:])
+            q = step * QSTEP + n
+            owner, rank = place_ref[q], place_ref[NPER + q]
+            if late:
+                highest = jnp.maximum(highest, peaks[owner, pl.ds(rank, 1), :])
+            out_ref[owner, pl.ds(rank, 1), :] = highest
+
+
+def finish(late, info, place, tensors, slips, before, table, weights, known):
+    smem = pl.BlockSpec(memory_space=pltpu.SMEM)
+    vmem = pl.BlockSpec(memory_space=pltpu.VMEM)
+    operands = [*tensors, slips, before, table, weights, *known]
+    out_shape = [jax.ShapeDtypeStruct((OWNERS, PMAX, 2 * V), jnp.float32)]
+    traces = (SPAN, HALF // SPAN * 2 * V)
+    scratch = []
+    if late:
+        scratch = [pltpu.VMEM(traces, jnp.bfloat16)]
+    else:
+        out_shape.append(jax.ShapeDtypeStruct(traces, jnp.bfloat16))
+    held = PADROWS + (192 if late else 128)
     return pl.pallas_call(
-        motion_kernel,
-        out_shape=jax.ShapeDtypeStruct((OWNERS, PMAX, 2 * V), jnp.float32),
-        grid_spec=pltpu.PrefetchScalarGridSpec(
-            num_scalar_prefetch=1,
-            grid=(NPER // QSTEP,),
-            in_specs=[
-                pl.BlockSpec((QSTEP, SPAN, 4 * SPAN), lambda s, place: (s, 0, 0)),
-                pl.BlockSpec((SPAN, 2 * SPAN), lambda s, place: (0, 0)),
-                pl.BlockSpec((2 * BLOCK, PHASES * V), lambda s, place: (0, 0)),
-            ],
-            out_specs=pl.BlockSpec((OWNERS, PMAX, 2 * V), lambda s, place: (0, 0, 0)),
-            scratch_shapes=[
-                pltpu.VMEM((SPAN, NT // SPAN * 2 * V), jnp.bfloat16),
-                pltpu.VMEM((4 * SPAN, NT // SPAN * 2 * V), jnp.bfloat16),
-            ],
+        functools.partial(finish_kernel, late),
+        out_shape=out_shape,
+        in_specs=[smem, smem] + [vmem] * len(operands),
+        out_specs=[vmem] * len(out_shape),
+        scratch_shapes=scratch
+        + [
+            pltpu.VMEM((2, 2, held, PHASES * PB), jnp.float32),
+            pltpu.VMEM((BLOCK, PHASES * V), jnp.float32),
+            pltpu.VMEM((4 * SPAN, HALF // SPAN * 2 * V), jnp.bfloat16),
+        ],
+        compiler_params=pltpu.CompilerParams(vmem_limit_bytes=LARGE),
+        cost_estimate=pl.CostEstimate(
+            flops=3600000000, bytes_accessed=8000000, transcendentals=0
         ),
-        compiler_params=pltpu.CompilerParams(vmem_limit_bytes=SMALL),
-        name="motion",
-    )(place, table, weights, total)
+        name="finish",
+    )(info, place, *operands)
 
 
 def send(block, n):
@@ -364,10 +462,19 @@
 ):
     here = lax.axis_index("sgt")
     rupture = here * OWNERS + lax.axis_index("work")
-    outgoing = project(STEPS, footprint, sgt_tensor, moment)
+    outgoing = list(project(STEPS, footprint, sgt_tensor, moment))
     tensors = [outgoing[0]]
-    for n in range(1, SLOTS - 1):
+    for n in range(1, SLOTS - 2):
         tensors.append(send(outgoing[n], n))
+    first, second = SLOTS - 2, SLOTS - 1
+    halves = {first: [], second: []}
+
+    def send_after(part, n, arrived):
+        block, tensors[arrived] = lax.optimization_barrier((outgoing[part], tensors[arrived]))
+        halves[n].append(send(block, n))
+
+    send_after(SLOTS - 2, first, 1)
+    send_after(SLOTS, second, 2)
     slip_rate, frequency, tensors[1] = lax.optimization_barrier(
         (slip_rate, frequency, tensors[1])
     )
@@ -391,10 +498,34 @@
     running = None
     for n, arrivals in enumerate(GROUPS):
         running = convolve(arrivals, info, [tensors[n] for n in arrivals], slips, running)
-        if n == 0:
-            last, running = lax.optimization_barrier((outgoing[SLOTS - 1], running))
-            tensors.append(send(last, SLOTS - 1))
-    peaks = motion(place, table, weights, running)
+        if n == 1:
+            outgoing[SLOTS - 1], outgoing[SLOTS + 1], running, table = lax.optimization_barrier(
+                (outgoing[SLOTS - 1], outgoing[SLOTS + 1], running, table)
+            )
+            send_after(SLOTS - 1, first, 4)
+            send_after(SLOTS + 1, second, 5)
+    peaks, known = finish(
+        False,
+        info,
+        place,
+        [halves[first][0], halves[second][0]],
+        slips,
+        running,
+        table,
+        weights,
+        [],
+    )
+    (peaks,) = finish(
+        True,
+        info,
+        place,
+        halves[first] + halves[second],
+        slips,
+        running,
+        table,
+        weights,
+        [known, peaks],
+    )
     peaks = lax.all_to_all(peaks, "work", split_axis=0, concat_axis=0, tiled=True)
     result = jnp.transpose(peaks.reshape(OWNERS, PMAX, 2, V), (1, 2, 0, 3))
     return result[None]

time: 87.7 us -> 84.9 us (0.968)
  waiting for transfers between devices: 10.3 us -> 7.03 us
  local copies, waits for them, and re-layouts: 8.53 us -> 5.68 us
  starting transfers between devices: 10.7 us -> 13.4 us
  Pallas kernels: 37 us -> 38.2 us
    pallas_call x1 -> x2, Pallas kernels: 7.02 us -> 14.5 us  [finish(): pl.pallas_call(functools.partial(finish_kernel, late), out_shape=out_shap...]
    pallas_call x5 -> x3, Pallas kernels: 19.6 us -> 12.1 us  [convolve(): pl.pallas_call(functools.partial(convolve_kernel, arrivals, begins), out_...]
    ppermute x7 -> x9, waiting for transfers between devices: 10.3 us -> 7.03 us  [send(): return lax.ppermute(block, 'sgt', pairs)]
    unnamed x26 -> x16, local copies, waits for them, and re-layouts: 3.04 us -> 0.03 us
    ppermute x7 -> x9, starting transfers between devices: 10.7 us -> 13.4 us  [send(): return lax.ppermute(block, 'sgt', pairs)]
    pallas_call x1, Pallas kernels: 6.5 us -> 7.62 us  [project(): pl.pallas_call(functools.partial(project_kernel, steps), out_shape=[jax.S...]
  transfers between devices with their start and end apart: 7 -> 9, of which waited for: 4 -> 3; matrix products, arithmetic and copies ran while one was open for 12% -> 13% of each run, Pallas kernels for 24% -> 27%
where the time goes in v3:
time: 84.9 us; the launch traced here: 84.7 us
  Pallas kernels  38.2 us (45%)
  blocking collectives  13.9 us (16%)
  starting transfers between devices  13.4 us (16%)
  waiting for transfers between devices  7.03 us (8%)
  other arithmetic  6.16 us (7%)
  local copies, waits for them, and re-layouts  5.68 us (7%)
    pallas_call x2, Pallas kernels, finish(): pl.pallas_call(functools.partial(finish_kernel, late), out_shape=out_shap...  14.5 us
    all_to_all x1, blocking collectives, local(): lax.all_to_all(peaks, 'work', split_axis=0, concat_axis=0, tiled=True)  13.9 us
    ppermute x9, starting transfers between devices, send(): return lax.ppermute(block, 'sgt', pairs)  13.4 us
    pallas_call x3, Pallas kernels, convolve(): pl.pallas_call(functools.partial(convolve_kernel, arrivals, begins), out_...  12.1 us
    pallas_call x1, Pallas kernels, project(): pl.pallas_call(functools.partial(project_kernel, steps), out_shape=[jax.S...  7.62 us
    ppermute x9, waiting for transfers between devices, send(): return lax.ppermute(block, 'sgt', pairs)  7.03 us
    pallas_call x1, Pallas kernels, tables(): pl.pallas_call(tables_kernel, out_shape=jax.ShapeDtypeStruct((NPER, SPAN,...  3.88 us
    transpose x1, local copies, waits for them, and re-layouts, local(): slips = jnp.transpose(slip_rate[0], (0, 3, 1, 2)).reshape(SLOTS, L * V, PB)  3.87 us
  transfers between devices with their start and end apart: 9, of which 3 were waited for; matrix products, arithmetic and copies ran while one was open for 13% of the time, Pallas kernels for 27%

profile of v3, /device:TPU:0, one launch (start us, length us, event | category | flops | bytes accessed | tf_op | source)
XLA Modules:
  0.0 84.7 jit_solution(12152503913984047477)
XLA Ops:
  0.0 0.0 copy-start
  0.0 0.0 copy-start.2
  0.0 0.0 copy-start.6
  0.0 0.0 copy-start.7
  0.0 0.0 copy-start.3
  0.0 7.6 %project.1 = (bf16[256,1024]{1,0:T(8,128)(2,1)}, bf16[256,1024]{1,0:T(8,128)(2,1)}, bf16[256,1024]{1,0:T(8,128)(2,1)}, bf16[256,1024]{1,0:T(8,128)(2,1)}, bf16[2...) custom-call(s32[8,128]{1,0:T(8,128)} %bitcast.29, ...), custom_call_target="tpu_custom_call" | custom-call | flops 400000000 | bytes 12800000 | tf_op jit(solution)/shard_map/project/pallas_call | solution.py:115
  7.6 0.1 collective-permute-start
  7.7 5.0 %collective-permute-start.2 = (bf16[256,1024]{1,0:T(8,128)(2,1)}, bf16[256,1024]{1,0:T(8,128)(2,1)S(1)}, u32[]{:S(2)}, u32[]{:S(2)}) collective-permute-start(bf16[256,1024]{1,0:T(8,128)(2,1)} %get-tuple-element.38), channel_id=1, source_target_pairs={{0,64},{16,80},{32,96},{48,112},{64,0},{80,16},{96,32},{112,48},{1... | collective-permute-start | bytes 1572872 | tf_op jit(solution)/shard_map/ppermute | solution.py:457
  12.8 0.1 collective-permute-start.3
  12.8 1.3 %collective-permute-start.4 = (bf16[256,1024]{1,0:T(8,128)(2,1)}, bf16[256,1024]{1,0:T(8,128)(2,1)S(1)}, u32[]{:S(2)}, u32[]{:S(2)}) collective-permute-start(bf16[256,1024]{1,0:T(8,128)(2,1)} %get-tuple-element.47), channel_id=1, source_target_pairs={{0,32},{16,48},{32,64},{48,80},{64,96},{80,112},{96,0},{112,16},{1... | collective-permute-start | bytes 1572872 | tf_op jit(solution)/shard_map/ppermute | solution.py:457
  14.1 2.4 %collective-permute-start.7 = (bf16[256,1024]{1,0:T(8,128)(2,1)}, bf16[256,1024]{1,0:T(8,128)(2,1)S(1)}, u32[]{:S(2)}, u32[]{:S(2)}) collective-permute-start(bf16[256,1024]{1,0:T(8,128)(2,1)} %get-tuple-element.51), channel_id=1, source_target_pairs={{0,96},{16,112},{32,0},{48,16},{64,32},{80,48},{96,64},{112,80},{1... | collective-permute-start | bytes 1572872 | tf_op jit(solution)/shard_map/ppermute | solution.py:457
  16.6 0.0 copy-done.2
  16.6 0.2 shift-right-arithmetic_reduce_fusion
  16.8 0.0 copy-done.6
  16.8 0.7 dynamic_slice.12
  17.4 0.0 copy-done
  17.4 0.2 dynamic-slice_reduce_fusion
  17.6 0.1 stack.45
  17.7 0.2 fusion.5
  17.9 0.7 compare_select_fusion.7
  18.6 0.1 pad_add_fusion.info_ref
  18.7 0.0 copy-done.7
  18.7 0.2 convert_reduce_fusion
  18.9 0.1 pad_add_fusion.1.place_ref
  18.9 0.0 collective-permute-done.rest_1_
  18.9 0.0 copy-done.3
  19.0 3.7 %fusion.2 = (f32[44,1,640]{2,1,0:T(1,128)S(1)}, f32[44,1,640]{2,1,0:T(1,128)S(1)}) fusion(f32[640]{0:T(1024)S(1)} %subtract_convert_fusion, f32[44]{0:T(128)S(1)} %get-tuple-element.67, f32[44]{0:T(128)S(1)} %get-tuple-element.66, f32[44]{0:T(128)S(1)} %get-tuple-element.65), kind=kLoop, calls=%fused_computation.6 | loop fusion | flops 168960 | bytes 228368 | tf_op jit(solution)/shard_map/mul | solution.py:179
  22.7 0.1 fusion
  22.9 0.1 reshape.393.v_ref
  23.0 0.7 sine_multiply_fusion
  23.7 0.1 fusion.3
  23.8 0.1 collective-permute-start.1
  23.9 2.0 %collective-permute-done.2.rest_0_ = bf16[256,1024]{1,0:T(8,128)(2,1)S(1)} collective-permute-done((bf16[256,1024]{1,0:T(8,128)(2,1)}, bf16[256,1024]{1,0:T(8,128)(2,1)S(1)}, u32[]{:S(2)}, u32[]{:S(2)}) %collective-permute-start.2) | collective-permute-done | bytes 524320 | tf_op jit(solution)/shard_map/ppermute | solution.py:457
  25.9 2.6 %collective-permute-start.6 = (bf16[256,512]{1,0:T(8,128)(2,1)}, bf16[256,512]{1,0:T(8,128)(2,1)S(1)}, u32[]{:S(2)}, u32[]{:S(2)}) collective-permute-start(bf16[256,512]{1,0:T(8,128)(2,1)} %get-tuple-element.49), channel_id=1, source_target_pairs={{0,112},{16,96},{32,16},{48,0},{64,48},{80,32},{96,80},{112,64},{1... | collective-permute-start | bytes 786440 | tf_op jit(solution)/shard_map/ppermute | solution.py:457
  28.5 0.0 copy-start.1
  28.5 3.9 %copy.15 = bf16[8,32,64,128]{3,2,1,0:T(8,128)(2,1)S(1)} copy(bf16[8,32,64,128]{3,1,2,0:T(8,128)(2,1)} %bitcast.27) | data formatting | bytes 8388608 | tf_op jit(solution)/shard_map/transpose | solution.py:490
  32.4 3.9 %tables.1.rest_4_.rest_6_ = bf16[44,128,512]{2,1,0:T(8,128)(2,1)S(1)} custom-call(f32[11,8,128]{2,1,0:T(8,128)S(1)} %bitcast.26, f32[11,8,384]{2,1,0:T(8,128)S(1)} %reshape.393.v_ref), custom_call_target="tpu_custom_call" | custom-call | flops 14417920 | bytes 6000000 | tf_op jit(solution)/shard_map/tables/pallas_call | solution.py:183
  36.3 0.0 copy-done.1
  36.3 4.0 %convolve.3.rest_3_ = f32[512,256]{1,0:T(8,128)S(1)} custom-call(s32[16]{0:T(128)S(1)} %pad_add_fusion.info_ref, bf16[256,1024]{1,0:T(8,128)(2,1)S(1)} %copy-done.1, bf16[256,1024]{1,0:T(8,128)(2,1)S(1)} %collective-permute-done.rest_1_, bf16[8,2048,128]{2,1,0:T(8,128)(2,1)S(1)} %bitcast.21), custom_call_target="tpu_custom_call" | custom-call | flops 3600000000 | bytes 2097152 | tf_op jit(solution)/shard_map/convolve/pallas_call | solution.py:275
  40.4 0.0 copy-start.5
  40.4 0.0 copy-start.4
  40.4 0.0 collective-permute-done.3.rest_1_
  40.4 4.0 %convolve.4.rest_3_ = f32[512,256]{1,0:T(8,128)S(1)} custom-call(s32[16]{0:T(128)S(1)} %pad_add_fusion.info_ref, bf16[256,1024]{1,0:T(8,128)(2,1)S(1)} %collective-permute-done.2.rest_0_, bf16[256,1024]{1,0:T(8,128)(2,1)S(1)} %collective-permute-done.3.rest_1_, bf16[8,2048,128]{2,1,0:T(8,128)(2,1)S(1)} %bitcast.22, f32[512,256]{1,0:T(8,128)S(1)} %convolve.3.rest_3_), custom_call_target="tpu_custom_call" | custom-call | flops 3600000000 | bytes 2097152 | tf_op jit(solution)/shard_map/convolve/pallas_call | solution.py:275
  44.5 3.5 %collective-permute-done.4.rest_0_ = bf16[256,1024]{1,0:T(8,128)(2,1)S(1)} collective-permute-done((bf16[256,1024]{1,0:T(8,128)(2,1)}, bf16[256,1024]{1,0:T(8,128)(2,1)S(1)}, u32[]{:S(2)}, u32[]{:S(2)}) %collective-permute-start.4) | collective-permute-done | bytes 524320 | tf_op jit(solution)/shard_map/ppermute | solution.py:457
  48.0 1.5 %collective-permute-done.7.rest_1_ = bf16[256,1024]{1,0:T(8,128)(2,1)S(1)} collective-permute-done((bf16[256,1024]{1,0:T(8,128)(2,1)}, bf16[256,1024]{1,0:T(8,128)(2,1)S(1)}, u32[]{:S(2)}, u32[]{:S(2)}) %collective-permute-start.7) | collective-permute-done | bytes 524320 | tf_op jit(solution)/shard_map/ppermute | solution.py:457
  49.5 0.0 copy-done.5
  49.5 1.8 %collective-permute-start.8 = (bf16[256,512]{1,0:T(8,128)(2,1)S(1)}, bf16[256,512]{1,0:T(8,128)(2,1)S(1)}, u32[]{:S(2)}, u32[]{:S(2)}) collective-permute-start(bf16[256,512]{1,0:T(8,128)(2,1)S(1)} %copy-done.5), channel_id=1, source_target_pairs={{0,112},{16,96},{32,16},{48,0},{64,48},{80,32},{96,80},{112,64},{1... | collective-permute-start | bytes 786440 | tf_op jit(solution)/shard_map/ppermute | solution.py:457
  51.3 0.0 copy-done.4
  51.3 0.0 collective-permute-start.5
  51.4 4.1 %convolve.5.rest_3_.rest_5_ = f32[512,256]{1,0:T(8,128)S(1)} custom-call(s32[16]{0:T(128)S(1)} %pad_add_fusion.info_ref, bf16[256,1024]{1,0:T(8,128)(2,1)S(1)} %collective-permute-done.4.rest_0_, bf16[256,1024]{1,0:T(8,128)(2,1)S(1)} %collective-permute-done.7.rest_1_, bf16[8,2048,128]{2,1,0:T(8,128)(2,1)S(1)} %bitcast.23, f32[512,256]{1,0:T(8,128)S(1)} %convolve.4.rest_3_), custom_call_target="tpu_custom_call" | custom-call | flops 3600000000 | bytes 2097152 | tf_op jit(solution)/shard_map/convolve/pallas_call | solution.py:275
  55.4 0.0 collective-permute-done.1.rest_0_
  55.4 0.0 collective-permute-done.6.rest_1_.rest_2_
  55.4 6.8 %finish.2 = (f32[16,3,128]{2,1,0:T(4,128)S(1)}, bf16[128,512]{1,0:T(8,128)(2,1)S(1)}) custom-call(s32[16]{0:T(128)S(1)} %pad_add_fusion.info_ref, s32[88]{0:T(128)S(1)} %pad_add_fusion.1.place_ref, bf16[256,512]{1,0:T(8,128)(2,1)S(1)} %collective-permute-done.1.rest_0_, bf16[256,512]{1,0:T(8,128)(2,1)S(1)} %collective-permute-done.6.rest_1_.rest_2_, ...), custom_call_target="tpu_custom_call" | custom-call | flops 3600000000 | bytes 8000000 | tf_op jit(solution)/shard_map/finish/pallas_call | solution.py:436
  62.2 0.0 collective-permute-done.8.rest_3_
  62.3 0.0 collective-permute-done.5.rest_1_
  62.3 7.7 %finish.3 = f32[16,3,128]{2,1,0:T(4,128)S(1)} custom-call(s32[16]{0:T(128)S(1)} %pad_add_fusion.info_ref, s32[88]{0:T(128)S(1)} %pad_add_fusion.1.place_ref, bf16[256,512]{1,0:T(8,128)(2,1)S(1)} %collective-permute-done.1.rest_0_, bf16[256,512]{1,0:T(8,128)(2,1)S(1)} %collective-permute-done.5.rest_1_, ...), custom_call_target="tpu_custom_call" | custom-call | flops 3600000000 | bytes 8000000 | tf_op jit(solution)/shard_map/finish/pallas_call | solution.py:436
  70.0 13.9 %all_to_all.5 = f32[16,3,128]{2,1,0:T(4,128)S(1)} all-to-all(f32[16,3,128]{2,1,0:T(4,128)S(1)} %finish.3), channel_id=1, replica_groups=mesh['sgt'=8,'work'=16] {'work'}, dimensions={0} | all-to-all | bytes 49152 | tf_op jit(solution)/shard_map/all_to_all | solution.py:529
  83.9 0.1 reshape.395
  84.0 0.6 copy.17
  (7 shorter events, 0.1 us)
Async XLA Ops:
  0.0 17.4 %copy-start = (s32[128,8]{0,1:T(8,128)S(1)}, s32[128,8]{0,1:T(8,128)}, u32[]{:S(2)}) copy-start(s32[128,8]{0,1:T(8,128)} %param.14) | copy-start | bytes 12292
  0.0 16.6 %copy-start.2 = (s32[128,8]{0,1:T(8,128)S(1)}, s32[128,8]{0,1:T(8,128)}, u32[]{:S(2)}) copy-start(s32[128,8]{0,1:T(8,128)} %param.12) | copy-start | bytes 12292
  0.0 16.8 %copy-start.6 = (s32[128]{0:T(128)S(1)}, s32[128]{0:T(128)}, u32[]{:S(2)}) copy-start(s32[128]{0:T(128)} %param.13) | copy-start | bytes 1540
  0.0 18.7 %copy-start.7 = (s32[44]{0:T(128)S(1)}, s32[44]{0:T(128)}, u32[]{:S(2)}) copy-start(s32[44]{0:T(128)} %param.16) | copy-start | bytes 532
  0.0 18.9 %copy-start.3 = (f32[44]{0:T(128)S(1)}, f32[44]{0:T(128)}, u32[]{:S(2)}) copy-start(f32[44]{0:T(128)} %param.15) | copy-start | bytes 532
  7.6 11.3 %collective-permute-start = (bf16[256,1024]{1,0:T(8,128)(2,1)}, bf16[256,1024]{1,0:T(8,128)(2,1)S(1)}, u32[]{:S(2)}, u32[]{:S(2)}) collective-permute-start(bf16[256,1024]{1,0:T(8,128)(2,1)} %get-tuple-element.33), channel_id=1, source_target_pairs={{0,16},{16,0},{32,48},{48,32},{64,80},{80,64},{96,112},{112,96},{1... | collective-permute-start | bytes 1572872 | tf_op jit(solution)/shard_map/ppermute | solution.py:457
  7.7 18.1 %collective-permute-start.2 = (bf16[256,1024]{1,0:T(8,128)(2,1)}, bf16[256,1024]{1,0:T(8,128)(2,1)S(1)}, u32[]{:S(2)}, u32[]{:S(2)}) collective-permute-start(bf16[256,1024]{1,0:T(8,128)(2,1)} %get-tuple-element.38), channel_id=1, source_target_pairs={{0,64},{16,80},{32,96},{48,112},{64,0},{80,16},{96,32},{112,48},{1... | collective-permute-start | bytes 1572872 | tf_op jit(solution)/shard_map/ppermute | solution.py:457
  12.8 27.6 %collective-permute-start.3 = (bf16[256,1024]{1,0:T(8,128)(2,1)}, bf16[256,1024]{1,0:T(8,128)(2,1)S(1)}, u32[]{:S(2)}, u32[]{:S(2)}) collective-permute-start(bf16[256,1024]{1,0:T(8,128)(2,1)} %get-tuple-element.40), channel_id=1, source_target_pairs={{0,80},{16,64},{32,112},{48,96},{64,16},{80,0},{96,48},{112,32},{1... | collective-permute-start | bytes 1572872 | tf_op jit(solution)/shard_map/ppermute | solution.py:457
  12.8 35.2 %collective-permute-start.4 = (bf16[256,1024]{1,0:T(8,128)(2,1)}, bf16[256,1024]{1,0:T(8,128)(2,1)S(1)}, u32[]{:S(2)}, u32[]{:S(2)}) collective-permute-start(bf16[256,1024]{1,0:T(8,128)(2,1)} %get-tuple-element.47), channel_id=1, source_target_pairs={{0,32},{16,48},{32,64},{48,80},{64,96},{80,112},{96,0},{112,16},{1... | collective-permute-start | bytes 1572872 | tf_op jit(solution)/shard_map/ppermute | solution.py:457
  14.1 35.4 %collective-permute-start.7 = (bf16[256,1024]{1,0:T(8,128)(2,1)}, bf16[256,1024]{1,0:T(8,128)(2,1)S(1)}, u32[]{:S(2)}, u32[]{:S(2)}) collective-permute-start(bf16[256,1024]{1,0:T(8,128)(2,1)} %get-tuple-element.51), channel_id=1, source_target_pairs={{0,96},{16,112},{32,0},{48,16},{64,32},{80,48},{96,64},{112,80},{1... | collective-permute-start | bytes 1572872 | tf_op jit(solution)/shard_map/ppermute | solution.py:457
  23.8 31.6 %collective-permute-start.1 = (bf16[256,512]{1,0:T(8,128)(2,1)}, bf16[256,512]{1,0:T(8,128)(2,1)S(1)}, u32[]{:S(2)}, u32[]{:S(2)}) collective-permute-start(bf16[256,512]{1,0:T(8,128)(2,1)} %get-tuple-element.34), channel_id=1, source_target_pairs={{0,48},{16,32},{32,80},{48,64},{64,112},{80,96},{96,16},{112,0},{1... | collective-permute-start | bytes 786440 | tf_op jit(solution)/shard_map/ppermute | solution.py:457
  25.9 29.6 %collective-permute-start.6 = (bf16[256,512]{1,0:T(8,128)(2,1)}, bf16[256,512]{1,0:T(8,128)(2,1)S(1)}, u32[]{:S(2)}, u32[]{:S(2)}) collective-permute-start(bf16[256,512]{1,0:T(8,128)(2,1)} %get-tuple-element.49), channel_id=1, source_target_pairs={{0,112},{16,96},{32,16},{48,0},{64,48},{80,32},{96,80},{112,64},{1... | collective-permute-start | bytes 786440 | tf_op jit(solution)/shard_map/ppermute | solution.py:457
  28.5 7.8 %copy-start.1 = (bf16[256,1024]{1,0:T(8,128)(2,1)S(1)}, bf16[256,1024]{1,0:T(8,128)(2,1)}, u32[]{:S(2)}) copy-start(bf16[256,1024]{1,0:T(8,128)(2,1)} %get-tuple-element.43.rest_0_) | copy-start | bytes 1572868
  40.4 9.2 %copy-start.5 = (bf16[256,512]{1,0:T(8,128)(2,1)S(1)}, bf16[256,512]{1,0:T(8,128)(2,1)}, u32[]{:S(2)}) copy-start(bf16[256,512]{1,0:T(8,128)(2,1)} %get-tuple-element.52) | copy-start | bytes 786436
  40.4 11.0 %copy-start.4 = (bf16[256,512]{1,0:T(8,128)(2,1)S(1)}, bf16[256,512]{1,0:T(8,128)(2,1)}, u32[]{:S(2)}) copy-start(bf16[256,512]{1,0:T(8,128)(2,1)} %get-tuple-element.48) | copy-start | bytes 786436
  49.5 12.7 %collective-permute-start.8 = (bf16[256,512]{1,0:T(8,128)(2,1)S(1)}, bf16[256,512]{1,0:T(8,128)(2,1)S(1)}, u32[]{:S(2)}, u32[]{:S(2)}) collective-permute-start(bf16[256,512]{1,0:T(8,128)(2,1)S(1)} %copy-done.5), channel_id=1, source_target_pairs={{0,112},{16,96},{32,16},{48,0},{64,48},{80,32},{96,80},{112,64},{1... | collective-permute-start | bytes 786440 | tf_op jit(solution)/shard_map/ppermute | solution.py:457
  51.3 10.9 %collective-permute-start.5 = (bf16[256,512]{1,0:T(8,128)(2,1)S(1)}, bf16[256,512]{1,0:T(8,128)(2,1)S(1)}, u32[]{:S(2)}, u32[]{:S(2)}) collective-permute-start(bf16[256,512]{1,0:T(8,128)(2,1)S(1)} %copy-done.4), channel_id=1, source_target_pairs={{0,48},{16,32},{32,80},{48,64},{64,112},{80,96},{96,16},{112,0},{1... | collective-permute-start | bytes 786440 | tf_op jit(solution)/shard_map/ppermute | solution.py:457

commit v4 on v3

--- a/solution.py
+++ b/solution.py
@@ -28,7 +28,7 @@
 HALF = NT // 2
 SPAN = 128
 TSTEP = 4
-QSTEP = 11
+QSTEP = 22
 SMALL = 12 * 1024 * 1024
 LARGE = 28 * 1024 * 1024
 PROJECT = 60 * 1024 * 1024
@@ -67,11 +67,11 @@
 def project_kernel(steps, fp_ref, sgt_ref, mom_ref, *rest):
     parts = pieces(steps)
     outs, rest = rest[: len(parts)], rest[len(parts) :]
-    taken, scr, table, moments, in_sem, out_sem, small_sem = rest
+    taken, scr, table, chosen, moments, in_sem, out_sem, small_sem = rest
     fetch_table = pltpu.make_async_copy(fp_ref, table, small_sem.at[0])
     fetch_moments = pltpu.make_async_copy(mom_ref, moments, small_sem.at[1])
+    fetch_moments.start()
     fetch_table.start()
-    fetch_moments.start()
     me = lax.axis_index("sgt")
     work = lax.axis_index("work")
 
@@ -83,15 +83,6 @@
     for n in range(HELD):
         for c in range(2):
             load(n, c).start()
-    fetch_table.wait()
-    chosen = []
-    for dz, dc in steps:
-        rupture = target(me, dz, dc) * OWNERS + work
-        found = jnp.int32(0)
-        for k in range(SLOTS):
-            block = table[k, rupture]
-            found = jnp.where((block >> 2) == me, block & 3, found)
-        chosen.append(found)
     fetch_moments.wait()
 
     @pl.loop(0, HELD)
@@ -102,6 +93,18 @@
         for c in range(2):
             load(n, c).wait()
             project_block(weights, taken.at[n], scr.at[n], c)
+
+        @pl.when(n == 0)
+        def _():
+            fetch_table.wait()
+            for m, (dz, dc) in enumerate(steps):
+                rupture = target(me, dz, dc) * OWNERS + work
+                found = jnp.int32(0)
+                for k in range(SLOTS):
+                    block = table[k, rupture]
+                    found = jnp.where((block >> 2) == me, block & 3, found)
+                chosen[m] = found
+
         for m, (step, span) in enumerate(parts):
             copy = pltpu.make_async_copy(scr.at[n, :, span], outs[m], out_sem.at[m])
             pl.when(chosen[step] == n)(copy.start)
@@ -127,6 +130,7 @@
             pltpu.VMEM((HELD, NJ, 2, PB, NT), jnp.bfloat16),
             pltpu.VMEM((HELD, 2 * PB, NT), jnp.bfloat16),
             pltpu.SMEM((SLOTS, 128), jnp.int32),
+            pltpu.SMEM((SLOTS,), jnp.int32),
             pltpu.VMEM((NJ, HELD, PB), jnp.float32),
             pltpu.SemaphoreType.DMA((2 * HELD,)),
             pltpu.SemaphoreType.DMA((len(parts),)),

time: 84.9 us -> 84 us (0.989)
  starting transfers between devices: 13.4 us -> 11.9 us
    ppermute x9, starting transfers between devices: 13.4 us -> 11.9 us  [send(): return lax.ppermute(block, 'sgt', pairs)]
where the time goes in v4:
time: 84 us
  Pallas kernels  38.4 us (46%)
  blocking collectives  14.3 us (17%)
  starting transfers between devices  11.9 us (14%)
  waiting for transfers between devices  7.35 us (9%)
  other arithmetic  6.16 us (7%)
  local copies, waits for them, and re-layouts  5.68 us (7%)
    all_to_all x1, blocking collectives, local(): lax.all_to_all(peaks, 'work', split_axis=0, concat_axis=0, tiled=True)  14.3 us
    pallas_call x2, Pallas kernels, finish(): pl.pallas_call(functools.partial(finish_kernel, late), out_shape=out_shap...  13.9 us
    pallas_call x3, Pallas kernels, convolve(): pl.pallas_call(functools.partial(convolve_kernel, arrivals, begins), out_...  12.1 us
    ppermute x9, starting transfers between devices, send(): return lax.ppermute(block, 'sgt', pairs)  11.9 us
    pallas_call x1, Pallas kernels, project(): pl.pallas_call(functools.partial(project_kernel, steps), out_shape=[jax.S...  8.44 us
    ppermute x9, waiting for transfers between devices, send(): return lax.ppermute(block, 'sgt', pairs)  7.35 us
    pallas_call x1, Pallas kernels, tables(): pl.pallas_call(tables_kernel, out_shape=jax.ShapeDtypeStruct((NPER, SPAN,...  3.88 us
    transpose x1, local copies, waits for them, and re-layouts, local(): slips = jnp.transpose(slip_rate[0], (0, 3, 1, 2)).reshape(SLOTS, L * V, PB)  3.87 us
  transfers between devices with their start and end apart: 9, of which 3 were waited for; matrix products, arithmetic and copies ran while one was open for 13% of the time, Pallas kernels for 27%

profile of v4, /device:TPU:0, one launch (start us, length us, event | category | flops | bytes accessed | tf_op | source)
XLA Modules:
  0.0 84.0 jit_solution(3965681622804656416)
XLA Ops:
  0.0 0.0 copy-start
  0.0 0.0 copy-start.2
  0.0 0.0 copy-start.6
  0.0 0.0 copy-start.7
  0.0 0.0 copy-start.3
  0.0 8.4 %project.1 = (bf16[256,1024]{1,0:T(8,128)(2,1)}, bf16[256,1024]{1,0:T(8,128)(2,1)}, bf16[256,1024]{1,0:T(8,128)(2,1)}, bf16[256,1024]{1,0:T(8,128)(2,1)}, bf16[2...) custom-call(s32[8,128]{1,0:T(8,128)} %bitcast.29, ...), custom_call_target="tpu_custom_call" | custom-call | flops 400000000 | bytes 12800000 | tf_op jit(solution)/shard_map/project/pallas_call | solution.py:118
  8.5 0.1 collective-permute-start
  8.6 4.1 %collective-permute-start.2 = (bf16[256,1024]{1,0:T(8,128)(2,1)}, bf16[256,1024]{1,0:T(8,128)(2,1)S(1)}, u32[]{:S(2)}, u32[]{:S(2)}) collective-permute-start(bf16[256,1024]{1,0:T(8,128)(2,1)} %get-tuple-element.38), channel_id=1, source_target_pairs={{0,64},{16,80},{32,96},{48,112},{64,0},{80,16},{96,32},{112,48},{1... | collective-permute-start | bytes 1572872 | tf_op jit(solution)/shard_map/ppermute | solution.py:461
  12.7 0.1 collective-permute-start.3
  12.7 1.2 %collective-permute-start.4 = (bf16[256,1024]{1,0:T(8,128)(2,1)}, bf16[256,1024]{1,0:T(8,128)(2,1)S(1)}, u32[]{:S(2)}, u32[]{:S(2)}) collective-permute-start(bf16[256,1024]{1,0:T(8,128)(2,1)} %get-tuple-element.47), channel_id=1, source_target_pairs={{0,32},{16,48},{32,64},{48,80},{64,96},{80,112},{96,0},{112,16},{1... | collective-permute-start | bytes 1572872 | tf_op jit(solution)/shard_map/ppermute | solution.py:461
  14.0 2.2 %collective-permute-start.7 = (bf16[256,1024]{1,0:T(8,128)(2,1)}, bf16[256,1024]{1,0:T(8,128)(2,1)S(1)}, u32[]{:S(2)}, u32[]{:S(2)}) collective-permute-start(bf16[256,1024]{1,0:T(8,128)(2,1)} %get-tuple-element.51), channel_id=1, source_target_pairs={{0,96},{16,112},{32,0},{48,16},{64,32},{80,48},{96,64},{112,80},{1... | collective-permute-start | bytes 1572872 | tf_op jit(solution)/shard_map/ppermute | solution.py:461
  16.2 0.0 copy-done.2
  16.2 0.2 shift-right-arithmetic_reduce_fusion
  16.4 0.0 copy-done.6
  16.4 0.7 dynamic_slice.12
  17.0 0.0 copy-done
  17.0 0.2 dynamic-slice_reduce_fusion
  17.2 0.1 stack.45
  17.3 0.2 fusion.5
  17.5 0.7 compare_select_fusion.7
  18.2 0.1 pad_add_fusion.info_ref
  18.3 0.0 copy-done.7
  18.3 0.2 convert_reduce_fusion
  18.5 0.1 pad_add_fusion.1.place_ref
  18.5 0.0 collective-permute-done.rest_1_
  18.5 0.0 copy-done.3
  18.6 3.7 %fusion.2 = (f32[44,1,640]{2,1,0:T(1,128)S(1)}, f32[44,1,640]{2,1,0:T(1,128)S(1)}) fusion(f32[640]{0:T(1024)S(1)} %subtract_convert_fusion, f32[44]{0:T(128)S(1)} %get-tuple-element.67, f32[44]{0:T(128)S(1)} %get-tuple-element.66, f32[44]{0:T(128)S(1)} %get-tuple-element.65), kind=kLoop, calls=%fused_computation.6 | loop fusion | flops 168960 | bytes 228368 | tf_op jit(solution)/shard_map/mul | solution.py:183
  22.3 0.1 fusion
  22.5 0.1 reshape.393.v_ref
  22.6 0.7 sine_multiply_fusion
  23.3 0.1 fusion.3
  23.4 0.1 collective-permute-start.1
  23.5 2.3 %collective-permute-done.2.rest_0_ = bf16[256,1024]{1,0:T(8,128)(2,1)S(1)} collective-permute-done((bf16[256,1024]{1,0:T(8,128)(2,1)}, bf16[256,1024]{1,0:T(8,128)(2,1)S(1)}, u32[]{:S(2)}, u32[]{:S(2)}) %collective-permute-start.2) | collective-permute-done | bytes 524320 | tf_op jit(solution)/shard_map/ppermute | solution.py:461
  25.8 2.3 %collective-permute-start.6 = (bf16[256,512]{1,0:T(8,128)(2,1)}, bf16[256,512]{1,0:T(8,128)(2,1)S(1)}, u32[]{:S(2)}, u32[]{:S(2)}) collective-permute-start(bf16[256,512]{1,0:T(8,128)(2,1)} %get-tuple-element.49), channel_id=1, source_target_pairs={{0,112},{16,96},{32,16},{48,0},{64,48},{80,32},{96,80},{112,64},{1... | collective-permute-start | bytes 786440 | tf_op jit(solution)/shard_map/ppermute | solution.py:461
  28.1 0.0 copy-start.1
  28.1 3.9 %copy.15 = bf16[8,32,64,128]{3,2,1,0:T(8,128)(2,1)S(1)} copy(bf16[8,32,64,128]{3,1,2,0:T(8,128)(2,1)} %bitcast.27) | data formatting | bytes 8388608 | tf_op jit(solution)/shard_map/transpose | solution.py:494
  32.0 3.9 %tables.1.rest_4_.rest_6_ = bf16[44,128,512]{2,1,0:T(8,128)(2,1)S(1)} custom-call(f32[11,8,128]{2,1,0:T(8,128)S(1)} %bitcast.26, f32[11,8,384]{2,1,0:T(8,128)S(1)} %reshape.393.v_ref), custom_call_target="tpu_custom_call" | custom-call | flops 14417920 | bytes 6000000 | tf_op jit(solution)/shard_map/tables/pallas_call | solution.py:187
  35.9 0.0 copy-done.1
  35.9 4.0 %convolve.3.rest_3_ = f32[512,256]{1,0:T(8,128)S(1)} custom-call(s32[16]{0:T(128)S(1)} %pad_add_fusion.info_ref, bf16[256,1024]{1,0:T(8,128)(2,1)S(1)} %copy-done.1, bf16[256,1024]{1,0:T(8,128)(2,1)S(1)} %collective-permute-done.rest_1_, bf16[8,2048,128]{2,1,0:T(8,128)(2,1)S(1)} %bitcast.21), custom_call_target="tpu_custom_call" | custom-call | flops 3600000000 | bytes 2097152 | tf_op jit(solution)/shard_map/convolve/pallas_call | solution.py:279
  40.0 0.0 copy-start.5
  40.0 0.0 copy-start.4
  40.0 0.0 collective-permute-done.3.rest_1_
  40.0 4.0 %convolve.4.rest_3_ = f32[512,256]{1,0:T(8,128)S(1)} custom-call(s32[16]{0:T(128)S(1)} %pad_add_fusion.info_ref, bf16[256,1024]{1,0:T(8,128)(2,1)S(1)} %collective-permute-done.2.rest_0_, bf16[256,1024]{1,0:T(8,128)(2,1)S(1)} %collective-permute-done.3.rest_1_, bf16[8,2048,128]{2,1,0:T(8,128)(2,1)S(1)} %bitcast.22, f32[512,256]{1,0:T(8,128)S(1)} %convolve.3.rest_3_), custom_call_target="tpu_custom_call" | custom-call | flops 3600000000 | bytes 2097152 | tf_op jit(solution)/shard_map/convolve/pallas_call | solution.py:279
  44.0 3.8 %collective-permute-done.4.rest_0_ = bf16[256,1024]{1,0:T(8,128)(2,1)S(1)} collective-permute-done((bf16[256,1024]{1,0:T(8,128)(2,1)}, bf16[256,1024]{1,0:T(8,128)(2,1)S(1)}, u32[]{:S(2)}, u32[]{:S(2)}) %collective-permute-start.4) | collective-permute-done | bytes 524320 | tf_op jit(solution)/shard_map/ppermute | solution.py:461
  47.9 1.2 %collective-permute-done.7.rest_1_ = bf16[256,1024]{1,0:T(8,128)(2,1)S(1)} collective-permute-done((bf16[256,1024]{1,0:T(8,128)(2,1)}, bf16[256,1024]{1,0:T(8,128)(2,1)S(1)}, u32[]{:S(2)}, u32[]{:S(2)}) %collective-permute-start.7) | collective-permute-done | bytes 524320 | tf_op jit(solution)/shard_map/ppermute | solution.py:461
  49.1 0.0 copy-done.5
  49.1 1.8 %collective-permute-start.8 = (bf16[256,512]{1,0:T(8,128)(2,1)S(1)}, bf16[256,512]{1,0:T(8,128)(2,1)S(1)}, u32[]{:S(2)}, u32[]{:S(2)}) collective-permute-start(bf16[256,512]{1,0:T(8,128)(2,1)S(1)} %copy-done.5), channel_id=1, source_target_pairs={{0,112},{16,96},{32,16},{48,0},{64,48},{80,32},{96,80},{112,64},{1... | collective-permute-start | bytes 786440 | tf_op jit(solution)/shard_map/ppermute | solution.py:461
  50.9 0.0 copy-done.4
  50.9 0.0 collective-permute-start.5
  51.0 4.0 %convolve.5.rest_3_.rest_5_ = f32[512,256]{1,0:T(8,128)S(1)} custom-call(s32[16]{0:T(128)S(1)} %pad_add_fusion.info_ref, bf16[256,1024]{1,0:T(8,128)(2,1)S(1)} %collective-permute-done.4.rest_0_, bf16[256,1024]{1,0:T(8,128)(2,1)S(1)} %collective-permute-done.7.rest_1_, bf16[8,2048,128]{2,1,0:T(8,128)(2,1)S(1)} %bitcast.23, f32[512,256]{1,0:T(8,128)S(1)} %convolve.4.rest_3_), custom_call_target="tpu_custom_call" | custom-call | flops 3600000000 | bytes 2097152 | tf_op jit(solution)/shard_map/convolve/pallas_call | solution.py:279
  55.0 0.0 collective-permute-done.1.rest_0_
  55.0 0.0 collective-permute-done.6.rest_1_.rest_2_
  55.0 6.5 %finish.2 = (f32[16,3,128]{2,1,0:T(4,128)S(1)}, bf16[128,512]{1,0:T(8,128)(2,1)S(1)}) custom-call(s32[16]{0:T(128)S(1)} %pad_add_fusion.info_ref, s32[88]{0:T(128)S(1)} %pad_add_fusion.1.place_ref, bf16[256,512]{1,0:T(8,128)(2,1)S(1)} %collective-permute-done.1.rest_0_, bf16[256,512]{1,0:T(8,128)(2,1)S(1)} %collective-permute-done.6.rest_1_.rest_2_, ...), custom_call_target="tpu_custom_call" | custom-call | flops 3600000000 | bytes 8000000 | tf_op jit(solution)/shard_map/finish/pallas_call | solution.py:440
  61.5 0.0 collective-permute-done.8.rest_3_
  61.5 0.0 collective-permute-done.5.rest_1_
  61.5 7.4 %finish.3 = f32[16,3,128]{2,1,0:T(4,128)S(1)} custom-call(s32[16]{0:T(128)S(1)} %pad_add_fusion.info_ref, s32[88]{0:T(128)S(1)} %pad_add_fusion.1.place_ref, bf16[256,512]{1,0:T(8,128)(2,1)S(1)} %collective-permute-done.1.rest_0_, bf16[256,512]{1,0:T(8,128)(2,1)S(1)} %collective-permute-done.5.rest_1_, ...), custom_call_target="tpu_custom_call" | custom-call | flops 3600000000 | bytes 8000000 | tf_op jit(solution)/shard_map/finish/pallas_call | solution.py:440
  69.0 14.3 %all_to_all.5 = f32[16,3,128]{2,1,0:T(4,128)S(1)} all-to-all(f32[16,3,128]{2,1,0:T(4,128)S(1)} %finish.3), channel_id=1, replica_groups=mesh['sgt'=8,'work'=16] {'work'}, dimensions={0} | all-to-all | bytes 49152 | tf_op jit(solution)/shard_map/all_to_all | solution.py:533
  83.2 0.1 reshape.395
  83.3 0.6 copy.17
  (7 shorter events, 0.1 us)
Async XLA Ops:
  0.0 17.0 %copy-start = (s32[128,8]{0,1:T(8,128)S(1)}, s32[128,8]{0,1:T(8,128)}, u32[]{:S(2)}) copy-start(s32[128,8]{0,1:T(8,128)} %param.14) | copy-start | bytes 12292
  0.0 16.2 %copy-start.2 = (s32[128,8]{0,1:T(8,128)S(1)}, s32[128,8]{0,1:T(8,128)}, u32[]{:S(2)}) copy-start(s32[128,8]{0,1:T(8,128)} %param.12) | copy-start | bytes 12292
  0.0 16.4 %copy-start.6 = (s32[128]{0:T(128)S(1)}, s32[128]{0:T(128)}, u32[]{:S(2)}) copy-start(s32[128]{0:T(128)} %param.13) | copy-start | bytes 1540
  0.0 18.3 %copy-start.7 = (s32[44]{0:T(128)S(1)}, s32[44]{0:T(128)}, u32[]{:S(2)}) copy-start(s32[44]{0:T(128)} %param.16) | copy-start | bytes 532
  0.0 18.5 %copy-start.3 = (f32[44]{0:T(128)S(1)}, f32[44]{0:T(128)}, u32[]{:S(2)}) copy-start(f32[44]{0:T(128)} %param.15) | copy-start | bytes 532
  8.5 10.1 %collective-permute-start = (bf16[256,1024]{1,0:T(8,128)(2,1)}, bf16[256,1024]{1,0:T(8,128)(2,1)S(1)}, u32[]{:S(2)}, u32[]{:S(2)}) collective-permute-start(bf16[256,1024]{1,0:T(8,128)(2,1)} %get-tuple-element.33), channel_id=1, source_target_pairs={{0,16},{16,0},{32,48},{48,32},{64,80},{80,64},{96,112},{112,96},{1... | collective-permute-start | bytes 1572872 | tf_op jit(solution)/shard_map/ppermute | solution.py:461
  8.6 17.2 %collective-permute-start.2 = (bf16[256,1024]{1,0:T(8,128)(2,1)}, bf16[256,1024]{1,0:T(8,128)(2,1)S(1)}, u32[]{:S(2)}, u32[]{:S(2)}) collective-permute-start(bf16[256,1024]{1,0:T(8,128)(2,1)} %get-tuple-element.38), channel_id=1, source_target_pairs={{0,64},{16,80},{32,96},{48,112},{64,0},{80,16},{96,32},{112,48},{1... | collective-permute-start | bytes 1572872 | tf_op jit(solution)/shard_map/ppermute | solution.py:461
  12.7 27.3 %collective-permute-start.3 = (bf16[256,1024]{1,0:T(8,128)(2,1)}, bf16[256,1024]{1,0:T(8,128)(2,1)S(1)}, u32[]{:S(2)}, u32[]{:S(2)}) collective-permute-start(bf16[256,1024]{1,0:T(8,128)(2,1)} %get-tuple-element.40), channel_id=1, source_target_pairs={{0,80},{16,64},{32,112},{48,96},{64,16},{80,0},{96,48},{112,32},{1... | collective-permute-start | bytes 1572872 | tf_op jit(solution)/shard_map/ppermute | solution.py:461
  12.7 35.1 %collective-permute-start.4 = (bf16[256,1024]{1,0:T(8,128)(2,1)}, bf16[256,1024]{1,0:T(8,128)(2,1)S(1)}, u32[]{:S(2)}, u32[]{:S(2)}) collective-permute-start(bf16[256,1024]{1,0:T(8,128)(2,1)} %get-tuple-element.47), channel_id=1, source_target_pairs={{0,32},{16,48},{32,64},{48,80},{64,96},{80,112},{96,0},{112,16},{1... | collective-permute-start | bytes 1572872 | tf_op jit(solution)/shard_map/ppermute | solution.py:461
  14.0 35.1 %collective-permute-start.7 = (bf16[256,1024]{1,0:T(8,128)(2,1)}, bf16[256,1024]{1,0:T(8,128)(2,1)S(1)}, u32[]{:S(2)}, u32[]{:S(2)}) collective-permute-start(bf16[256,1024]{1,0:T(8,128)(2,1)} %get-tuple-element.51), channel_id=1, source_target_pairs={{0,96},{16,112},{32,0},{48,16},{64,32},{80,48},{96,64},{112,80},{1... | collective-permute-start | bytes 1572872 | tf_op jit(solution)/shard_map/ppermute | solution.py:461
  23.4 31.6 %collective-permute-start.1 = (bf16[256,512]{1,0:T(8,128)(2,1)}, bf16[256,512]{1,0:T(8,128)(2,1)S(1)}, u32[]{:S(2)}, u32[]{:S(2)}) collective-permute-start(bf16[256,512]{1,0:T(8,128)(2,1)} %get-tuple-element.34), channel_id=1, source_target_pairs={{0,48},{16,32},{32,80},{48,64},{64,112},{80,96},{96,16},{112,0},{1... | collective-permute-start | bytes 786440 | tf_op jit(solution)/shard_map/ppermute | solution.py:461
  25.8 29.3 %collective-permute-start.6 = (bf16[256,512]{1,0:T(8,128)(2,1)}, bf16[256,512]{1,0:T(8,128)(2,1)S(1)}, u32[]{:S(2)}, u32[]{:S(2)}) collective-permute-start(bf16[256,512]{1,0:T(8,128)(2,1)} %get-tuple-element.49), channel_id=1, source_target_pairs={{0,112},{16,96},{32,16},{48,0},{64,48},{80,32},{96,80},{112,64},{1... | collective-permute-start | bytes 786440 | tf_op jit(solution)/shard_map/ppermute | solution.py:461
  28.1 7.8 %copy-start.1 = (bf16[256,1024]{1,0:T(8,128)(2,1)S(1)}, bf16[256,1024]{1,0:T(8,128)(2,1)}, u32[]{:S(2)}) copy-start(bf16[256,1024]{1,0:T(8,128)(2,1)} %get-tuple-element.43.rest_0_) | copy-start | bytes 1572868
  40.0 9.2 %copy-start.5 = (bf16[256,512]{1,0:T(8,128)(2,1)S(1)}, bf16[256,512]{1,0:T(8,128)(2,1)}, u32[]{:S(2)}) copy-start(bf16[256,512]{1,0:T(8,128)(2,1)} %get-tuple-element.52) | copy-start | bytes 786436
  40.0 11.0 %copy-start.4 = (bf16[256,512]{1,0:T(8,128)(2,1)S(1)}, bf16[256,512]{1,0:T(8,128)(2,1)}, u32[]{:S(2)}) copy-start(bf16[256,512]{1,0:T(8,128)(2,1)} %get-tuple-element.48) | copy-start | bytes 786436
  49.1 12.4 %collective-permute-start.8 = (bf16[256,512]{1,0:T(8,128)(2,1)S(1)}, bf16[256,512]{1,0:T(8,128)(2,1)S(1)}, u32[]{:S(2)}, u32[]{:S(2)}) collective-permute-start(bf16[256,512]{1,0:T(8,128)(2,1)S(1)} %copy-done.5), channel_id=1, source_target_pairs={{0,112},{16,96},{32,16},{48,0},{64,48},{80,32},{96,80},{112,64},{1... | collective-permute-start | bytes 786440 | tf_op jit(solution)/shard_map/ppermute | solution.py:461
  50.9 10.6 %collective-permute-start.5 = (bf16[256,512]{1,0:T(8,128)(2,1)S(1)}, bf16[256,512]{1,0:T(8,128)(2,1)S(1)}, u32[]{:S(2)}, u32[]{:S(2)}) collective-permute-start(bf16[256,512]{1,0:T(8,128)(2,1)S(1)} %copy-done.4), channel_id=1, source_target_pairs={{0,48},{16,32},{32,80},{48,64},{64,112},{80,96},{96,16},{112,0},{1... | collective-permute-start | bytes 786440 | tf_op jit(solution)/shard_map/ppermute | solution.py:461

commit v5 on v4

--- a/solution.py
+++ b/solution.py
@@ -27,6 +27,7 @@
 BLOCK = 256
 HALF = NT // 2
 SPAN = 128
+AHEAD = 4
 TSTEP = 4
 QSTEP = 22
 SMALL = 12 * 1024 * 1024
@@ -80,7 +81,7 @@
             sgt_ref.at[n, :, c], taken.at[n, :, c], in_sem.at[2 * n + c]
         )
 
-    for n in range(HELD):
+    for n in range(AHEAD // 2):
         for c in range(2):
             load(n, c).start()
     fetch_moments.wait()
@@ -92,6 +93,7 @@
         )
         for c in range(2):
             load(n, c).wait()
+            pl.when(n + AHEAD // 2 < HELD)(load(n + AHEAD // 2, c).start)
             project_block(weights, taken.at[n], scr.at[n], c)
 
         @pl.when(n == 0)

time: 84 us -> 83.1 us (0.989)
  Pallas kernels: 38.4 us -> 37 us
    pallas_call x1, Pallas kernels: 8.44 us -> 7.1 us  [project(): pl.pallas_call(functools.partial(project_kernel, steps), out_shape=[jax.S...]
where the time goes in v5:
time: 83.1 us; the launch traced here: 82.9 us
  Pallas kernels  37 us (45%)
  blocking collectives  14.4 us (17%)
  starting transfers between devices  12.2 us (15%)
  waiting for transfers between devices  7.17 us (9%)
  other arithmetic  6.16 us (7%)
  local copies, waits for them, and re-layouts  5.68 us (7%)
    all_to_all x1, blocking collectives, local(): lax.all_to_all(peaks, 'work', split_axis=0, concat_axis=0, tiled=True)  14.4 us
    pallas_call x2, Pallas kernels, finish(): pl.pallas_call(functools.partial(finish_kernel, late), out_shape=out_shap...  13.9 us
    ppermute x9, starting transfers between devices, send(): return lax.ppermute(block, 'sgt', pairs)  12.2 us
    pallas_call x3, Pallas kernels, convolve(): pl.pallas_call(functools.partial(convolve_kernel, arrivals, begins), out_...  12.1 us
    ppermute x9, waiting for transfers between devices, send(): return lax.ppermute(block, 'sgt', pairs)  7.17 us
    pallas_call x1, Pallas kernels, project(): pl.pallas_call(functools.partial(project_kernel, steps), out_shape=[jax.S...  7.1 us
    pallas_call x1, Pallas kernels, tables(): pl.pallas_call(tables_kernel, out_shape=jax.ShapeDtypeStruct((NPER, SPAN,...  3.88 us
    transpose x1, local copies, waits for them, and re-layouts, local(): slips = jnp.transpose(slip_rate[0], (0, 3, 1, 2)).reshape(SLOTS, L * V, PB)  3.87 us
  transfers between devices with their start and end apart: 9, of which 3 were waited for; matrix products, arithmetic and copies ran while one was open for 13% of the time, Pallas kernels for 27%

profile of v5, /device:TPU:0, one launch (start us, length us, event | category | flops | bytes accessed | tf_op | source)
XLA Modules:
  0.0 82.9 jit_solution(10692945894557686919)
XLA Ops:
  0.0 0.0 copy-start
  0.0 0.0 copy-start.2
  0.0 0.0 copy-start.6
  0.0 0.0 copy-start.7
  0.0 0.0 copy-start.3
  0.0 7.1 %project.1 = (bf16[256,1024]{1,0:T(8,128)(2,1)}, bf16[256,1024]{1,0:T(8,128)(2,1)}, bf16[256,1024]{1,0:T(8,128)(2,1)}, bf16[256,1024]{1,0:T(8,128)(2,1)}, bf16[2...) custom-call(s32[8,128]{1,0:T(8,128)} %bitcast.29, ...), custom_call_target="tpu_custom_call" | custom-call | flops 400000000 | bytes 12800000 | tf_op jit(solution)/shard_map/project/pallas_call | solution.py:120
  7.1 0.1 collective-permute-start
  7.2 4.1 %collective-permute-start.2 = (bf16[256,1024]{1,0:T(8,128)(2,1)}, bf16[256,1024]{1,0:T(8,128)(2,1)S(1)}, u32[]{:S(2)}, u32[]{:S(2)}) collective-permute-start(bf16[256,1024]{1,0:T(8,128)(2,1)} %get-tuple-element.38), channel_id=1, source_target_pairs={{0,64},{16,80},{32,96},{48,112},{64,0},{80,16},{96,32},{112,48},{1... | collective-permute-start | bytes 1572872 | tf_op jit(solution)/shard_map/ppermute | solution.py:463
  11.3 0.1 collective-permute-start.3
  11.3 1.4 %collective-permute-start.4 = (bf16[256,1024]{1,0:T(8,128)(2,1)}, bf16[256,1024]{1,0:T(8,128)(2,1)S(1)}, u32[]{:S(2)}, u32[]{:S(2)}) collective-permute-start(bf16[256,1024]{1,0:T(8,128)(2,1)} %get-tuple-element.47), channel_id=1, source_target_pairs={{0,32},{16,48},{32,64},{48,80},{64,96},{80,112},{96,0},{112,16},{1... | collective-permute-start | bytes 1572872 | tf_op jit(solution)/shard_map/ppermute | solution.py:463
  12.8 2.2 %collective-permute-start.7 = (bf16[256,1024]{1,0:T(8,128)(2,1)}, bf16[256,1024]{1,0:T(8,128)(2,1)S(1)}, u32[]{:S(2)}, u32[]{:S(2)}) collective-permute-start(bf16[256,1024]{1,0:T(8,128)(2,1)} %get-tuple-element.51), channel_id=1, source_target_pairs={{0,96},{16,112},{32,0},{48,16},{64,32},{80,48},{96,64},{112,80},{1... | collective-permute-start | bytes 1572872 | tf_op jit(solution)/shard_map/ppermute | solution.py:463
  15.0 0.0 copy-done.2
  15.0 0.2 shift-right-arithmetic_reduce_fusion
  15.1 0.0 copy-done.6
  15.2 0.7 dynamic_slice.12
  15.8 0.0 copy-done
  15.8 0.2 dynamic-slice_reduce_fusion
  16.0 0.1 stack.45
  16.1 0.2 fusion.5
  16.3 0.7 compare_select_fusion.7
  17.0 0.1 pad_add_fusion.info_ref
  17.1 0.0 copy-done.7
  17.1 0.2 convert_reduce_fusion
  17.2 0.1 pad_add_fusion.1.place_ref
  17.3 0.0 collective-permute-done.rest_1_
  17.3 0.0 copy-done.3
  17.4 3.7 %fusion.2 = (f32[44,1,640]{2,1,0:T(1,128)S(1)}, f32[44,1,640]{2,1,0:T(1,128)S(1)}) fusion(f32[640]{0:T(1024)S(1)} %subtract_convert_fusion, f32[44]{0:T(128)S(1)} %get-tuple-element.67, f32[44]{0:T(128)S(1)} %get-tuple-element.66, f32[44]{0:T(128)S(1)} %get-tuple-element.65), kind=kLoop, calls=%fused_computation.6 | loop fusion | flops 168960 | bytes 228368 | tf_op jit(solution)/shard_map/mul | solution.py:185
  21.1 0.1 fusion
  21.2 0.1 reshape.393.v_ref
  21.4 0.7 sine_multiply_fusion
  22.1 0.1 fusion.3
  22.2 0.1 collective-permute-start.1
  22.3 2.1 %collective-permute-done.2.rest_0_ = bf16[256,1024]{1,0:T(8,128)(2,1)S(1)} collective-permute-done((bf16[256,1024]{1,0:T(8,128)(2,1)}, bf16[256,1024]{1,0:T(8,128)(2,1)S(1)}, u32[]{:S(2)}, u32[]{:S(2)}) %collective-permute-start.2) | collective-permute-done | bytes 524320 | tf_op jit(solution)/shard_map/ppermute | solution.py:463
  24.4 2.5 %collective-permute-start.6 = (bf16[256,512]{1,0:T(8,128)(2,1)}, bf16[256,512]{1,0:T(8,128)(2,1)S(1)}, u32[]{:S(2)}, u32[]{:S(2)}) collective-permute-start(bf16[256,512]{1,0:T(8,128)(2,1)} %get-tuple-element.49), channel_id=1, source_target_pairs={{0,112},{16,96},{32,16},{48,0},{64,48},{80,32},{96,80},{112,64},{1... | collective-permute-start | bytes 786440 | tf_op jit(solution)/shard_map/ppermute | solution.py:463
  26.9 0.0 copy-start.1
  26.9 3.9 %copy.15 = bf16[8,32,64,128]{3,2,1,0:T(8,128)(2,1)S(1)} copy(bf16[8,32,64,128]{3,1,2,0:T(8,128)(2,1)} %bitcast.27) | data formatting | bytes 8388608 | tf_op jit(solution)/shard_map/transpose | solution.py:496
  30.8 3.9 %tables.1.rest_4_.rest_6_ = bf16[44,128,512]{2,1,0:T(8,128)(2,1)S(1)} custom-call(f32[11,8,128]{2,1,0:T(8,128)S(1)} %bitcast.26, f32[11,8,384]{2,1,0:T(8,128)S(1)} %reshape.393.v_ref), custom_call_target="tpu_custom_call" | custom-call | flops 14417920 | bytes 6000000 | tf_op jit(solution)/shard_map/tables/pallas_call | solution.py:189
  34.7 0.0 copy-done.1
  34.7 4.0 %convolve.3.rest_3_ = f32[512,256]{1,0:T(8,128)S(1)} custom-call(s32[16]{0:T(128)S(1)} %pad_add_fusion.info_ref, bf16[256,1024]{1,0:T(8,128)(2,1)S(1)} %copy-done.1, bf16[256,1024]{1,0:T(8,128)(2,1)S(1)} %collective-permute-done.rest_1_, bf16[8,2048,128]{2,1,0:T(8,128)(2,1)S(1)} %bitcast.21), custom_call_target="tpu_custom_call" | custom-call | flops 3600000000 | bytes 2097152 | tf_op jit(solution)/shard_map/convolve/pallas_call | solution.py:281
  38.8 0.0 copy-start.5
  38.8 0.0 copy-start.4
  38.8 0.0 collective-permute-done.3.rest_1_
  38.8 4.0 %convolve.4.rest_3_ = f32[512,256]{1,0:T(8,128)S(1)} custom-call(s32[16]{0:T(128)S(1)} %pad_add_fusion.info_ref, bf16[256,1024]{1,0:T(8,128)(2,1)S(1)} %collective-permute-done.2.rest_0_, bf16[256,1024]{1,0:T(8,128)(2,1)S(1)} %collective-permute-done.3.rest_1_, bf16[8,2048,128]{2,1,0:T(8,128)(2,1)S(1)} %bitcast.22, f32[512,256]{1,0:T(8,128)S(1)} %convolve.3.rest_3_), custom_call_target="tpu_custom_call" | custom-call | flops 3600000000 | bytes 2097152 | tf_op jit(solution)/shard_map/convolve/pallas_call | solution.py:281
  42.8 3.7 %collective-permute-done.4.rest_0_ = bf16[256,1024]{1,0:T(8,128)(2,1)S(1)} collective-permute-done((bf16[256,1024]{1,0:T(8,128)(2,1)}, bf16[256,1024]{1,0:T(8,128)(2,1)S(1)}, u32[]{:S(2)}, u32[]{:S(2)}) %collective-permute-start.4) | collective-permute-done | bytes 524320 | tf_op jit(solution)/shard_map/ppermute | solution.py:463
  46.5 1.4 %collective-permute-done.7.rest_1_ = bf16[256,1024]{1,0:T(8,128)(2,1)S(1)} collective-permute-done((bf16[256,1024]{1,0:T(8,128)(2,1)}, bf16[256,1024]{1,0:T(8,128)(2,1)S(1)}, u32[]{:S(2)}, u32[]{:S(2)}) %collective-permute-start.7) | collective-permute-done | bytes 524320 | tf_op jit(solution)/shard_map/ppermute | solution.py:463
  47.9 0.0 copy-done.5
  47.9 1.8 %collective-permute-start.8 = (bf16[256,512]{1,0:T(8,128)(2,1)S(1)}, bf16[256,512]{1,0:T(8,128)(2,1)S(1)}, u32[]{:S(2)}, u32[]{:S(2)}) collective-permute-start(bf16[256,512]{1,0:T(8,128)(2,1)S(1)} %copy-done.5), channel_id=1, source_target_pairs={{0,112},{16,96},{32,16},{48,0},{64,48},{80,32},{96,80},{112,64},{1... | collective-permute-start | bytes 786440 | tf_op jit(solution)/shard_map/ppermute | solution.py:463
  49.7 0.0 copy-done.4
  49.7 0.0 collective-permute-start.5
  49.7 4.0 %convolve.5.rest_3_.rest_5_ = f32[512,256]{1,0:T(8,128)S(1)} custom-call(s32[16]{0:T(128)S(1)} %pad_add_fusion.info_ref, bf16[256,1024]{1,0:T(8,128)(2,1)S(1)} %collective-permute-done.4.rest_0_, bf16[256,1024]{1,0:T(8,128)(2,1)S(1)} %collective-permute-done.7.rest_1_, bf16[8,2048,128]{2,1,0:T(8,128)(2,1)S(1)} %bitcast.23, f32[512,256]{1,0:T(8,128)S(1)} %convolve.4.rest_3_), custom_call_target="tpu_custom_call" | custom-call | flops 3600000000 | bytes 2097152 | tf_op jit(solution)/shard_map/convolve/pallas_call | solution.py:281
  53.8 0.0 collective-permute-done.1.rest_0_
  53.8 0.0 collective-permute-done.6.rest_1_.rest_2_
  53.8 6.5 %finish.2 = (f32[16,3,128]{2,1,0:T(4,128)S(1)}, bf16[128,512]{1,0:T(8,128)(2,1)S(1)}) custom-call(s32[16]{0:T(128)S(1)} %pad_add_fusion.info_ref, s32[88]{0:T(128)S(1)} %pad_add_fusion.1.place_ref, bf16[256,512]{1,0:T(8,128)(2,1)S(1)} %collective-permute-done.1.rest_0_, bf16[256,512]{1,0:T(8,128)(2,1)S(1)} %collective-permute-done.6.rest_1_.rest_2_, ...), custom_call_target="tpu_custom_call" | custom-call | flops 3600000000 | bytes 8000000 | tf_op jit(solution)/shard_map/finish/pallas_call | solution.py:442
  60.3 0.0 collective-permute-done.8.rest_3_
  60.3 0.0 collective-permute-done.5.rest_1_
  60.3 7.4 %finish.3 = f32[16,3,128]{2,1,0:T(4,128)S(1)} custom-call(s32[16]{0:T(128)S(1)} %pad_add_fusion.info_ref, s32[88]{0:T(128)S(1)} %pad_add_fusion.1.place_ref, bf16[256,512]{1,0:T(8,128)(2,1)S(1)} %collective-permute-done.1.rest_0_, bf16[256,512]{1,0:T(8,128)(2,1)S(1)} %collective-permute-done.5.rest_1_, ...), custom_call_target="tpu_custom_call" | custom-call | flops 3600000000 | bytes 8000000 | tf_op jit(solution)/shard_map/finish/pallas_call | solution.py:442
  67.8 14.4 %all_to_all.5 = f32[16,3,128]{2,1,0:T(4,128)S(1)} all-to-all(f32[16,3,128]{2,1,0:T(4,128)S(1)} %finish.3), channel_id=1, replica_groups=mesh['sgt'=8,'work'=16] {'work'}, dimensions={0} | all-to-all | bytes 49152 | tf_op jit(solution)/shard_map/all_to_all | solution.py:535
  82.2 0.1 reshape.395
  82.3 0.6 copy.17
  (7 shorter events, 0.1 us)
Async XLA Ops:
  0.0 15.8 %copy-start = (s32[128,8]{0,1:T(8,128)S(1)}, s32[128,8]{0,1:T(8,128)}, u32[]{:S(2)}) copy-start(s32[128,8]{0,1:T(8,128)} %param.14) | copy-start | bytes 12292
  0.0 15.0 %copy-start.2 = (s32[128,8]{0,1:T(8,128)S(1)}, s32[128,8]{0,1:T(8,128)}, u32[]{:S(2)}) copy-start(s32[128,8]{0,1:T(8,128)} %param.12) | copy-start | bytes 12292
  0.0 15.1 %copy-start.6 = (s32[128]{0:T(128)S(1)}, s32[128]{0:T(128)}, u32[]{:S(2)}) copy-start(s32[128]{0:T(128)} %param.13) | copy-start | bytes 1540
  0.0 17.1 %copy-start.7 = (s32[44]{0:T(128)S(1)}, s32[44]{0:T(128)}, u32[]{:S(2)}) copy-start(s32[44]{0:T(128)} %param.16) | copy-start | bytes 532
  0.0 17.3 %copy-start.3 = (f32[44]{0:T(128)S(1)}, f32[44]{0:T(128)}, u32[]{:S(2)}) copy-start(f32[44]{0:T(128)} %param.15) | copy-start | bytes 532
  7.1 10.2 %collective-permute-start = (bf16[256,1024]{1,0:T(8,128)(2,1)}, bf16[256,1024]{1,0:T(8,128)(2,1)S(1)}, u32[]{:S(2)}, u32[]{:S(2)}) collective-permute-start(bf16[256,1024]{1,0:T(8,128)(2,1)} %get-tuple-element.33), channel_id=1, source_target_pairs={{0,16},{16,0},{32,48},{48,32},{64,80},{80,64},{96,112},{112,96},{1... | collective-permute-start | bytes 1572872 | tf_op jit(solution)/shard_map/ppermute | solution.py:463
  7.2 17.2 %collective-permute-start.2 = (bf16[256,1024]{1,0:T(8,128)(2,1)}, bf16[256,1024]{1,0:T(8,128)(2,1)S(1)}, u32[]{:S(2)}, u32[]{:S(2)}) collective-permute-start(bf16[256,1024]{1,0:T(8,128)(2,1)} %get-tuple-element.38), channel_id=1, source_target_pairs={{0,64},{16,80},{32,96},{48,112},{64,0},{80,16},{96,32},{112,48},{1... | collective-permute-start | bytes 1572872 | tf_op jit(solution)/shard_map/ppermute | solution.py:463
  11.3 27.5 %collective-permute-start.3 = (bf16[256,1024]{1,0:T(8,128)(2,1)}, bf16[256,1024]{1,0:T(8,128)(2,1)S(1)}, u32[]{:S(2)}, u32[]{:S(2)}) collective-permute-start(bf16[256,1024]{1,0:T(8,128)(2,1)} %get-tuple-element.40), channel_id=1, source_target_pairs={{0,80},{16,64},{32,112},{48,96},{64,16},{80,0},{96,48},{112,32},{1... | collective-permute-start | bytes 1572872 | tf_op jit(solution)/shard_map/ppermute | solution.py:463
  11.3 35.1 %collective-permute-start.4 = (bf16[256,1024]{1,0:T(8,128)(2,1)}, bf16[256,1024]{1,0:T(8,128)(2,1)S(1)}, u32[]{:S(2)}, u32[]{:S(2)}) collective-permute-start(bf16[256,1024]{1,0:T(8,128)(2,1)} %get-tuple-element.47), channel_id=1, source_target_pairs={{0,32},{16,48},{32,64},{48,80},{64,96},{80,112},{96,0},{112,16},{1... | collective-permute-start | bytes 1572872 | tf_op jit(solution)/shard_map/ppermute | solution.py:463
  12.8 35.1 %collective-permute-start.7 = (bf16[256,1024]{1,0:T(8,128)(2,1)}, bf16[256,1024]{1,0:T(8,128)(2,1)S(1)}, u32[]{:S(2)}, u32[]{:S(2)}) collective-permute-start(bf16[256,1024]{1,0:T(8,128)(2,1)} %get-tuple-element.51), channel_id=1, source_target_pairs={{0,96},{16,112},{32,0},{48,16},{64,32},{80,48},{96,64},{112,80},{1... | collective-permute-start | bytes 1572872 | tf_op jit(solution)/shard_map/ppermute | solution.py:463
  22.2 31.6 %collective-permute-start.1 = (bf16[256,512]{1,0:T(8,128)(2,1)}, bf16[256,512]{1,0:T(8,128)(2,1)S(1)}, u32[]{:S(2)}, u32[]{:S(2)}) collective-permute-start(bf16[256,512]{1,0:T(8,128)(2,1)} %get-tuple-element.34), channel_id=1, source_target_pairs={{0,48},{16,32},{32,80},{48,64},{64,112},{80,96},{96,16},{112,0},{1... | collective-permute-start | bytes 786440 | tf_op jit(solution)/shard_map/ppermute | solution.py:463
  24.4 29.4 %collective-permute-start.6 = (bf16[256,512]{1,0:T(8,128)(2,1)}, bf16[256,512]{1,0:T(8,128)(2,1)S(1)}, u32[]{:S(2)}, u32[]{:S(2)}) collective-permute-start(bf16[256,512]{1,0:T(8,128)(2,1)} %get-tuple-element.49), channel_id=1, source_target_pairs={{0,112},{16,96},{32,16},{48,0},{64,48},{80,32},{96,80},{112,64},{1... | collective-permute-start | bytes 786440 | tf_op jit(solution)/shard_map/ppermute | solution.py:463
  26.9 7.8 %copy-start.1 = (bf16[256,1024]{1,0:T(8,128)(2,1)S(1)}, bf16[256,1024]{1,0:T(8,128)(2,1)}, u32[]{:S(2)}) copy-start(bf16[256,1024]{1,0:T(8,128)(2,1)} %get-tuple-element.43.rest_0_) | copy-start | bytes 1572868
  38.8 9.2 %copy-start.5 = (bf16[256,512]{1,0:T(8,128)(2,1)S(1)}, bf16[256,512]{1,0:T(8,128)(2,1)}, u32[]{:S(2)}) copy-start(bf16[256,512]{1,0:T(8,128)(2,1)} %get-tuple-element.52) | copy-start | bytes 786436
  38.8 11.0 %copy-start.4 = (bf16[256,512]{1,0:T(8,128)(2,1)S(1)}, bf16[256,512]{1,0:T(8,128)(2,1)}, u32[]{:S(2)}) copy-start(bf16[256,512]{1,0:T(8,128)(2,1)} %get-tuple-element.48) | copy-start | bytes 786436
  47.9 12.4 %collective-permute-start.8 = (bf16[256,512]{1,0:T(8,128)(2,1)S(1)}, bf16[256,512]{1,0:T(8,128)(2,1)S(1)}, u32[]{:S(2)}, u32[]{:S(2)}) collective-permute-start(bf16[256,512]{1,0:T(8,128)(2,1)S(1)} %copy-done.5), channel_id=1, source_target_pairs={{0,112},{16,96},{32,16},{48,0},{64,48},{80,32},{96,80},{112,64},{1... | collective-permute-start | bytes 786440 | tf_op jit(solution)/shard_map/ppermute | solution.py:463
  49.7 10.6 %collective-permute-start.5 = (bf16[256,512]{1,0:T(8,128)(2,1)S(1)}, bf16[256,512]{1,0:T(8,128)(2,1)S(1)}, u32[]{:S(2)}, u32[]{:S(2)}) collective-permute-start(bf16[256,512]{1,0:T(8,128)(2,1)S(1)} %copy-done.4), channel_id=1, source_target_pairs={{0,48},{16,32},{32,80},{48,64},{64,112},{80,96},{96,16},{112,0},{1... | collective-permute-start | bytes 786440 | tf_op jit(solution)/shard_map/ppermute | solution.py:463

commit v6 on v5

--- a/solution.py
+++ b/solution.py
@@ -27,7 +27,7 @@
 BLOCK = 256
 HALF = NT // 2
 SPAN = 128
-AHEAD = 4
+AHEAD = 6
 TSTEP = 4
 QSTEP = 22
 SMALL = 12 * 1024 * 1024

time: 83.1 us -> 83.2 us (level)
  blocking collectives: 14.4 us -> 15.8 us
  starting transfers between devices: 12.2 us -> 10.8 us
    all_to_all x1, blocking collectives: 14.4 us -> 15.8 us  [local(): lax.all_to_all(peaks, 'work', split_axis=0, concat_axis=0, tiled=True)]
    ppermute x9, starting transfers between devices: 12.2 us -> 10.8 us  [send(): return lax.ppermute(block, 'sgt', pairs)]
where the time goes in v6:
time: 83.2 us; the launch traced here: 83.4 us
  Pallas kernels  37.2 us (45%)
  blocking collectives  15.8 us (19%)
  starting transfers between devices  10.8 us (13%)
  waiting for transfers between devices  7.51 us (9%)
  other arithmetic  6.16 us (7%)
  local copies, waits for them, and re-layouts  5.68 us (7%)
    all_to_all x1, blocking collectives, local(): lax.all_to_all(peaks, 'work', split_axis=0, concat_axis=0, tiled=True)  15.8 us
    pallas_call x2, Pallas kernels, finish(): pl.pallas_call(functools.partial(finish_kernel, late), out_shape=out_shap...  13.9 us
    pallas_call x3, Pallas kernels, convolve(): pl.pallas_call(functools.partial(convolve_kernel, arrivals, begins), out_...  12.1 us
    ppermute x9, starting transfers between devices, send(): return lax.ppermute(block, 'sgt', pairs)  10.8 us
    ppermute x9, waiting for transfers between devices, send(): return lax.ppermute(block, 'sgt', pairs)  7.51 us
    pallas_call x1, Pallas kernels, project(): pl.pallas_call(functools.partial(project_kernel, steps), out_shape=[jax.S...  7.28 us
    pallas_call x1, Pallas kernels, tables(): pl.pallas_call(tables_kernel, out_shape=jax.ShapeDtypeStruct((NPER, SPAN,...  3.88 us
    transpose x1, local copies, waits for them, and re-layouts, local(): slips = jnp.transpose(slip_rate[0], (0, 3, 1, 2)).reshape(SLOTS, L * V, PB)  3.87 us
  transfers between devices with their start and end apart: 9, of which 3 were waited for; matrix products, arithmetic and copies ran while one was open for 13% of the time, Pallas kernels for 27%

profile of v6, /device:TPU:0, one launch (start us, length us, event | category | flops | bytes accessed | tf_op | source)
XLA Modules:
  0.0 83.4 jit_solution(7535046724130568923)
XLA Ops:
  0.0 0.0 copy-start
  0.0 0.0 copy-start.2
  0.0 0.0 copy-start.6
  0.0 0.0 copy-start.7
  0.0 0.0 copy-start.3
  0.0 7.3 %project.1 = (bf16[256,1024]{1,0:T(8,128)(2,1)}, bf16[256,1024]{1,0:T(8,128)(2,1)}, bf16[256,1024]{1,0:T(8,128)(2,1)}, bf16[256,1024]{1,0:T(8,128)(2,1)}, bf16[2...) custom-call(s32[8,128]{1,0:T(8,128)} %bitcast.29, ...), custom_call_target="tpu_custom_call" | custom-call | flops 400000000 | bytes 12800000 | tf_op jit(solution)/shard_map/project/pallas_call | solution.py:120
  7.3 0.1 collective-permute-start
  7.4 3.9 %collective-permute-start.2 = (bf16[256,1024]{1,0:T(8,128)(2,1)}, bf16[256,1024]{1,0:T(8,128)(2,1)S(1)}, u32[]{:S(2)}, u32[]{:S(2)}) collective-permute-start(bf16[256,1024]{1,0:T(8,128)(2,1)} %get-tuple-element.38), channel_id=1, source_target_pairs={{0,64},{16,80},{32,96},{48,112},{64,0},{80,16},{96,32},{112,48},{1... | collective-permute-start | bytes 1572872 | tf_op jit(solution)/shard_map/ppermute | solution.py:463
  11.3 0.1 collective-permute-start.3
  11.3 1.3 %collective-permute-start.4 = (bf16[256,1024]{1,0:T(8,128)(2,1)}, bf16[256,1024]{1,0:T(8,128)(2,1)S(1)}, u32[]{:S(2)}, u32[]{:S(2)}) collective-permute-start(bf16[256,1024]{1,0:T(8,128)(2,1)} %get-tuple-element.47), channel_id=1, source_target_pairs={{0,32},{16,48},{32,64},{48,80},{64,96},{80,112},{96,0},{112,16},{1... | collective-permute-start | bytes 1572872 | tf_op jit(solution)/shard_map/ppermute | solution.py:463
  12.6 2.0 %collective-permute-start.7 = (bf16[256,1024]{1,0:T(8,128)(2,1)}, bf16[256,1024]{1,0:T(8,128)(2,1)S(1)}, u32[]{:S(2)}, u32[]{:S(2)}) collective-permute-start(bf16[256,1024]{1,0:T(8,128)(2,1)} %get-tuple-element.51), channel_id=1, source_target_pairs={{0,96},{16,112},{32,0},{48,16},{64,32},{80,48},{96,64},{112,80},{1... | collective-permute-start | bytes 1572872 | tf_op jit(solution)/shard_map/ppermute | solution.py:463
  14.6 0.0 copy-done.2
  14.6 0.2 shift-right-arithmetic_reduce_fusion
  14.8 0.0 copy-done.6
  14.8 0.7 dynamic_slice.12
  15.5 0.0 copy-done
  15.5 0.2 dynamic-slice_reduce_fusion
  15.7 0.1 stack.45
  15.7 0.2 fusion.5
  15.9 0.7 compare_select_fusion.7
  16.6 0.1 pad_add_fusion.info_ref
  16.7 0.0 copy-done.7
  16.7 0.2 convert_reduce_fusion
  16.9 0.1 pad_add_fusion.1.place_ref
  17.0 0.0 collective-permute-done.rest_1_
  17.0 0.0 copy-done.3
  17.0 3.7 %fusion.2 = (f32[44,1,640]{2,1,0:T(1,128)S(1)}, f32[44,1,640]{2,1,0:T(1,128)S(1)}) fusion(f32[640]{0:T(1024)S(1)} %subtract_convert_fusion, f32[44]{0:T(128)S(1)} %get-tuple-element.67, f32[44]{0:T(128)S(1)} %get-tuple-element.66, f32[44]{0:T(128)S(1)} %get-tuple-element.65), kind=kLoop, calls=%fused_computation.6 | loop fusion | flops 168960 | bytes 228368 | tf_op jit(solution)/shard_map/mul | solution.py:185
  20.8 0.1 fusion
  20.9 0.1 reshape.393.v_ref
  21.0 0.7 sine_multiply_fusion
  21.7 0.1 fusion.3
  21.8 0.1 collective-permute-start.1
  21.9 2.4 %collective-permute-done.2.rest_0_ = bf16[256,1024]{1,0:T(8,128)(2,1)S(1)} collective-permute-done((bf16[256,1024]{1,0:T(8,128)(2,1)}, bf16[256,1024]{1,0:T(8,128)(2,1)S(1)}, u32[]{:S(2)}, u32[]{:S(2)}) %collective-permute-start.2) | collective-permute-done | bytes 524320 | tf_op jit(solution)/shard_map/ppermute | solution.py:463
  24.4 1.7 %collective-permute-start.6 = (bf16[256,512]{1,0:T(8,128)(2,1)}, bf16[256,512]{1,0:T(8,128)(2,1)S(1)}, u32[]{:S(2)}, u32[]{:S(2)}) collective-permute-start(bf16[256,512]{1,0:T(8,128)(2,1)} %get-tuple-element.49), channel_id=1, source_target_pairs={{0,112},{16,96},{32,16},{48,0},{64,48},{80,32},{96,80},{112,64},{1... | collective-permute-start | bytes 786440 | tf_op jit(solution)/shard_map/ppermute | solution.py:463
  26.1 0.0 copy-start.1
  26.1 3.9 %copy.15 = bf16[8,32,64,128]{3,2,1,0:T(8,128)(2,1)S(1)} copy(bf16[8,32,64,128]{3,1,2,0:T(8,128)(2,1)} %bitcast.27) | data formatting | bytes 8388608 | tf_op jit(solution)/shard_map/transpose | solution.py:496
  30.0 3.9 %tables.1.rest_4_.rest_6_ = bf16[44,128,512]{2,1,0:T(8,128)(2,1)S(1)} custom-call(f32[11,8,128]{2,1,0:T(8,128)S(1)} %bitcast.26, f32[11,8,384]{2,1,0:T(8,128)S(1)} %reshape.393.v_ref), custom_call_target="tpu_custom_call" | custom-call | flops 14417920 | bytes 6000000 | tf_op jit(solution)/shard_map/tables/pallas_call | solution.py:189
  33.9 0.0 copy-done.1
  33.9 4.0 %convolve.3.rest_3_ = f32[512,256]{1,0:T(8,128)S(1)} custom-call(s32[16]{0:T(128)S(1)} %pad_add_fusion.info_ref, bf16[256,1024]{1,0:T(8,128)(2,1)S(1)} %copy-done.1, bf16[256,1024]{1,0:T(8,128)(2,1)S(1)} %collective-permute-done.rest_1_, bf16[8,2048,128]{2,1,0:T(8,128)(2,1)S(1)} %bitcast.21), custom_call_target="tpu_custom_call" | custom-call | flops 3600000000 | bytes 2097152 | tf_op jit(solution)/shard_map/convolve/pallas_call | solution.py:281
  37.9 0.0 copy-start.5
  37.9 0.0 copy-start.4
  38.0 0.0 collective-permute-done.3.rest_1_
  38.0 4.0 %convolve.4.rest_3_ = f32[512,256]{1,0:T(8,128)S(1)} custom-call(s32[16]{0:T(128)S(1)} %pad_add_fusion.info_ref, bf16[256,1024]{1,0:T(8,128)(2,1)S(1)} %collective-permute-done.2.rest_0_, bf16[256,1024]{1,0:T(8,128)(2,1)S(1)} %collective-permute-done.3.rest_1_, bf16[8,2048,128]{2,1,0:T(8,128)(2,1)S(1)} %bitcast.22, f32[512,256]{1,0:T(8,128)S(1)} %convolve.3.rest_3_), custom_call_target="tpu_custom_call" | custom-call | flops 3600000000 | bytes 2097152 | tf_op jit(solution)/shard_map/convolve/pallas_call | solution.py:281
  42.0 4.5 %collective-permute-done.4.rest_0_ = bf16[256,1024]{1,0:T(8,128)(2,1)S(1)} collective-permute-done((bf16[256,1024]{1,0:T(8,128)(2,1)}, bf16[256,1024]{1,0:T(8,128)(2,1)S(1)}, u32[]{:S(2)}, u32[]{:S(2)}) %collective-permute-start.4) | collective-permute-done | bytes 524320 | tf_op jit(solution)/shard_map/ppermute | solution.py:463
  46.5 0.6 collective-permute-done.7.rest_1_
  47.1 0.0 copy-done.5
  47.1 1.8 %collective-permute-start.8 = (bf16[256,512]{1,0:T(8,128)(2,1)S(1)}, bf16[256,512]{1,0:T(8,128)(2,1)S(1)}, u32[]{:S(2)}, u32[]{:S(2)}) collective-permute-start(bf16[256,512]{1,0:T(8,128)(2,1)S(1)} %copy-done.5), channel_id=1, source_target_pairs={{0,112},{16,96},{32,16},{48,0},{64,48},{80,32},{96,80},{112,64},{1... | collective-permute-start | bytes 786440 | tf_op jit(solution)/shard_map/ppermute | solution.py:463
  48.9 0.0 copy-done.4
  48.9 0.0 collective-permute-start.5
  48.9 4.0 %convolve.5.rest_3_.rest_5_ = f32[512,256]{1,0:T(8,128)S(1)} custom-call(s32[16]{0:T(128)S(1)} %pad_add_fusion.info_ref, bf16[256,1024]{1,0:T(8,128)(2,1)S(1)} %collective-permute-done.4.rest_0_, bf16[256,1024]{1,0:T(8,128)(2,1)S(1)} %collective-permute-done.7.rest_1_, bf16[8,2048,128]{2,1,0:T(8,128)(2,1)S(1)} %bitcast.23, f32[512,256]{1,0:T(8,128)S(1)} %convolve.4.rest_3_), custom_call_target="tpu_custom_call" | custom-call | flops 3600000000 | bytes 2097152 | tf_op jit(solution)/shard_map/convolve/pallas_call | solution.py:281
  52.9 0.0 collective-permute-done.1.rest_0_
  52.9 0.0 collective-permute-done.6.rest_1_.rest_2_
  53.0 6.5 %finish.2 = (f32[16,3,128]{2,1,0:T(4,128)S(1)}, bf16[128,512]{1,0:T(8,128)(2,1)S(1)}) custom-call(s32[16]{0:T(128)S(1)} %pad_add_fusion.info_ref, s32[88]{0:T(128)S(1)} %pad_add_fusion.1.place_ref, bf16[256,512]{1,0:T(8,128)(2,1)S(1)} %collective-permute-done.1.rest_0_, bf16[256,512]{1,0:T(8,128)(2,1)S(1)} %collective-permute-done.6.rest_1_.rest_2_, ...), custom_call_target="tpu_custom_call" | custom-call | flops 3600000000 | bytes 8000000 | tf_op jit(solution)/shard_map/finish/pallas_call | solution.py:442
  59.5 0.0 collective-permute-done.8.rest_3_
  59.5 0.0 collective-permute-done.5.rest_1_
  59.5 7.4 %finish.3 = f32[16,3,128]{2,1,0:T(4,128)S(1)} custom-call(s32[16]{0:T(128)S(1)} %pad_add_fusion.info_ref, s32[88]{0:T(128)S(1)} %pad_add_fusion.1.place_ref, bf16[256,512]{1,0:T(8,128)(2,1)S(1)} %collective-permute-done.1.rest_0_, bf16[256,512]{1,0:T(8,128)(2,1)S(1)} %collective-permute-done.5.rest_1_, ...), custom_call_target="tpu_custom_call" | custom-call | flops 3600000000 | bytes 8000000 | tf_op jit(solution)/shard_map/finish/pallas_call | solution.py:442
  66.9 15.8 %all_to_all.5 = f32[16,3,128]{2,1,0:T(4,128)S(1)} all-to-all(f32[16,3,128]{2,1,0:T(4,128)S(1)} %finish.3), channel_id=1, replica_groups=mesh['sgt'=8,'work'=16] {'work'}, dimensions={0} | all-to-all | bytes 49152 | tf_op jit(solution)/shard_map/all_to_all | solution.py:535
  82.7 0.1 reshape.395
  82.8 0.6 copy.17
  (7 shorter events, 0.1 us)
Async XLA Ops:
  0.0 15.5 %copy-start = (s32[128,8]{0,1:T(8,128)S(1)}, s32[128,8]{0,1:T(8,128)}, u32[]{:S(2)}) copy-start(s32[128,8]{0,1:T(8,128)} %param.14) | copy-start | bytes 12292
  0.0 14.6 %copy-start.2 = (s32[128,8]{0,1:T(8,128)S(1)}, s32[128,8]{0,1:T(8,128)}, u32[]{:S(2)}) copy-start(s32[128,8]{0,1:T(8,128)} %param.12) | copy-start | bytes 12292
  0.0 14.8 %copy-start.6 = (s32[128]{0:T(128)S(1)}, s32[128]{0:T(128)}, u32[]{:S(2)}) copy-start(s32[128]{0:T(128)} %param.13) | copy-start | bytes 1540
  0.0 16.7 %copy-start.7 = (s32[44]{0:T(128)S(1)}, s32[44]{0:T(128)}, u32[]{:S(2)}) copy-start(s32[44]{0:T(128)} %param.16) | copy-start | bytes 532
  0.0 17.0 %copy-start.3 = (f32[44]{0:T(128)S(1)}, f32[44]{0:T(128)}, u32[]{:S(2)}) copy-start(f32[44]{0:T(128)} %param.15) | copy-start | bytes 532
  7.3 9.7 %collective-permute-start = (bf16[256,1024]{1,0:T(8,128)(2,1)}, bf16[256,1024]{1,0:T(8,128)(2,1)S(1)}, u32[]{:S(2)}, u32[]{:S(2)}) collective-permute-start(bf16[256,1024]{1,0:T(8,128)(2,1)} %get-tuple-element.33), channel_id=1, source_target_pairs={{0,16},{16,0},{32,48},{48,32},{64,80},{80,64},{96,112},{112,96},{1... | collective-permute-start | bytes 1572872 | tf_op jit(solution)/shard_map/ppermute | solution.py:463
  7.4 17.0 %collective-permute-start.2 = (bf16[256,1024]{1,0:T(8,128)(2,1)}, bf16[256,1024]{1,0:T(8,128)(2,1)S(1)}, u32[]{:S(2)}, u32[]{:S(2)}) collective-permute-start(bf16[256,1024]{1,0:T(8,128)(2,1)} %get-tuple-element.38), channel_id=1, source_target_pairs={{0,64},{16,80},{32,96},{48,112},{64,0},{80,16},{96,32},{112,48},{1... | collective-permute-start | bytes 1572872 | tf_op jit(solution)/shard_map/ppermute | solution.py:463
  11.3 26.7 %collective-permute-start.3 = (bf16[256,1024]{1,0:T(8,128)(2,1)}, bf16[256,1024]{1,0:T(8,128)(2,1)S(1)}, u32[]{:S(2)}, u32[]{:S(2)}) collective-permute-start(bf16[256,1024]{1,0:T(8,128)(2,1)} %get-tuple-element.40), channel_id=1, source_target_pairs={{0,80},{16,64},{32,112},{48,96},{64,16},{80,0},{96,48},{112,32},{1... | collective-permute-start | bytes 1572872 | tf_op jit(solution)/shard_map/ppermute | solution.py:463
  11.3 35.2 %collective-permute-start.4 = (bf16[256,1024]{1,0:T(8,128)(2,1)}, bf16[256,1024]{1,0:T(8,128)(2,1)S(1)}, u32[]{:S(2)}, u32[]{:S(2)}) collective-permute-start(bf16[256,1024]{1,0:T(8,128)(2,1)} %get-tuple-element.47), channel_id=1, source_target_pairs={{0,32},{16,48},{32,64},{48,80},{64,96},{80,112},{96,0},{112,16},{1... | collective-permute-start | bytes 1572872 | tf_op jit(solution)/shard_map/ppermute | solution.py:463
  12.6 34.5 %collective-permute-start.7 = (bf16[256,1024]{1,0:T(8,128)(2,1)}, bf16[256,1024]{1,0:T(8,128)(2,1)S(1)}, u32[]{:S(2)}, u32[]{:S(2)}) collective-permute-start(bf16[256,1024]{1,0:T(8,128)(2,1)} %get-tuple-element.51), channel_id=1, source_target_pairs={{0,96},{16,112},{32,0},{48,16},{64,32},{80,48},{96,64},{112,80},{1... | collective-permute-start | bytes 1572872 | tf_op jit(solution)/shard_map/ppermute | solution.py:463
  21.8 31.1 %collective-permute-start.1 = (bf16[256,512]{1,0:T(8,128)(2,1)}, bf16[256,512]{1,0:T(8,128)(2,1)S(1)}, u32[]{:S(2)}, u32[]{:S(2)}) collective-permute-start(bf16[256,512]{1,0:T(8,128)(2,1)} %get-tuple-element.34), channel_id=1, source_target_pairs={{0,48},{16,32},{32,80},{48,64},{64,112},{80,96},{96,16},{112,0},{1... | collective-permute-start | bytes 786440 | tf_op jit(solution)/shard_map/ppermute | solution.py:463
  24.4 28.6 %collective-permute-start.6 = (bf16[256,512]{1,0:T(8,128)(2,1)}, bf16[256,512]{1,0:T(8,128)(2,1)S(1)}, u32[]{:S(2)}, u32[]{:S(2)}) collective-permute-start(bf16[256,512]{1,0:T(8,128)(2,1)} %get-tuple-element.49), channel_id=1, source_target_pairs={{0,112},{16,96},{32,16},{48,0},{64,48},{80,32},{96,80},{112,64},{1... | collective-permute-start | bytes 786440 | tf_op jit(solution)/shard_map/ppermute | solution.py:463
  26.1 7.8 %copy-start.1 = (bf16[256,1024]{1,0:T(8,128)(2,1)S(1)}, bf16[256,1024]{1,0:T(8,128)(2,1)}, u32[]{:S(2)}) copy-start(bf16[256,1024]{1,0:T(8,128)(2,1)} %get-tuple-element.43.rest_0_) | copy-start | bytes 1572868
  37.9 9.2 %copy-start.5 = (bf16[256,512]{1,0:T(8,128)(2,1)S(1)}, bf16[256,512]{1,0:T(8,128)(2,1)}, u32[]{:S(2)}) copy-start(bf16[256,512]{1,0:T(8,128)(2,1)} %get-tuple-element.52) | copy-start | bytes 786436
  37.9 10.9 %copy-start.4 = (bf16[256,512]{1,0:T(8,128)(2,1)S(1)}, bf16[256,512]{1,0:T(8,128)(2,1)}, u32[]{:S(2)}) copy-start(bf16[256,512]{1,0:T(8,128)(2,1)} %get-tuple-element.48) | copy-start | bytes 786436
  47.1 12.4 %collective-permute-start.8 = (bf16[256,512]{1,0:T(8,128)(2,1)S(1)}, bf16[256,512]{1,0:T(8,128)(2,1)S(1)}, u32[]{:S(2)}, u32[]{:S(2)}) collective-permute-start(bf16[256,512]{1,0:T(8,128)(2,1)S(1)} %copy-done.5), channel_id=1, source_target_pairs={{0,112},{16,96},{32,16},{48,0},{64,48},{80,32},{96,80},{112,64},{1... | collective-permute-start | bytes 786440 | tf_op jit(solution)/shard_map/ppermute | solution.py:463
  48.9 10.6 %collective-permute-start.5 = (bf16[256,512]{1,0:T(8,128)(2,1)S(1)}, bf16[256,512]{1,0:T(8,128)(2,1)S(1)}, u32[]{:S(2)}, u32[]{:S(2)}) collective-permute-start(bf16[256,512]{1,0:T(8,128)(2,1)S(1)} %copy-done.4), channel_id=1, source_target_pairs={{0,48},{16,32},{32,80},{48,64},{64,112},{80,96},{96,16},{112,0},{1... | collective-permute-start | bytes 786440 | tf_op jit(solution)/shard_map/ppermute | solution.py:463
